TPU v7x, 32 devices: a whole 2x2x4 slice. The times are simulated.
32 devices in a mesh: rep: 4 (over y, x), shard: 8 (over z, core).
Axes of the slice: x: 2, y: 2, z: 4, core: 2. Of those that a mesh axis runs over, the one named last changes fastest.
Arguments:
- tokens: bfloat16 [8, 512, 2560], P('shard', 'rep'), may hold values from -6 to 6
- cotangent: bfloat16 [8, 512, 2560], P('shard', 'rep'), may hold values from -6 to 6
- doc_lengths: int32 [8, 4], P('shard'), may hold values from 1 to 509, as said below
- gain_attn: bfloat16 [2560], P('shard'), may hold values from 0.25 to 1.75
- query_down: bfloat16 [2560, 768], P('shard'), may hold values from -0.125 to 0.125
- gain_query: bfloat16 [768], P('shard'), may hold values from 0.25 to 1.75
- query_up: bfloat16 [768, 3840], P('shard'), may hold values from -0.3125 to 0.3125
- latent_down: bfloat16 [2560, 288], P('shard'), may hold values from -0.125 to 0.125
- gain_latent: bfloat16 [256], P('shard'), may hold values from 0.25 to 1.75
- latent_up: bfloat16 [256, 5120], P('shard'), may hold values from -0.375 to 0.375
- attn_out: bfloat16 [2560, 2560], P('shard'), may hold values from -6 to 6
- gain_ffn: bfloat16 [2560], P('shard'), may hold values from 0.25 to 1.75
- w_gate: bfloat16 [2560, 6400], P('shard'), may hold values from -0.125 to 0.125
- w_up: bfloat16 [2560, 6400], P('shard'), may hold values from -0.125 to 0.125
- w_down: bfloat16 [6400, 2560], P('shard'), may hold values from -0.4375 to 0.4375
Outputs:
- layer_out: bfloat16 [8, 512, 2560], P('shard', 'rep')
- tokens_grad: bfloat16 [8, 512, 2560], P('shard', 'rep')
- gain_attn_grad: float32 [2560], P('shard')
- query_down_grad: float32 [2560, 768], P('shard')
- gain_query_grad: float32 [768], P('shard')
- query_up_grad: float32 [768, 3840], P('shard')
- latent_down_grad: float32 [2560, 288], P('shard')
- gain_latent_grad: float32 [256], P('shard')
- latent_up_grad: float32 [256, 5120], P('shard')
- attn_out_grad: float32 [2560, 2560], P('shard')
- gain_ffn_grad: float32 [2560], P('shard')
- w_gate_grad: float32 [2560, 6400], P('shard')
- w_up_grad: float32 [2560, 6400], P('shard')
- w_down_grad: float32 [6400, 2560], P('shard')
Inputs may be any that keep to these rules, and one draw needn't show every extreme that they name: `doc_lengths`: each row holds the lengths of the 4 documents of one sequence, in order, and sums to 512; the second document begins within the sequence's first 128 tokens and ends within its last 128; in some sequence every document but the second has length 1.
All inputs are finite; a program needn't handle non-finite values.
Results may differ from a plain program's by a relative error of at most 0.022.
Values may be sent and summed in bfloat16 or wider, within the bound.
A program may use at most 640 MiB of HBM per device.

v0:
```python
import math

import jax
import jax.numpy as jnp
from jax import lax
from jax.sharding import PartitionSpec as P

KR = 256
H = 40
ND = 64
RD = 32
VD = 64
FF = 6400


epsilon = 1e-05
residual_scale = 1.4 / math.sqrt(62.0)
rope_base = 10000.0
masked_score = -1e30


def rms_scale(values, gain):
    return values * lax.rsqrt(jnp.mean(values * values, axis=-1, keepdims=True) + epsilon) * gain


def rotate(values, cos_part, sin_part):
    midpoint = values.shape[-1] // 2
    former = values[..., :midpoint]
    latter = values[..., midpoint:]
    return jnp.concatenate(
        [former * cos_part - latter * sin_part, latter * cos_part + former * sin_part], axis=-1
    )


def segment_of(lengths, positions):
    doc_ends = jnp.cumsum(lengths)
    doc_starts = doc_ends - lengths
    segment = jnp.sum((positions[:, None] >= doc_ends[None, :]).astype(jnp.int32), axis=1)
    chosen = segment[:, None] == jnp.arange(lengths.shape[0], dtype=jnp.int32)[None, :]
    offsets = positions - jnp.sum(jnp.where(chosen, doc_starts[None, :], 0), axis=1)
    return (segment, offsets)


def rope_tables(offsets, rope_width):
    exponents = jnp.arange(0, rope_width, 2, dtype=jnp.float32) / rope_width
    angles = offsets.astype(jnp.float32)[:, None] * (rope_base ** (-exponents))[None, :]
    return (jnp.cos(angles), jnp.sin(angles))


def swiglu(gate_vals, up_vals):
    return jax.nn.silu(gate_vals) * up_vals


def inner_rows(leading, trailing):
    return lax.dot_general(
        leading, trailing, (((0,), (0,)), ((), ())), preferred_element_type=jnp.float32
    )


def outer_cols(leading, trailing):
    return lax.dot_general(
        leading, trailing, (((1,), (1,)), ((), ())), preferred_element_type=jnp.float32
    )


def body(
    tokens,
    cotangent,
    doc_lengths,
    gain_attn,
    query_down,
    gain_query,
    query_up,
    latent_down,
    gain_latent,
    latent_up,
    attn_out,
    gain_ffn,
    w_gate,
    w_up,
    w_down,
):
    low_type = jnp.bfloat16
    wide_type = jnp.float32
    tok_rows = tokens.shape[1]
    seq_len = tok_rows * lax.axis_size("rep")
    head_dim = ND + RD
    group_size = math.gcd(H, 8)
    group_count = H // group_size
    softmax_scale = head_dim ** (-0.5)
    local_pos = lax.axis_index("rep") * tok_rows + jnp.arange(tok_rows, dtype=jnp.int32)
    key_pos = jnp.arange(seq_len, dtype=jnp.int32)
    query_seg, query_off = segment_of(doc_lengths[0], local_pos)
    key_seg = segment_of(doc_lengths[0], key_pos)[0]
    allowed = (query_seg[:, None] == key_seg[None, :]) & (key_pos[None, :] <= local_pos[:, None])
    cos_part, sin_part = rope_tables(query_off, RD)
    (
        gain_in_full,
        qdown_full,
        gain_q_full,
        qup_full,
        ldown_full,
        gain_l_full,
        lup_full,
        aout_full,
        gain_f_full,
    ) = (
        lax.all_gather(gain_attn, "shard", axis=0, tiled=True),
        lax.all_gather(query_down, "shard", axis=0, tiled=True),
        lax.all_gather(gain_query, "shard", axis=0, tiled=True),
        lax.all_gather(query_up, "shard", axis=0, tiled=True),
        lax.all_gather(latent_down, "shard", axis=0, tiled=True),
        lax.all_gather(gain_latent, "shard", axis=0, tiled=True),
        lax.all_gather(latent_up, "shard", axis=0, tiled=True),
        lax.all_gather(attn_out, "shard", axis=0, tiled=True),
        lax.all_gather(gain_ffn, "shard", axis=0, tiled=True),
    )
    inputs = tokens[0].astype(wide_type)
    normed, norm_in_back = jax.vjp(rms_scale, inputs, gain_in_full.astype(wide_type))
    normed_low = normed.astype(low_type)
    query_lat = jnp.dot(normed_low, qdown_full, preferred_element_type=wide_type)
    query_norm, norm_q_back = jax.vjp(rms_scale, query_lat, gain_q_full.astype(wide_type))
    query_low = query_norm.astype(low_type)
    query_proj = jnp.dot(query_low, qup_full, preferred_element_type=wide_type).reshape(
        tok_rows, H, head_dim
    )

    def query_rope(values):
        return jnp.concatenate(
            [
                values[..., :ND],
                rotate(values[..., ND:], cos_part[:, None, :], sin_part[:, None, :]),
            ],
            axis=-1,
        )

    query_rot, query_back = jax.vjp(query_rope, query_proj)
    query_used = query_rot.astype(low_type)
    latent_proj = jnp.dot(normed_low, ldown_full, preferred_element_type=wide_type)
    latent_norm, norm_l_back = jax.vjp(
        rms_scale, latent_proj[:, :KR], gain_l_full.astype(wide_type)
    )
    latent_low = latent_norm.astype(low_type)

    def key_rotate(values):
        return rotate(values, cos_part, sin_part)

    key_rot, key_back = jax.vjp(key_rotate, latent_proj[:, KR:])
    key_rope = key_rot.astype(low_type)
    keyvals = jnp.dot(latent_low, lup_full, preferred_element_type=wide_type).astype(low_type)
    all_keyvals, all_rope = (
        lax.all_gather(keyvals, "rep", axis=0, tiled=True),
        lax.all_gather(key_rope, "rep", axis=0, tiled=True),
    )
    queries = query_used.reshape(tok_rows, group_count, group_size, head_dim).transpose(1, 0, 2, 3)
    key_groups = all_keyvals.reshape(seq_len, group_count, group_size, ND + VD).transpose(
        1, 0, 2, 3
    )

    def scores_of(query_blk, key_blk):
        nope_part = jnp.einsum(
            "thd,shd->hts", query_blk[..., :ND], key_blk[..., :ND], preferred_element_type=wide_type
        )
        rope_part = jnp.einsum(
            "thd,sd->hts", query_blk[..., ND:], all_rope, preferred_element_type=wide_type
        )
        return jnp.where(allowed[None], (nope_part + rope_part) * softmax_scale, masked_score)

    def forward_group(carry, blocks):
        query_blk, key_blk = blocks
        scores = scores_of(query_blk, key_blk)
        row_max = jnp.max(scores, axis=-1, keepdims=True)
        exp_scores = jnp.exp(scores - row_max)
        totals = jnp.sum(exp_scores, axis=-1, keepdims=True)
        probs = (exp_scores / totals).astype(low_type)
        mixed = jnp.einsum(
            "hts,shd->thd", probs, key_blk[..., ND:], preferred_element_type=wide_type
        )
        return (carry, (mixed, row_max + jnp.log(totals)))

    start_carry = jnp.zeros((), wide_type)
    final_carry, (mixed_groups, log_totals) = lax.scan(
        forward_group, start_carry, (queries, key_groups)
    )
    mixed_low = mixed_groups.transpose(1, 0, 2, 3).reshape(tok_rows, H * VD).astype(low_type)
    branch = jnp.dot(mixed_low, aout_full, preferred_element_type=wide_type)
    residual = inputs + residual_scale * branch
    normed_ffn, norm_f_back = jax.vjp(rms_scale, residual, gain_f_full.astype(wide_type))
    ffn_low = normed_ffn.astype(low_type)
    gate_full, up_full, down_full = (
        lax.all_gather(w_gate, "shard", axis=0, tiled=True),
        lax.all_gather(w_up, "shard", axis=0, tiled=True),
        lax.all_gather(w_down, "shard", axis=0, tiled=True),
    )
    gate_pre = jnp.dot(ffn_low, gate_full, preferred_element_type=wide_type)
    up_pre = jnp.dot(ffn_low, up_full, preferred_element_type=wide_type)
    hidden, act_back = jax.vjp(swiglu, gate_pre, up_pre)
    hidden_low = hidden.astype(low_type)
    ffn_branch = jnp.dot(hidden_low, down_full, preferred_element_type=wide_type)
    layer_out = residual + residual_scale * ffn_branch
    grad_out = cotangent[0].astype(wide_type)
    grad_down_in = (residual_scale * grad_out).astype(low_type)
    gate_back_w, up_back_w, down_back_w = (
        lax.all_gather(w_gate, "shard", axis=0, tiled=True),
        lax.all_gather(w_up, "shard", axis=0, tiled=True),
        lax.all_gather(w_down, "shard", axis=0, tiled=True),
    )
    grad_hidden = outer_cols(grad_down_in, down_back_w)
    grad_gate_f, grad_up_f = act_back(grad_hidden)
    grad_gate = grad_gate_f.astype(low_type)
    grad_up = grad_up_f.astype(low_type)
    grad_ffn_in = outer_cols(grad_gate, gate_back_w) + outer_cols(grad_up, up_back_w)
    down_grad = lax.psum_scatter(
        inner_rows(hidden_low, grad_down_in).astype(jnp.bfloat16),
        "shard",
        scatter_dimension=0,
        tiled=True,
    )
    gate_up_in = jnp.concatenate([grad_gate, grad_up], axis=1)
    gate_up_grad = lax.psum_scatter(
        inner_rows(ffn_low, gate_up_in).astype(jnp.bfloat16),
        "shard",
        scatter_dimension=0,
        tiled=True,
    ).astype(jnp.float32)
    gate_grad = gate_up_grad[:, :FF]
    up_grad = gate_up_grad[:, FF:]
    grad_res_norm, grad_gain_ffn = norm_f_back(grad_ffn_in)
    grad_resid = grad_out + grad_res_norm
    qdown_back, qup_back, ldown_back, lup_back, aout_back = (
        lax.all_gather(query_down, "shard", axis=0, tiled=True),
        lax.all_gather(query_up, "shard", axis=0, tiled=True),
        lax.all_gather(latent_down, "shard", axis=0, tiled=True),
        lax.all_gather(latent_up, "shard", axis=0, tiled=True),
        lax.all_gather(attn_out, "shard", axis=0, tiled=True),
    )
    grad_branch = (residual_scale * grad_resid).astype(low_type)
    aout_grad = inner_rows(mixed_low, grad_branch)
    grad_mixed = outer_cols(grad_branch, aout_back).astype(low_type)
    grad_groups = grad_mixed.reshape(tok_rows, group_count, group_size, VD).transpose(1, 0, 2, 3)

    def backward_group(rope_acc, blocks):
        query_blk, key_blk, grad_blk, log_blk = blocks
        scores = scores_of(query_blk, key_blk)
        probs = jnp.exp(scores - log_blk)
        grad_probs = jnp.einsum(
            "thd,shd->hts", grad_blk, key_blk[..., ND:], preferred_element_type=wide_type
        )
        delta = jnp.sum(probs * grad_probs, axis=-1, keepdims=True)
        grad_scores = (probs * (grad_probs - delta)).astype(low_type)
        grad_query = (
            jnp.concatenate(
                [
                    jnp.einsum(
                        "hts,shd->thd",
                        grad_scores,
                        key_blk[..., :ND],
                        preferred_element_type=wide_type,
                    ),
                    jnp.einsum(
                        "hts,sd->thd", grad_scores, all_rope, preferred_element_type=wide_type
                    ),
                ],
                axis=-1,
            )
            * softmax_scale
        )
        grad_key = (
            jnp.einsum(
                "hts,thd->shd", grad_scores, query_blk[..., :ND], preferred_element_type=wide_type
            )
            * softmax_scale
        )
        grad_value = jnp.einsum(
            "hts,thd->shd", probs.astype(low_type), grad_blk, preferred_element_type=wide_type
        )
        rope_acc = (
            rope_acc
            + jnp.einsum(
                "hts,thd->sd", grad_scores, query_blk[..., ND:], preferred_element_type=wide_type
            )
            * softmax_scale
        )
        return (rope_acc, (grad_query, jnp.concatenate([grad_key, grad_value], axis=-1)))

    rope_start = jnp.zeros((seq_len, RD), wide_type)
    rope_sum, (grad_q_groups, grad_kv_groups) = lax.scan(
        backward_group, rope_start, (queries, key_groups, grad_groups, log_totals)
    )
    grad_kv_all = grad_kv_groups.transpose(1, 0, 2, 3).reshape(seq_len, H * (ND + VD))
    grad_kv_own, grad_rope_own = (
        lax.psum_scatter(
            grad_kv_all.astype(jnp.bfloat16), "rep", scatter_dimension=0, tiled=True
        ).astype(jnp.float32),
        lax.psum_scatter(
            rope_sum.astype(jnp.bfloat16), "rep", scatter_dimension=0, tiled=True
        ).astype(jnp.float32),
    )
    grad_q_full = grad_q_groups.transpose(1, 0, 2, 3).reshape(tok_rows, H, head_dim)
    grad_q_proj = query_back(grad_q_full)[0].reshape(tok_rows, H * head_dim).astype(low_type)
    qup_grad = inner_rows(query_low, grad_q_proj)
    grad_q_lat_f, grad_gain_query = norm_q_back(outer_cols(grad_q_proj, qup_back))
    grad_q_lat = grad_q_lat_f.astype(low_type)
    grad_kv_low = grad_kv_own.astype(low_type)
    lup_grad = inner_rows(latent_low, grad_kv_low)
    grad_lat_c, grad_gain_latent = norm_l_back(outer_cols(grad_kv_low, lup_back))
    grad_lat_r = key_back(grad_rope_own)[0]
    grad_lat = jnp.concatenate([grad_lat_c, grad_lat_r], axis=1).astype(low_type)
    qdown_grad = inner_rows(normed_low, grad_q_lat)
    ldown_grad = inner_rows(normed_low, grad_lat)
    grad_normed = outer_cols(grad_q_lat, qdown_back) + outer_cols(grad_lat, ldown_back)
    grad_in_norm, grad_gain_attn = norm_in_back(grad_normed)
    tokens_grad = (grad_resid + grad_in_norm).astype(low_type)
    (
        owned_gain_attn,
        owned_qdown,
        owned_gain_query,
        owned_qup,
        owned_ldown,
        owned_gain_latent,
        owned_lup,
        owned_aout,
        owned_gain_ffn,
    ) = (
        lax.psum_scatter(
            grad_gain_attn.astype(jnp.bfloat16), "shard", scatter_dimension=0, tiled=True
        ).astype(jnp.float32),
        lax.psum_scatter(
            qdown_grad.astype(jnp.bfloat16), "shard", scatter_dimension=0, tiled=True
        ).astype(jnp.float32),
        lax.psum_scatter(
            grad_gain_query.astype(jnp.bfloat16), "shard", scatter_dimension=0, tiled=True
        ).astype(jnp.float32),
        lax.psum_scatter(
            qup_grad.astype(jnp.bfloat16), "shard", scatter_dimension=0, tiled=True
        ).astype(jnp.float32),
        lax.psum_scatter(
            ldown_grad.astype(jnp.bfloat16), "shard", scatter_dimension=0, tiled=True
        ).astype(jnp.float32),
        lax.psum_scatter(
            grad_gain_latent.astype(jnp.bfloat16), "shard", scatter_dimension=0, tiled=True
        ).astype(jnp.float32),
        lax.psum_scatter(
            lup_grad.astype(jnp.bfloat16), "shard", scatter_dimension=0, tiled=True
        ).astype(jnp.float32),
        lax.psum_scatter(
            aout_grad.astype(jnp.bfloat16), "shard", scatter_dimension=0, tiled=True
        ).astype(jnp.float32),
        lax.psum_scatter(
            grad_gain_ffn.astype(jnp.bfloat16), "shard", scatter_dimension=0, tiled=True
        ).astype(jnp.float32),
    )
    summed = (
        lax.psum(owned_gain_attn.astype(jnp.bfloat16), "rep").astype(jnp.float32),
        lax.psum(owned_qdown.astype(jnp.bfloat16), "rep").astype(jnp.float32),
        lax.psum(owned_gain_query.astype(jnp.bfloat16), "rep").astype(jnp.float32),
        lax.psum(owned_qup.astype(jnp.bfloat16), "rep").astype(jnp.float32),
        lax.psum(owned_ldown.astype(jnp.bfloat16), "rep").astype(jnp.float32),
        lax.psum(owned_gain_latent.astype(jnp.bfloat16), "rep").astype(jnp.float32),
        lax.psum(owned_lup.astype(jnp.bfloat16), "rep").astype(jnp.float32),
        lax.psum(owned_aout.astype(jnp.bfloat16), "rep").astype(jnp.float32),
        lax.psum(owned_gain_ffn.astype(jnp.bfloat16), "rep").astype(jnp.float32),
        lax.psum(gate_grad.astype(jnp.bfloat16), "rep").astype(jnp.float32),
        lax.psum(up_grad.astype(jnp.bfloat16), "rep").astype(jnp.float32),
        lax.psum(down_grad, "rep").astype(jnp.float32),
    )
    return (
        layer_out.astype(low_type)[None],
        tokens_grad[None],
        summed[0],
        summed[1],
        summed[2],
        summed[3],
        summed[4],
        summed[5],
        summed[6],
        summed[7],
        summed[8],
        summed[9],
        summed[10],
        summed[11],
    )


def solution(mesh):
    placed = (
        P("shard", "rep", None),
        P("shard", "rep", None),
        P("shard", None),
        P("shard"),
        P("shard", None),
        P("shard"),
        P("shard", None),
        P("shard", None),
        P("shard"),
        P("shard", None),
        P("shard", None),
        P("shard"),
        P("shard", None),
        P("shard", None),
        P("shard", None),
    )
    return jax.shard_map(
        body,
        mesh=mesh,
        in_specs=placed,
        out_specs=(
            P("shard", "rep", None),
            P("shard", "rep", None),
            P("shard"),
            P("shard", None),
            P("shard"),
            P("shard", None),
            P("shard", None),
            P("shard"),
            P("shard", None),
            P("shard", None),
            P("shard"),
            P("shard", None),
            P("shard", None),
            P("shard", None),
        ),
        check_vma=False,
    )
```

profile of v0, /device:TPU:0, one launch (start us, length us, event | category | flops | bytes accessed | tf_op | source)
XLA Modules:
  0.0 3026.0 jit_solution(14104195124974946757)
XLA Ops:
  16.8 30.5 %all-reduce.14 = (bf16[2560]{0:T(1024)(128)(2,1)S(1)}, bf16[256]{0:T(256)(128)(2,1)S(1)}, bf16[768]{0:T(1024)(128)(2,1)S(1)}, bf16[2560]{0:T(1024)(128)(2,1)S(1)}) all-reduce(bf16[2560]{0:T(1024)(128)(2,1)S(1)} %dynamic-update-slice, bf16[256]{0:T(256)(128)(2,1)S(1)} %dynamic-update-slice.1, ...), channel_id=1, replica_groups=mesh['rep'=4,'shard'=8] {'shard'}, use_global_device_ids=true, to_apply=%add.5 | all-reduce | flops 6144 | bytes 24576
  54.2 20.2 all-gather.11.cloned.1.call-done
  89.8 30.0 all-gather.15.cloned.1.call-done
  122.8 58.9 %all-gather.17.cloned.1.call-done = bf16[768,3840]{1,0:T(8,128)(2,1)} async-done(((bf16[96,3840]{1,0:T(8,128)(2,1)}), bf16[768,3840]{1,0:T(8,128)(2,1)}) %all-gather.17.cloned.1.call-update) | async-done | bytes 5898256 | tf_op jit(solution)/shard_map/all_gather | solution.py:111
  187.1 57.0 %all-gather.13.cloned.1.call-done = bf16[512,5120]{1,0:T(8,128)(2,1)} async-done(((bf16[128,5120]{1,0:T(8,128)(2,1)}), bf16[512,5120]{1,0:T(8,128)(2,1)}) %all-gather.13.cloned.1.call-update) | async-done | bytes 5242896 | tf_op jit(solution)/shard_map/all_gather | solution.py:152
  244.1 8.4 copy.61
  252.5 20.7 while.28
  273.2 93.5 %all-gather.19.cloned.1.call-done = bf16[2560,2560]{1,0:T(8,128)(2,1)} async-done(((bf16[320,2560]{1,0:T(8,128)(2,1)}), bf16[2560,2560]{1,0:T(8,128)(2,1)}) %all-gather.19.cloned.1.call-update) | async-done | bytes 13107216 | tf_op jit(solution)/shard_map/all_gather | solution.py:115
  373.9 274.9 %all-gather.21.cloned.1.call-done = bf16[2560,6400]{1,0:T(8,128)(2,1)} async-done(((bf16[320,6400]{1,0:T(8,128)(2,1)}), bf16[2560,6400]{1,0:T(8,128)(2,1)}) %all-gather.21.cloned.1.call-update) | async-done | bytes 32768016 | tf_op jit(solution)/shard_map/all_gather | solution.py:191
  648.8 16.8 fusion.105
  665.5 265.3 %all-gather.23.cloned.1.call-done = bf16[2560,6400]{1,0:T(8,128)(2,1)} async-done(((bf16[320,6400]{1,0:T(8,128)(2,1)}), bf16[2560,6400]{1,0:T(8,128)(2,1)}) %all-gather.23.cloned.1.call-update) | async-done | bytes 32768016 | tf_op jit(solution)/shard_map/all_gather | solution.py:192
  930.8 16.8 fusion.106
  947.6 265.3 %all-gather.25.cloned.1.call-done = bf16[6400,2560]{1,0:T(8,128)(2,1)} async-done(((bf16[800,2560]{1,0:T(8,128)(2,1)}), bf16[6400,2560]{1,0:T(8,128)(2,1)}) %all-gather.25.cloned.1.call-update) | async-done | bytes 32768016 | tf_op jit(solution)/shard_map/all_gather | solution.py:193
  1212.9 19.2 multiply_convert_fusion.1
  1232.0 16.9 fusion.107
  1249.0 17.8 multiply_reduce_fusion.1
  1269.8 9.0 convolution_convert_fusion.8
  1279.2 50.7 %while.29 = (s32[]{:T(128)}, f32[512,32]{0,1:T(8,128)S(1)}, f32[5,128,8,96]{1,3,2,0:T(8,128)}, bf16[5,512,8,128]{1,3,2,0:T(8,128)(2,1)}, bf16[5,128,8,96]{1,3,2,...) while((s32[]{:T(128)}, f32[512,32]{0,1:T(8,128)S(1)}, ...), condition=%wide.region_15.16_spmd.clone, body=%wide.region_13.15_spmd.clone.sunk | while | flops 444513280 | bytes 52911448 | solution.py:287
  1338.8 14.1 reduce-scatter.30.cloned.1.call-done
  1353.9 64.3 %reduce-scatter.28.cloned.1.call-done = bf16[128,5120]{1,0:T(8,128)(2,1)} async-done(((bf16[512,5120]{1,0:T(8,128)(2,1)}), bf16[128,5120]{1,0:T(8,128)(2,1)}) %reduce-scatter.28.cloned.1.call-update) | async-done | bytes 1310736
  1426.5 26.3 convolution_convert_fusion
  1481.9 15.8 convolution_convert_fusion.1
  1499.6 588.7 %reduce-scatter.24.cloned.1.call-done = bf16[320,12800]{1,0:T(8,128)(2,1)} async-done(((bf16[2560,12800]{1,0:T(8,128)(2,1)}), bf16[320,12800]{1,0:T(8,128)(2,1)}) %reduce-scatter.24.cloned.1.call-update) | async-done | bytes 8192016 | tf_op jit(solution)/shard_map/reduce_scatter | solution.py:220
  2094.1 42.4 %reduce-scatter.16.cloned.1.call-done = bf16[320,768]{1,0:T(8,128)(2,1)} async-done(((bf16[2560,768]{1,0:T(8,128)(2,1)}), bf16[320,768]{1,0:T(8,128)(2,1)}) %reduce-scatter.16.cloned.1.call-update) | async-done | bytes 491536 | tf_op jit(solution)/shard_map/reduce_scatter | solution.py:328
  2136.5 67.1 %reduce-scatter.18.cloned.1.call-done = bf16[96,3840]{1,0:T(8,128)(2,1)} async-done(((bf16[768,3840]{1,0:T(8,128)(2,1)}), bf16[96,3840]{1,0:T(8,128)(2,1)}) %reduce-scatter.18.cloned.1.call-update) | async-done | bytes 737296 | tf_op jit(solution)/shard_map/reduce_scatter | solution.py:334
  2203.6 38.7 %reduce-scatter.20.cloned.1.call-done = bf16[32,5120]{1,0:T(8,128)(2,1)} async-done(((bf16[256,5120]{1,0:T(8,128)(2,1)}), bf16[32,5120]{1,0:T(8,128)(2,1)}) %reduce-scatter.20.cloned.1.call-update) | async-done | bytes 327696 | tf_op jit(solution)/shard_map/reduce_scatter | solution.py:343
  2242.3 135.4 %reduce-scatter.22.cloned.1.call-done = bf16[320,2560]{1,0:T(8,128)(2,1)} async-done(((bf16[2560,2560]{1,0:T(8,128)(2,1)}), bf16[320,2560]{1,0:T(8,128)(2,1)}) %reduce-scatter.22.cloned.1.call-update) | async-done | bytes 1638416 | tf_op jit(solution)/shard_map/reduce_scatter | solution.py:346
  2377.7 318.8 %reduce-scatter.26.cloned.1.call-done = bf16[800,2560]{1,0:T(8,128)(2,1)} async-done(((bf16[6400,2560]{1,0:T(8,128)(2,1)}), bf16[800,2560]{1,0:T(8,128)(2,1)}) %reduce-scatter.26.cloned.1.call-update) | async-done | bytes 4096016 | tf_op jit(solution)/shard_map/reduce_scatter | solution.py:213
  2702.1 15.2 fusion.46
  2718.2 25.9 all-reduce.13
  2744.4 10.1 all-reduce.15
  2758.0 238.8 %all-reduce.19.cloned.1.call-done = (bf16[320,768]{1,0:T(8,128)(2,1)}, bf16[96,3840]{1,0:T(8,128)(2,1)}, bf16[320,288]{0,1:T(8,128)(2,1)}, bf16[32,5120]{1,0:T(8...) async-done(((bf16[320,768]{1,0:T(8,128)(2,1)}, bf16[96,3840]{1,0:T(8,128)(2,1)}, ...) | async-done | bytes 15667216 | tf_op jit(solution)/shard_map/psum | solution.py:355
  (424 shorter events, 203.9 us)
Async XLA Ops:
  7.2 40.4 %all-gather.27.cloned.1.call-start = ((), (), s32[]{:S(2)}) async-start(), calls=%async_computation.23 | async-start | bytes 1990656 | tf_op jit(solution)/shard_map/all_gather | solution.py:112
  7.9 66.5 %all-gather.11.cloned.1.call-start = ((), (), s32[]{:S(2)}) async-start(), calls=%async_computation.9 | async-start | bytes 2949120 | tf_op jit(solution)/shard_map/all_gather | solution.py:114
  8.7 111.1 %all-gather.15.cloned.1.call-start = ((), (), s32[]{:S(2)}) async-start(), calls=%async_computation.11 | async-start | bytes 4423680 | tf_op jit(solution)/shard_map/all_gather | solution.py:109
  9.4 172.3 %all-gather.17.cloned.1.call-start = ((), (), s32[]{:S(2)}) async-start(), calls=%async_computation.12 | async-start | bytes 6635520 | tf_op jit(solution)/shard_map/all_gather | solution.py:111
  10.0 234.1 %all-gather.13.cloned.1.call-start = ((), (), s32[]{:S(2)}) async-start(), calls=%async_computation.10 | async-start | bytes 6553600 | tf_op jit(solution)/shard_map/all_gather | solution.py:152
  47.3 72.6 %copy-start.33 = (f32[2560]{0:T(1024)}, f32[2560]{0:T(1024)S(1)}, u32[]{:S(2)}) copy-start(f32[2560]{0:T(1024)S(1)} %convert_element_type.216) | copy-start | bytes 30724
  47.5 72.3 %copy-start.46 = (f32[128]{0:T(128)}, f32[128]{0:T(128)S(1)}, u32[]{:S(2)}) copy-start(f32[128]{0:T(128)S(1)} %fusion.84) | copy-start | bytes 1540
  77.8 288.8 %all-gather.19.cloned.1.call-start = ((), (), s32[]{:S(2)}) async-start(), calls=%async_computation.13 | async-start | bytes 14745600 | tf_op jit(solution)/shard_map/all_gather | solution.py:115
  78.4 570.3 %all-gather.21.cloned.1.call-start = ((), (), s32[]{:S(2)}) async-start(), calls=%async_computation.14 | async-start | bytes 36864000 | tf_op jit(solution)/shard_map/all_gather | solution.py:191
  79.2 851.6 %all-gather.23.cloned.1.call-start = ((), (), s32[]{:S(2)}) async-start(), calls=%async_computation.15 | async-start | bytes 36864000 | tf_op jit(solution)/shard_map/all_gather | solution.py:192
  79.9 1132.9 %all-gather.25.cloned.1.call-start = ((), (), s32[]{:S(2)}) async-start(), calls=%async_computation.16 | async-start | bytes 36864000 | tf_op jit(solution)/shard_map/all_gather | solution.py:193
  80.7 1272.2 %reduce-scatter.30.cloned.1.call-start = ((), (), s32[]{:S(2)}) async-start(), calls=%async_computation.25 | async-start | bytes 163840
  80.8 100.9 %copy-start.36 = (f32[768]{0:T(1024)}, f32[768]{0:T(1024)S(1)}, u32[]{:S(2)}) copy-start(f32[768]{0:T(1024)S(1)} %convert_element_type.223) | copy-start | bytes 9220
  81.4 105.5 %copy-start.39 = (f32[128,16]{0,1:T(8,128)}, f32[128,16]{0,1:T(8,128)S(1)}, u32[]{:S(2)}) copy-start(f32[128,16]{0,1:T(8,128)S(1)} %get-tuple-element.265) | copy-start | bytes 24580
  81.4 105.5 %copy-start.41 = (f32[128,16]{0,1:T(8,128)}, f32[128,16]{0,1:T(8,128)S(1)}, u32[]{:S(2)}) copy-start(f32[128,16]{0,1:T(8,128)S(1)} %get-tuple-element.266) | copy-start | bytes 24580
  273.2 93.5 %copy-start.23 = (bf16[5,128,8,64]{1,3,2,0:T(8,128)(2,1)}, bf16[5,128,8,64]{1,3,2,0:T(8,128)(2,1)S(1)}, u32[]{:S(2)}) copy-start(bf16[5,128,8,64]{1,3,2,0:T(8,128)(2,1)S(1)} %get-tuple-element.106) | copy-start | bytes 1966084
  373.6 893.2 %copy-start.4 = (f32[128,2560]{1,0:T(8,128)}, f32[128,2560]{1,0:T(8,128)S(1)}, u32[]{:S(2)}) copy-start(f32[128,2560]{1,0:T(8,128)S(1)} %get-tuple-element.272) | copy-start | bytes 3932164
  373.9 557.0 %copy-start.10 = (bf16[128,2560]{1,0:T(8,128)(2,1)}, bf16[128,2560]{1,0:T(8,128)(2,1)S(1)}, u32[]{:S(2)}) copy-start(bf16[128,2560]{1,0:T(8,128)(2,1)S(1)} %multiply_convert_fusion.4) | copy-start | bytes 1966084
  1330.7 87.5 %reduce-scatter.28.cloned.1.call-start = ((), (), s32[]{:S(2)}) async-start(), calls=%async_computation.24 | async-start | bytes 6553600
  1338.6 79.5 %copy-start.12 = (bf16[256,5120]{1,0:T(8,128)(2,1)S(1)}, bf16[256,5120]{1,0:T(8,128)(2,1)}, u32[]{:S(2)}) copy-start(bf16[256,5120]{1,0:T(8,128)(2,1)} %all-gather.11.cloned.1.call-done) | copy-start | bytes 7864324
  1338.7 79.5 %copy-start.30 = (f32[128,288]{0,1:T(8,128)S(1)}, f32[128,288]{0,1:T(8,128)}, u32[]{:S(2)}) copy-start(f32[128,288]{0,1:T(8,128)} %copy-done.29) | copy-start | bytes 442372
  1338.7 79.5 %copy-start.44 = (f32[256]{0:T(256)S(1)}, f32[256]{0:T(256)}, u32[]{:S(2)}) copy-start(f32[256]{0:T(256)} %copy-done.43) | copy-start | bytes 3076
  1338.7 79.5 %copy-start.49 = (f32[128]{0:T(128)S(1)}, f32[128]{0:T(128)}, u32[]{:S(2)}) copy-start(f32[128]{0:T(128)} %copy-done.48) | copy-start | bytes 1540
  1338.7 159.1 %reduce-scatter.32.cloned.1.call-start = ((), (), s32[]{:S(2)}) async-start(), calls=%async_computation.26 | async-start | bytes 2211840
  1353.9 66.7 %copy-start.3 = (bf16[1,128,2560]{2,1,0:T(8,128)(2,1)S(1)}, bf16[1,128,2560]{2,1,0:T(8,128)(2,1)}, u32[]{:S(2)}) copy-start(bf16[1,128,2560]{2,1,0:T(8,128)(2,1)} %param.19) | copy-start | bytes 1966084
  1426.4 661.9 %reduce-scatter.24.cloned.1.call-start = ((), (), s32[]{:S(2)}) async-start(), calls=%async_computation.21 | async-start | bytes 73728000 | tf_op jit(solution)/shard_map/reduce_scatter | solution.py:220
  1452.9 683.6 %reduce-scatter.16.cloned.1.call-start = ((), (), s32[]{:S(2)}) async-start(), calls=%async_computation.17 | async-start | bytes 4423680 | tf_op jit(solution)/shard_map/reduce_scatter | solution.py:328
  1464.2 739.4 %reduce-scatter.18.cloned.1.call-start = ((), (), s32[]{:S(2)}) async-start(), calls=%async_computation.18 | async-start | bytes 6635520 | tf_op jit(solution)/shard_map/reduce_scatter | solution.py:334
  1468.7 773.6 %reduce-scatter.20.cloned.1.call-start = ((), (), s32[]{:S(2)}) async-start(), calls=%async_computation.19 | async-start | bytes 2949120 | tf_op jit(solution)/shard_map/reduce_scatter | solution.py:343
  1472.6 905.1 %reduce-scatter.22.cloned.1.call-start = ((), (), s32[]{:S(2)}) async-start(), calls=%async_computation.20 | async-start | bytes 14745600 | tf_op jit(solution)/shard_map/reduce_scatter | solution.py:346
  1480.9 1215.6 %reduce-scatter.26.cloned.1.call-start = ((), (), s32[]{:S(2)}) async-start(), calls=%async_computation.22 | async-start | bytes 36864000 | tf_op jit(solution)/shard_map/reduce_scatter | solution.py:213
  1497.7 1499.1 %all-reduce.19.cloned.1.call-start = ((), (), s32[]{:S(2)}) async-start(), calls=%async_computation.27 | async-start | bytes 31408128 | tf_op jit(solution)/shard_map/psum | solution.py:355
  (75 other events, 820.1 us)
Sparse Core Ops, SparseCore 0:
  9.7 29.5 all-gather.26
  40.9 33.4 all-gather.10
  76.0 43.7 all-gather.14
  121.3 60.3 all-gather.16
  184.0 60.0 all-gather.12
  245.6 121.0 all-gather.18
  368.3 280.4 all-gather.20
  650.4 280.3 all-gather.22
  932.4 280.3 all-gather.24
  1330.8 22.0 reduce-scatter.29
  1356.7 61.4 reduce-scatter.27
  1426.5 35.5 reduce-scatter.31
  1464.5 623.7 reduce-scatter.23
  2090.6 45.8 reduce-scatter.15
  2139.3 64.2 reduce-scatter.17
  2206.3 35.8 reduce-scatter.19
  2244.4 133.1 reduce-scatter.21
  2379.9 316.4 reduce-scatter.25
  2702.9 293.9 all-reduce.18
where the time goes:
time: 3030 us
  waiting for transfers between devices  2580 us (85%)
  matrix products  238 us (8%)
  blocking collectives  74.5 us (2%)
  local copies, waits for them, and re-layouts  69.6 us (2%)
  other arithmetic  44.7 us (1%)
    reduce_scatter x1, waiting for transfers between devices, body(): lax.psum_scatter(inner_rows(ffn_low, gate_up_in).astype(jnp.bfloat16), 's...  589 us
    reduce_scatter x1, waiting for transfers between devices, body(): lax.psum_scatter(inner_rows(hidden_low, grad_down_in).astype(jnp.bfloat16...  319 us
    all_gather x1, waiting for transfers between devices, body(): lax.all_gather(w_gate, 'shard', axis=0, tiled=True)  275 us
    all_gather x1, waiting for transfers between devices, body(): lax.all_gather(w_up, 'shard', axis=0, tiled=True)  265 us
    all_gather x1, waiting for transfers between devices, body(): lax.all_gather(w_down, 'shard', axis=0, tiled=True)  265 us
    psum x1, waiting for transfers between devices, body(): lax.psum(owned_qdown.astype(jnp.bfloat16), 'rep').astype(jnp.float32)  239 us
    reduce_scatter x1, waiting for transfers between devices, body(): lax.psum_scatter(aout_grad.astype(jnp.bfloat16), 'shard', scatter_dimensi...  135 us
    all_gather x1, waiting for transfers between devices, body(): lax.all_gather(attn_out, 'shard', axis=0, tiled=True)  93.5 us
  transfers between devices with their start and end apart: 19, of which 17 were waited for; matrix products, arithmetic and copies ran while one was open for 7% of the time, Pallas kernels for 0%

commit v1 on v0

--- a/solution.py
+++ b/solution.py
@@ -1,8 +1,11 @@
+import functools
 import math
 
 import jax
 import jax.numpy as jnp
 from jax import lax
+from jax.experimental import pallas as pl
+from jax.experimental.pallas import tpu as pltpu
 from jax.sharding import PartitionSpec as P
 
 KR = 256
@@ -60,6 +63,1011 @@
 def outer_cols(leading, trailing):
     return lax.dot_general(
         leading, trailing, (((1,), (1,)), ((), ())), preferred_element_type=jnp.float32
+    )
+
+
+MESH = pl.DeviceIdType.MESH
+ANY = pl.BlockSpec(memory_space=pl.ANY)
+
+def place():
+    rep = lax.axis_index("rep")
+    shard = lax.axis_index("shard")
+    zpos, core = shard // 2, shard % 2
+    return rep, zpos, core
+
+def mult(value, by):
+    return pl.multiple_of(value, by)
+
+def greet(rep, zpos, core, plane=0, column=False):
+    barrier = pltpu.get_barrier_semaphore()
+    shard = zpos * 2 + core
+
+    def signal(r, s):
+        pl.semaphore_signal(barrier, inc=1, device_id=(r, s), device_id_type=MESH)
+
+    if column:
+        for m in range(1, 8):
+            signal(rep, column_place(zpos, core, m))
+        count = 7
+    else:
+        signal(rep, zpos * 2 + 1 - core)
+
+        @pl.when(zpos > 0)
+        def _():
+            signal(rep, shard - 2)
+
+        @pl.when(zpos < 3)
+        def _():
+            signal(rep, shard + 2)
+
+        count = 1 + jnp.minimum(zpos, 1) + jnp.minimum(3 - zpos, 1)
+    if plane:
+        for other in plane_places(rep)[:plane]:
+            signal(other, shard)
+        count = count + plane
+    pl.semaphore_wait(barrier, count)
+
+
+def plane_places(rep):
+    return rep + 1 - 2 * (rep % 2), (rep + 2) % 4, 3 - rep
+
+
+def column_place(zpos, core, m, back=False):
+    step = 4 - m // 2 if back else m // 2
+    return ((zpos + step) % 4) * 2 + (core + m) % 2
+
+
+def remote(src, dst, ssem, rsem, r, s):
+    return pltpu.make_async_remote_copy(
+        src_ref=src, dst_ref=dst, send_sem=ssem, recv_sem=rsem, device_id=(r, s), device_id_type=MESH
+    )
+
+
+def dma_sems(*dims):
+    return pltpu.SemaphoreType.DMA(dims)
+
+
+class Gather:
+    def __init__(self, ins, outs, sems):
+        self.ins, self.outs = ins, outs
+        self.zsend, self.zrecv, self.csend, self.crecv, self.own = sems
+        self.rep, self.zpos, self.core = place()
+        self.held = None
+
+    @staticmethod
+    def scratch(n):
+        return [dma_sems(2, 3, n), dma_sems(2, 3, n), dma_sems(7, n), dma_sems(7, n), dma_sems(2, n)]
+
+    def at(self, a, z, c):
+        rows = self.ins[a].shape[0]
+        return self.outs[a].at[pl.ds(mult((z * 2 + c) * rows, rows), rows)]
+
+    def hop_copy(self, a, way, hop, z, src=None):
+        dst = self.at(a, z, self.core)
+        return remote(dst if src is None else src, dst, self.zsend.at[way, hop, a], self.zrecv.at[way, hop, a],
+                      self.rep, (self.zpos + (1 - 2 * way)) * 2 + self.core)
+
+    def core_copy(self, a, slot, z, c, src=None):
+        dst = self.at(a, z, c)
+        return remote(dst if src is None else src, dst, self.csend.at[slot, a], self.crecv.at[slot, a],
+                      self.rep, self.zpos * 2 + 1 - self.core)
+
+    def keep(self, a):
+        return pltpu.make_async_copy(self.ins[a], self.at(a, self.zpos, self.core), self.own.at[0, a])
+
+    def onward(self, way):
+        return self.zpos < 3 if way == 0 else self.zpos > 0
+
+    def source(self, way, hop):
+        z = self.zpos - hop if way == 0 else self.zpos + hop
+        return z, (z >= 0 if way == 0 else z <= 3)
+
+    def start(self, which=None):
+        which = range(len(self.ins)) if which is None else which
+        for way in range(2):
+            @pl.when(self.onward(way))
+            def _():
+                for a in which:
+                    self.hop_copy(a, way, 0, self.zpos, src=self.ins[a]).start()
+        for a in which:
+            self.core_copy(a, 0, self.zpos, self.core, src=self.ins[a]).start()
+            self.keep(a).start()
+
+    def hop(self, hop, which=None):
+        which = range(len(self.ins)) if which is None else which
+        for way in range(2):
+            z, there = self.source(way, hop)
+
+            @pl.when(there)
+            def _():
+                for a in which:
+                    self.hop_copy(a, way, hop - 1, z).wait_recv()
+                    if hop < 3:
+                        @pl.when(self.onward(way))
+                        def _():
+                            self.hop_copy(a, way, hop, z).start()
+                    self.core_copy(a, way * 3 + hop, z, self.core).start()
+
+    def finish(self):
+        arrays = range(len(self.ins))
+        for way in range(2):
+            for hop in range(3):
+                z, there = self.source(way, hop)
+
+                @pl.when(there & self.onward(way))
+                def _():
+                    for a in arrays:
+                        self.hop_copy(a, way, hop, z).wait_send()
+        for a in arrays:
+            self.keep(a).wait()
+            self.core_copy(a, 0, self.zpos, self.core, src=self.ins[a]).wait_send()
+            self.core_copy(a, 0, self.zpos, 1 - self.core).wait_recv()
+        for way in range(2):
+            for hop in range(1, 4):
+                z, there = self.source(way, hop)
+
+                @pl.when(there)
+                def _():
+                    for a in arrays:
+                        self.core_copy(a, way * 3 + hop, z, self.core).wait_send()
+                        self.core_copy(a, way * 3 + hop, z, 1 - self.core).wait_recv()
+
+
+class Total:
+    def __init__(self, term, out, bufs, sems):
+        self.term, self.out = term, out
+        self.mine, self.theirs, self.stage, self.landed = bufs
+        self.zsend, self.zrecv, self.csend, self.crecv, self.own = sems
+        self.rep, self.zpos, self.core = place()
+
+    @staticmethod
+    def scratch(term):
+        four = pltpu.VMEM((4,) + term.shape[1:], term.dtype)
+        return [four] * 3 + [pltpu.VMEM((2, 4) + term.shape[1:], term.dtype),
+                             dma_sems(2, 4), dma_sems(2, 4), dma_sems(4), dma_sems(4), dma_sems(4)]
+
+    def pair_copy(self, z):
+        return remote(self.term.at[z * 2 + 1 - self.core], self.theirs.at[z], self.csend.at[z], self.crecv.at[z],
+                      self.rep, self.zpos * 2 + 1 - self.core)
+
+    def load(self, z):
+        return pltpu.make_async_copy(self.term.at[z * 2 + self.core], self.mine.at[z], self.own.at[z])
+
+    def hop_copy(self, way, z):
+        return remote(self.stage.at[z], self.landed.at[way, z], self.zsend.at[way, z], self.zrecv.at[way, z],
+                      self.rep, (self.zpos + (1 - 2 * way)) * 2 + self.core)
+
+    def each(self, step):
+        for way in range(2):
+            behind = self.zpos if way == 0 else 3 - self.zpos
+            target = self.zpos + 3 - step if way == 0 else self.zpos - 3 + step
+            yield way, behind, target, (behind <= step) & (behind < 3)
+
+    def start(self):
+        for z in (3, 0, 2, 1):
+            self.pair_copy(z).start()
+            self.load(z).start()
+
+    def pair(self):
+        for z in (3, 0, 2, 1):
+            self.load(z).wait()
+            self.pair_copy(z).wait_recv()
+
+    def step(self, step):
+        wide = jnp.float32
+        for way, behind, target, there in self.each(step):
+            @pl.when(there)
+            def _():
+                total = self.mine[target].astype(wide) + self.theirs[target].astype(wide)
+
+                @pl.when(behind == 0)
+                def _():
+                    self.stage[target] = total.astype(self.stage.dtype)
+
+                @pl.when(behind > 0)
+                def _():
+                    self.hop_copy(way, target).wait_recv()
+                    self.stage[target] = (total + self.landed[way, target].astype(wide)).astype(self.stage.dtype)
+                self.hop_copy(way, target).start()
+
+    def finish(self):
+        wide = jnp.float32
+        self.out[...] = self.mine[self.zpos].astype(wide) + self.theirs[self.zpos].astype(wide)
+        for way in range(2):
+            @pl.when(self.zpos > 0 if way == 0 else self.zpos < 3)
+            def _():
+                self.hop_copy(way, self.zpos).wait_recv()
+                self.out[...] += self.landed[way, self.zpos].astype(wide)
+        for step in range(3):
+            for way, behind, target, there in self.each(step):
+                @pl.when(there)
+                def _():
+                    self.hop_copy(way, target).wait_send()
+        for z in range(4):
+            self.pair_copy(z).wait_send()
+
+
+def kernel_params(cid):
+    return pltpu.CompilerParams(collective_id=cid, has_side_effects=True, vmem_limit_bytes=56 * 2**20)
+
+
+VMEM = pl.BlockSpec(memory_space=pltpu.VMEM)
+
+
+def chain_gather_kernel(n, *refs):
+    gather = Gather(refs[:n], refs[n : 2 * n], refs[2 * n :])
+    greet(*place())
+    gather.start()
+    for hop in range(1, 4):
+        gather.hop(hop)
+    gather.finish()
+
+
+def chain_gather(cid, *arrays):
+    n = len(arrays)
+    out = [jax.ShapeDtypeStruct((a.shape[0] * 8,) + a.shape[1:], a.dtype) for a in arrays]
+    return pl.pallas_call(
+        functools.partial(chain_gather_kernel, n), out_shape=out, in_specs=[ANY] * n, out_specs=[ANY] * n,
+        scratch_shapes=Gather.scratch(n), compiler_params=kernel_params(cid),
+    )(*arrays)
+
+
+def chain_sum_kernel(term, out, *refs):
+    total = Total(term, out, refs[:4], refs[4:])
+    greet(*place())
+    total.start()
+    total.pair()
+    for step in range(3):
+        total.step(step)
+    total.finish()
+
+
+def chain_sum(cid, term):
+    return pl.pallas_call(
+        chain_sum_kernel, out_shape=jax.ShapeDtypeStruct(term.shape[1:], jnp.float32), in_specs=[ANY], out_specs=VMEM,
+        scratch_shapes=Total.scratch(term), compiler_params=kernel_params(cid),
+    )(term)
+
+
+def late_kernel(*refs):
+    branch, lat, cols, term, parts, down = refs[:6]
+    branch_all, lat_all, cols_all, out, parts_all, down_all = refs[6:12]
+    scratch = list(refs[12:])
+    rep, zpos, core = place()
+    shard = zpos * 2 + core
+    xrep, yrep, drep = plane_places(rep)
+    gather = Gather((branch, lat), (branch_all, lat_all), scratch[:5])
+    total = Total(term, out, scratch[5:9], scratch[9:14])
+    asend, arecv, esend, erecv, psend, precv, dsend, drecv, own = scratch[14:]
+
+    def cols_copy(m, back=False):
+        s2 = column_place(zpos, core, m, back)
+        here = cols_all.at[s2 if back else shard]
+        return remote(cols.at[s2], here, asend.at[m - 1], arecv.at[m - 1], rep, s2)
+
+    def parts_copy(m, which, back=False):
+        s2 = column_place(zpos, core, m, back)
+        return remote(parts.at[s2, which], parts_all.at[s2 if back else shard, rep, which],
+                      esend.at[m - 1, which], erecv.at[m - 1, which], rep, s2)
+
+    def parts_plane(m, which, quarter, kind, r):
+        ref = parts_all.at[column_place(zpos, core, m, True), quarter, which]
+        src = parts.at[shard, which] if m == 0 and kind < 2 else ref
+        return remote(src, ref, psend.at[kind, m, which], precv.at[kind, m, which], r, shard)
+
+    def down_plane(half, quarter, kind, r):
+        width = down.shape[1] // 2
+        at = (slice(None), pl.ds(half * width, width))
+        dst = down_all.at[(quarter,) + at]
+        return remote(down.at[at] if kind < 2 else dst, dst, dsend.at[kind, half], drecv.at[kind, half], r, shard)
+
+    def own_copies():
+        return (pltpu.make_async_copy(cols.at[shard], cols_all.at[shard], own.at[0]),
+                pltpu.make_async_copy(parts.at[shard], parts_all.at[shard, rep], own.at[1]),
+                pltpu.make_async_copy(down, down_all.at[rep], own.at[2]))
+
+    greet(rep, zpos, core, plane=2, column=True)
+    near = (1, 2, 6, 3, 7, 4, 5)
+    for m in near:
+        for which in range(2):
+            parts_copy(m, which).start()
+    total.start()
+    for half in range(2):
+        down_plane(half, rep, 0, xrep).start()
+        down_plane(half, rep, 1, yrep).start()
+        parts_plane(0, half, rep, 0, xrep).start()
+        parts_plane(0, half, rep, 1, yrep).start()
+    gather.start()
+    for m in near:
+        cols_copy(m).start()
+    for copy in own_copies():
+        copy.start()
+
+    def onward(kind_of, half, *first):
+        kind_of(*first, half, xrep, 0, xrep).wait_recv()
+        kind_of(*first, half, yrep, 1, yrep).wait_recv()
+        if half == 0:
+            kind_of(*first, half, xrep, 2, yrep).start()
+        else:
+            kind_of(*first, half, yrep, 2, xrep).start()
+
+    def from_column(m):
+        for which in range(2):
+            parts_copy(m, which, True).wait_recv()
+            parts_plane(m, which, rep, 0, xrep).start()
+            parts_plane(m, which, rep, 1, yrep).start()
+
+    total.pair()
+    total.step(0)
+    for m in near[:3]:
+        from_column(m)
+    for half in range(2):
+        onward(down_plane, half)
+        onward(parts_plane, half, 0)
+    gather.hop(1)
+    total.step(1)
+    for m in near[3:]:
+        from_column(m)
+    for m in near[:3]:
+        for half in range(2):
+            onward(parts_plane, half, m)
+    gather.hop(2)
+    total.step(2)
+    for m in near[3:]:
+        for half in range(2):
+            onward(parts_plane, half, m)
+    gather.hop(3)
+    total.finish()
+    gather.finish()
+    for m in near:
+        cols_copy(m).wait_send()
+        cols_copy(m, True).wait_recv()
+        for which in range(2):
+            parts_copy(m, which).wait_send()
+
+    def settle(kind_of, half, *first):
+        kind_of(*first, half, rep, 0, xrep).wait_send()
+        kind_of(*first, half, rep, 1, yrep).wait_send()
+        if half == 0:
+            kind_of(*first, half, xrep, 2, yrep).wait_send()
+        else:
+            kind_of(*first, half, yrep, 2, xrep).wait_send()
+        kind_of(*first, half, drep, 2, drep).wait_recv()
+
+    for half in range(2):
+        settle(down_plane, half)
+        for m in range(8):
+            settle(parts_plane, half, m)
+    for copy in own_copies():
+        copy.wait()
+
+
+def late_exchange(cid, branch, lat, cols, term, parts, down):
+    out = [jax.ShapeDtypeStruct((8 * branch.shape[0], branch.shape[1]), branch.dtype),
+           jax.ShapeDtypeStruct((8 * lat.shape[0], lat.shape[1]), lat.dtype),
+           jax.ShapeDtypeStruct(cols.shape, cols.dtype),
+           jax.ShapeDtypeStruct(term.shape[1:], jnp.float32),
+           jax.ShapeDtypeStruct((8, 4) + parts.shape[1:], parts.dtype),
+           jax.ShapeDtypeStruct((4,) + down.shape, down.dtype)]
+    return pl.pallas_call(
+        late_kernel, out_shape=out, in_specs=[ANY] * 6, out_specs=[ANY, ANY, ANY, VMEM, ANY, ANY],
+        scratch_shapes=Gather.scratch(2) + Total.scratch(term) + [
+            dma_sems(7), dma_sems(7), dma_sems(7, 2), dma_sems(7, 2), dma_sems(3, 8, 2), dma_sems(3, 8, 2),
+            dma_sems(3, 2), dma_sems(3, 2), dma_sems(3)],
+        compiler_params=kernel_params(cid),
+    )(branch, lat, cols, term, parts, down)
+
+
+def last_kernel(n, *refs):
+    terms, gain = refs[:n], refs[n]
+    outs, gain_out = refs[n + 1 : 2 * n + 1], refs[2 * n + 1]
+    scratch = list(refs[2 * n + 2 :])
+    landed, sums = scratch[:n], scratch[n : 2 * n]
+    gain_landed, gain_sum, gain_plane, ssend, srecv, tsend, trecv, gsend, grecv, hsend, hrecv = scratch[2 * n :]
+    rep, zpos, core = place()
+    shard = zpos * 2 + core
+    places = plane_places(rep)
+    wide = jnp.float32
+    greet(rep, zpos, core, plane=3, column=True)
+
+    def term_copy(a, k):
+        return remote(terms[a].at[places[k]], landed[a].at[k], ssend.at[k, a], srecv.at[k, a], places[k], shard)
+
+    def sum_copy(a, k, back=False):
+        return remote(sums[a], outs[a].at[places[k] if back else rep], tsend.at[k, a], trecv.at[k, a], places[k], shard)
+
+    def gain_copy(m):
+        s2 = column_place(zpos, core, m)
+        return remote(gain.at[s2], gain_landed.at[m - 1], gsend.at[m - 1], grecv.at[m - 1], rep, s2)
+
+    def gain_on(k):
+        return remote(gain_sum, gain_plane.at[k], hsend.at[k], hrecv.at[k], places[k], shard)
+
+    for m in range(1, 8):
+        gain_copy(m).start()
+    for a in range(n):
+        for k in range(3):
+            term_copy(a, k).start()
+    gain_sum[...] = gain[shard]
+    for m in range(1, 8):
+        gain_copy(m).wait_recv()
+        gain_sum[...] += gain_landed[m - 1]
+    for k in range(3):
+        gain_on(k).start()
+    for a in range(n):
+        total = terms[a][rep].astype(wide)
+        for k in range(3):
+            term_copy(a, k).wait_recv()
+            total = total + landed[a][k].astype(wide)
+        sums[a][...] = total.astype(jnp.bfloat16)
+        for k in range(3):
+            sum_copy(a, k).start()
+        outs[a][rep] = sums[a][...]
+    gain_out[...] = gain_sum[...]
+    for k in range(3):
+        gain_on(k).wait_recv()
+        gain_out[...] += gain_plane[k]
+    for k in range(3):
+        gain_on(k).wait_send()
+        for a in range(n):
+            term_copy(a, k).wait_send()
+            sum_copy(a, k).wait_send()
+            sum_copy(a, k, True).wait_recv()
+    for m in range(1, 8):
+        gain_copy(m).wait_send()
+
+
+def last_sums(cid, terms, gain):
+    n = len(terms)
+    out = [jax.ShapeDtypeStruct(t.shape, jnp.bfloat16) for t in terms] + [jax.ShapeDtypeStruct(gain.shape[1:], gain.dtype)]
+    block = pltpu.VMEM(gain.shape[1:], gain.dtype)
+    return pl.pallas_call(
+        functools.partial(last_kernel, n), out_shape=out, in_specs=[VMEM] * (n + 1), out_specs=[VMEM] * (n + 1),
+        scratch_shapes=[pltpu.VMEM((3,) + t.shape[1:], t.dtype) for t in terms]
+        + [pltpu.VMEM(t.shape[1:], t.dtype) for t in terms]
+        + [pltpu.VMEM((7,) + gain.shape[1:], gain.dtype), block, pltpu.VMEM((3,) + gain.shape[1:], gain.dtype)]
+        + [dma_sems(3, n)] * 4 + [dma_sems(7)] * 2 + [dma_sems(3)] * 2,
+        compiler_params=kernel_params(cid),
+    )(*terms, gain)
+
+def start_kernel(*refs):
+    ins, (gate, up) = refs[:7], refs[7:9]
+    outs, cols = refs[9:16], refs[16:18]
+    (zsend, zrecv, xsend, xrecv, ysend, yrecv, dsend, drecv, csend, crecv, own, gsend, grecv, psend, precv) = refs[18:33]
+    held, strips = refs[33:40], refs[40:42]
+    rep, zpos, core = place()
+    xrep, yrep, drep = plane_places(rep)
+    shard = zpos * 2 + core
+
+    def whole(a, z, c):
+        rows = ins[a].shape[0]
+        return outs[a].at[pl.ds(mult((z * 2 + c) * rows, rows), rows)]
+
+    def pieces(a, z, c, quarter, act, own_ref=False):
+        def part(b, first, rows):
+            full = ins[b].shape[0]
+            if own_ref:
+                return ins[b].at[pl.ds(mult(first, 16), rows)]
+            return outs[b].at[pl.ds(mult((z * 2 + c) * full + first, 16), rows)]
+
+        if a < 3:
+            rows = ins[a].shape[0] // 4
+            act(part(a, quarter * rows, rows))
+        elif a == 3:
+            @pl.when(quarter < 3)
+            def _():
+                act(part(3, jnp.minimum(quarter, 2) * 32, 32))
+
+            @pl.when(quarter == 3)
+            def _():
+                act(part(4, 0, 32))
+        else:
+            act(ins[a + 1] if own_ref else whole(a + 1, z, c))
+
+    copy = remote
+
+    def hop(a, way, h, z, what):
+        def act(ref):
+            c = copy(ref, ref, zsend.at[way, h, a], zrecv.at[way, h, a], rep, (zpos + 1 - 2 * way) * 2 + core)
+            getattr(c, what)()
+        pieces(a, z, core, rep, act)
+
+    def to_plane(a, k, z, quarter, what, sems, r):
+        def act(ref):
+            getattr(copy(ref, ref, sems[0].at[k, a], sems[1].at[k, a], r, shard), what)()
+        pieces(a, z, core, quarter, act)
+
+    def to_core(a, slot, z, c, what, src=None):
+        ref = whole(a, z, c)
+        getattr(copy(ref if src is None else src, ref, csend.at[slot, a], crecv.at[slot, a], rep, zpos * 2 + 1 - core), what)()
+
+    greet(rep, zpos, core, plane=2, column=True)
+    def send_own(a):
+        def first(way):
+            def go(src):
+                def act(ref):
+                    copy(src, ref, zsend.at[way, 0, a], zrecv.at[way, 0, a], rep, (zpos + 1 - 2 * way) * 2 + core).start()
+                return act
+            return go
+        for way in range(2):
+            @pl.when(zpos < 3 if way == 0 else zpos > 0)
+            def _():
+                if a < 3:
+                    rows = ins[a].shape[0] // 4
+                    src = ins[a].at[pl.ds(mult(rep * rows, 16), rows)]
+                    pieces(a, zpos, core, rep, first(way)(src))
+                elif a == 3:
+                    @pl.when(rep < 3)
+                    def _():
+                        start = mult(jnp.minimum(rep, 2) * 32, 16)
+                        src = ins[3].at[pl.ds(start, 32)]
+                        dst = outs[3].at[pl.ds(mult(shard * 96 + start, 16), 32)]
+                        first(way)(src)(dst)
+
+                    @pl.when(rep == 3)
+                    def _():
+                        first(way)(ins[4])(whole(4, zpos, core))
+                else:
+                    first(way)(ins[a + 1])(whole(a + 1, zpos, core))
+
+    def keep(a, half):
+        if half == 0:
+            return pltpu.make_async_copy(ins[a], held[a], own.at[0, a])
+        return pltpu.make_async_copy(held[a], whole(a, zpos, core), own.at[1, a])
+
+    for a in range(4):
+        send_own(a)
+
+    strip = cols[0].shape[1]
+    quarter_rows = gate.shape[0] // 4
+
+    def slice_of(which, s, first, rows):
+        start = mult((s * 25 // 4) * 128, 128)
+        return (gate, up)[which].at[pl.ds(mult(first, 16), rows), pl.ds(start, strip)]
+
+    def rows_of(which, s, quarter):
+        return cols[which].at[pl.ds(mult(s * gate.shape[0] + quarter * quarter_rows, 16), quarter_rows)]
+
+    def slice_copy(m, which):
+        s2 = column_place(zpos, core, m)
+        return remote(slice_of(which, s2, rep * quarter_rows, quarter_rows), rows_of(which, shard, rep),
+                      gsend.at[m - 1, which], grecv.at[m - 1, which], rep, s2)
+
+    def slice_plane(m, which, quarter, kind, r):
+        ref = rows_of(which, column_place(zpos, core, m, back=True), quarter)
+        return remote(ref, ref, psend.at[kind, m - 1, which], precv.at[kind, m - 1, which], r, shard)
+
+    def own_slice(which, half):
+        if half == 0:
+            return pltpu.make_async_copy(slice_of(which, shard, 0, gate.shape[0]), strips[which], own.at[0, 7 + which])
+        rows = gate.shape[0]
+        return pltpu.make_async_copy(strips[which], cols[which].at[pl.ds(mult(shard * rows, rows), rows)], own.at[1, 7 + which])
+
+    near = (1, 2, 6, 3, 7, 4, 5)
+    for a in range(7):
+        to_core(a, 0, zpos, core, "start", src=ins[a])
+        keep(a, 0).start()
+    for which in range(2):
+        own_slice(which, 0).start()
+    for a in range(7):
+        keep(a, 0).wait()
+        keep(a, 1).start()
+    for which in range(2):
+        own_slice(which, 0).wait()
+        own_slice(which, 1).start()
+
+    def slices_from_column(m):
+        for which in range(2):
+            s2 = column_place(zpos, core, m, back=True)
+            ref = rows_of(which, s2, rep)
+            remote(ref, ref, gsend.at[m - 1, which], grecv.at[m - 1, which], rep, s2).wait_recv()
+            slice_plane(m, which, rep, 0, xrep).start()
+            slice_plane(m, which, rep, 1, yrep).start()
+
+    def slices_from_plane(m):
+        for which in range(2):
+            slice_plane(m, which, xrep, 0, xrep).wait_recv()
+            slice_plane(m, which, yrep, 1, yrep).wait_recv()
+            if which == 0:
+                slice_plane(m, which, xrep, 2, yrep).start()
+            else:
+                slice_plane(m, which, yrep, 2, xrep).start()
+
+    def from_column(h, way, z, slots=range(4)):
+        for a in slots:
+            hop(a, way, h - 1, z, "wait_recv")
+            if h < 3:
+                @pl.when(zpos < 3 if way == 0 else zpos > 0)
+                def _():
+                    hop(a, way, h, z, "start")
+            if a < 4:
+                to_plane(a, way * 3 + h - 1, z, rep, "start", (xsend, xrecv), xrep)
+                to_plane(a, way * 3 + h - 1, z, rep, "start", (ysend, yrecv), yrep)
+            else:
+                to_core(a + 1, way * 3 + h, z, core, "start")
+
+    def from_plane(h, way, z):
+        k = way * 3 + h - 1
+        for a in range(4):
+            to_plane(a, k, z, xrep, "wait_recv", (xsend, xrecv), xrep)
+            if a == 0:
+                to_plane(a, k, z, xrep, "start", (dsend, drecv), yrep)
+            to_plane(a, k, z, yrep, "wait_recv", (ysend, yrecv), yrep)
+            if a > 0:
+                to_plane(a, k, z, yrep, "start", (dsend, drecv), xrep)
+
+    def from_corner(h, way, z):
+        k = way * 3 + h - 1
+        for a in range(4):
+            to_plane(a, k, z, drep, "wait_recv", (dsend, drecv), drep)
+        for a in range(5):
+            to_core(a, k + 1, z, core, "start")
+
+    def by_hop(stage, h, *more):
+        for way in range(2):
+            z = zpos - h if way == 0 else zpos + h
+
+            @pl.when(z >= 0 if way == 0 else z <= 3)
+            def _():
+                stage(h, way, z, *more)
+
+    by_hop(from_column, 1)
+    by_hop(from_column, 2)
+    for m in near:
+        for which in range(2):
+            slice_copy(m, which).start()
+    by_hop(from_plane, 1)
+    by_hop(from_column, 3)
+    by_hop(from_plane, 2)
+    by_hop(from_corner, 1)
+    for m in near[:3]:
+        slices_from_column(m)
+    send_own(4)
+    send_own(5)
+    by_hop(from_plane, 3)
+    for m in near[3:]:
+        slices_from_column(m)
+    by_hop(from_corner, 2)
+    for m in near[:3]:
+        slices_from_plane(m)
+    by_hop(from_column, 1, (5, 4))
+    by_hop(from_corner, 3)
+    for m in near[3:]:
+        slices_from_plane(m)
+    by_hop(from_column, 2, (5, 4))
+    by_hop(from_column, 3, (5, 4))
+    for a in range(7):
+        to_core(a, 0, zpos, core, "wait_send", src=ins[a])
+        to_core(a, 0, zpos, 1 - core, "wait_recv")
+        keep(a, 1).wait()
+    for which in range(2):
+        own_slice(which, 1).wait()
+        for m in near:
+            slice_copy(m, which).wait_send()
+            slice_plane(m, which, rep, 0, xrep).wait_send()
+            slice_plane(m, which, rep, 1, yrep).wait_send()
+            if which == 0:
+                slice_plane(m, which, xrep, 2, yrep).wait_send()
+            else:
+                slice_plane(m, which, yrep, 2, xrep).wait_send()
+            slice_plane(m, which, drep, 2, drep).wait_recv()
+    for way in range(2):
+        for h in range(3):
+            z = zpos - h if way == 0 else zpos + h
+
+            @pl.when((z >= 0) & (zpos < 3) if way == 0 else (z <= 3) & (zpos > 0))
+            def _():
+                for a in range(6):
+                    hop(a, way, h, z, "wait_send")
+    for h in range(1, 4):
+        for way in range(2):
+            z = zpos - h if way == 0 else zpos + h
+            k = way * 3 + h - 1
+
+            @pl.when(z >= 0 if way == 0 else z <= 3)
+            def _():
+                for a in range(4):
+                    to_plane(a, k, z, rep, "wait_send", (xsend, xrecv), xrep)
+                    to_plane(a, k, z, rep, "wait_send", (ysend, yrecv), yrep)
+                    to_plane(a, k, z, xrep if a == 0 else yrep, "wait_send", (dsend, drecv), yrep)
+                for a in range(7):
+                    to_core(a, k + 1, z, core, "wait_send")
+                    to_core(a, k + 1, z, 1 - core, "wait_recv")
+
+def start_gather(cid, weights, gate, up, strip):
+    out = [jax.ShapeDtypeStruct((a.shape[0] * 8,) + a.shape[1:], a.dtype) for a in weights]
+    out += [jax.ShapeDtypeStruct((gate.shape[0] * 8, strip), gate.dtype)] * 2
+    return pl.pallas_call(
+        start_kernel, out_shape=out, in_specs=[ANY] * 9, out_specs=[ANY] * 9,
+        scratch_shapes=[dma_sems(2, 3, 6), dma_sems(2, 3, 6)] + [dma_sems(6, 4)] * 6
+        + [dma_sems(7, 7), dma_sems(7, 7), dma_sems(2, 9), dma_sems(7, 2), dma_sems(7, 2), dma_sems(3, 7, 2), dma_sems(3, 7, 2)]
+        + [pltpu.VMEM(a.shape, a.dtype) for a in weights] + [pltpu.VMEM((gate.shape[0], strip), gate.dtype)] * 2,
+        compiler_params=kernel_params(cid),
+    )(*weights, gate, up)
+
+def plane_swap(values, j):
+    return lax.ppermute(values, "rep", [(i, i ^ j) for i in range(4)])
+
+
+def column_body(
+    tokens,
+    cotangent,
+    doc_lengths,
+    gain_attn,
+    query_down,
+    gain_query,
+    query_up,
+    latent_down,
+    gain_latent,
+    latent_up,
+    attn_out,
+    gain_ffn,
+    w_gate,
+    w_up,
+    w_down,
+):
+    low = jnp.bfloat16
+    wide = jnp.float32
+    rows, width = tokens.shape[1], tokens.shape[2]
+    seq_len = rows * 4
+    head_dim = ND + RD
+    group = 8
+    groups = H // group
+    scale = head_dim ** (-0.5)
+    rep, shard = lax.axis_index("rep"), lax.axis_index("shard")
+    slice_ff = FF // 8
+    strip = 896
+    shift = (slice_ff * shard) % 128
+
+    small = jnp.concatenate(
+        [v.astype(wide) for v in (gain_attn, gain_ffn, gain_query, gain_latent)]
+        + [jnp.zeros((1024 - 768,), wide)]
+    ).reshape(8, 128)
+    grad_out = cotangent[0].astype(wide)
+    grad_down_in = (residual_scale * grad_out).astype(low)
+    aout, qdown, ldown, qup, lup, gd_all, small_all, gate_w, up_w = start_gather(
+        0, (attn_out, query_down, latent_down, query_up, latent_up, grad_down_in, small), w_gate, w_up, strip
+    )
+    small_all = small_all.reshape(8, 1024)
+    gain_in = small_all[:, :320].reshape(-1)
+    gain_f = small_all[:, 320:640].reshape(-1)
+    gain_q = small_all[:, 640:736].reshape(-1)
+    gain_l = small_all[:, 736:768].reshape(-1)
+
+    down_w = lax.dynamic_update_slice(jnp.zeros((strip, width), low), w_down, (shift, 0))
+
+    local_pos = rep * rows + jnp.arange(rows, dtype=jnp.int32)
+    key_pos = jnp.concatenate(
+        [(rep ^ j) * rows + jnp.arange(rows, dtype=jnp.int32) for j in range(4)]
+    )
+    query_seg, query_off = segment_of(doc_lengths[0], local_pos)
+    key_seg = segment_of(doc_lengths[0], key_pos)[0]
+    allowed = (query_seg[:, None] == key_seg[None, :]) & (key_pos[None, :] <= local_pos[:, None])
+    cos_part, sin_part = rope_tables(query_off, RD)
+    inputs = tokens[0].astype(wide)
+    normed, norm_in_back = jax.vjp(rms_scale, inputs, gain_in)
+    normed_low = normed.astype(low)
+    latent_proj = jnp.dot(normed_low, ldown, preferred_element_type=wide)
+    latent_norm, norm_l_back = jax.vjp(rms_scale, latent_proj[:, :KR], gain_l)
+
+    def key_rotate(values):
+        return rotate(values, cos_part, sin_part)
+
+    key_rot, key_back = jax.vjp(key_rotate, latent_proj[:, KR:])
+    latents = jnp.concatenate([latent_norm.astype(low), key_rot.astype(low)], axis=1)
+    latents = jnp.concatenate([latents] + [plane_swap(latents, j) for j in range(1, 4)], axis=0)
+    latent_low, all_rope = latents[:, :KR], latents[:, KR:]
+    query_lat = jnp.dot(normed_low, qdown, preferred_element_type=wide)
+    query_norm, norm_q_back = jax.vjp(rms_scale, query_lat, gain_q)
+    query_low = query_norm.astype(low)
+    query_proj = jnp.dot(query_low, qup, preferred_element_type=wide).reshape(rows, H, head_dim)
+
+    def query_rope(values):
+        return jnp.concatenate(
+            [
+                values[..., :ND],
+                rotate(values[..., ND:], cos_part[:, None, :], sin_part[:, None, :]),
+            ],
+            axis=-1,
+        )
+
+    query_rot, query_back = jax.vjp(query_rope, query_proj)
+    query_used = query_rot.astype(low)
+    keyvals = jnp.dot(latent_low, lup, preferred_element_type=wide).astype(low)
+    queries = query_used.reshape(rows, groups, group, head_dim).transpose(1, 0, 2, 3)
+    key_groups = keyvals.reshape(seq_len, groups, group, ND + VD).transpose(1, 0, 2, 3)
+
+    def scores_of(query_blk, key_blk):
+        nope_part = jnp.einsum(
+            "thd,shd->hts", query_blk[..., :ND], key_blk[..., :ND], preferred_element_type=wide
+        )
+        rope_part = jnp.einsum(
+            "thd,sd->hts", query_blk[..., ND:], all_rope, preferred_element_type=wide
+        )
+        return jnp.where(allowed[None], (nope_part + rope_part) * scale, masked_score)
+
+    def forward_group(carry, blocks):
+        query_blk, key_blk = blocks
+        scores = scores_of(query_blk, key_blk)
+        row_max = jnp.max(scores, axis=-1, keepdims=True)
+        exp_scores = jnp.exp(scores - row_max)
+        totals = jnp.sum(exp_scores, axis=-1, keepdims=True)
+        probs = (exp_scores / totals).astype(low)
+        mixed = jnp.einsum("hts,shd->thd", probs, key_blk[..., ND:], preferred_element_type=wide)
+        return (carry, (mixed, row_max + jnp.log(totals)))
+
+    _, (mixed_groups, log_totals) = lax.scan(
+        forward_group, jnp.zeros((), wide), (queries, key_groups)
+    )
+    mixed_low = mixed_groups.transpose(1, 0, 2, 3).reshape(rows, H * VD).astype(low)
+    branch = jnp.dot(mixed_low, aout, preferred_element_type=wide)
+    residual = inputs + residual_scale * branch
+    normed_ffn, norm_f_back = jax.vjp(rms_scale, residual, gain_f)
+    ffn_low = normed_ffn.astype(low)
+
+    (ffn_all,) = chain_gather(1, ffn_low)
+    gate_pre = jnp.dot(ffn_all, gate_w, preferred_element_type=wide)
+    up_pre = jnp.dot(ffn_all, up_w, preferred_element_type=wide)
+    hidden, act_back = jax.vjp(swiglu, gate_pre, up_pre)
+    hidden_low = hidden.astype(low)
+    grad_hidden = outer_cols(gd_all, down_w)
+    grad_gate_f, grad_up_f = act_back(grad_hidden)
+    grad_gate = grad_gate_f.astype(low)
+    grad_up = grad_up_f.astype(low)
+    ffn_in_part = (outer_cols(grad_gate, gate_w) + outer_cols(grad_up, up_w)).astype(low)
+    grad_ffn_in = chain_sum(2, ffn_in_part.reshape(8, rows, width))
+    out_part = jnp.dot(hidden_low, down_w, preferred_element_type=wide).astype(low)
+    down_part = lax.dynamic_slice(
+        inner_rows(hidden_low, gd_all).astype(low), (shift, 0), (slice_ff, width)
+    )
+    gate_part = inner_rows(ffn_all, grad_gate).astype(low)
+    up_part = inner_rows(ffn_all, grad_up).astype(low)
+    down_own = lax.psum_scatter(
+        down_part.reshape(4, slice_ff // 4, width), "rep", scatter_dimension=0, tiled=False
+    )
+    parts_own = lax.psum_scatter(
+        jnp.stack([gate_part.reshape(8, 4, 80, strip), up_part.reshape(8, 4, 80, strip)])
+        .transpose(2, 1, 0, 3, 4),
+        "rep",
+        scatter_dimension=0,
+        tiled=False,
+    )
+
+    grad_res_norm, grad_gain_ffn = norm_f_back(grad_ffn_in)
+    grad_resid = grad_out + grad_res_norm
+    grad_branch = (residual_scale * grad_resid).astype(low)
+    grad_mixed = outer_cols(grad_branch, aout).astype(low)
+    grad_groups = grad_mixed.reshape(rows, groups, group, VD).transpose(1, 0, 2, 3)
+
+    def backward_group(rope_acc, blocks):
+        query_blk, key_blk, grad_blk, log_blk = blocks
+        scores = scores_of(query_blk, key_blk)
+        probs = jnp.exp(scores - log_blk)
+        grad_probs = jnp.einsum(
+            "thd,shd->hts", grad_blk, key_blk[..., ND:], preferred_element_type=wide
+        )
+        delta = jnp.sum(probs * grad_probs, axis=-1, keepdims=True)
+        grad_scores = (probs * (grad_probs - delta)).astype(low)
+        grad_query = (
+            jnp.concatenate(
+                [
+                    jnp.einsum(
+                        "hts,shd->thd",
+                        grad_scores,
+                        key_blk[..., :ND],
+                        preferred_element_type=wide,
+                    ),
+                    jnp.einsum(
+                        "hts,sd->thd", grad_scores, all_rope, preferred_element_type=wide
+                    ),
+                ],
+                axis=-1,
+            )
+            * scale
+        )
+        grad_key = (
+            jnp.einsum(
+                "hts,thd->shd", grad_scores, query_blk[..., :ND], preferred_element_type=wide
+            )
+            * scale
+        )
+        grad_value = jnp.einsum(
+            "hts,thd->shd", probs.astype(low), grad_blk, preferred_element_type=wide
+        )
+        rope_acc = (
+            rope_acc
+            + jnp.einsum(
+                "hts,thd->sd", grad_scores, query_blk[..., ND:], preferred_element_type=wide
+            )
+            * scale
+        )
+        return (rope_acc, (grad_query, jnp.concatenate([grad_key, grad_value], axis=-1)))
+
+    rope_sum, (grad_q_groups, grad_kv_groups) = lax.scan(
+        backward_group,
+        jnp.zeros((seq_len, RD), wide),
+        (queries, key_groups, grad_groups, log_totals),
+    )
+    grad_kv = grad_kv_groups.transpose(1, 0, 2, 3).reshape(seq_len, H * (ND + VD)).astype(low)
+    grad_lat_part = jnp.concatenate([outer_cols(grad_kv, lup), rope_sum], axis=1).astype(low)
+    grad_lat_own = grad_lat_part[:rows].astype(wide)
+    for j in range(1, 4):
+        grad_lat_own = grad_lat_own + plane_swap(
+            grad_lat_part[j * rows : (j + 1) * rows], j
+        ).astype(wide)
+    grad_q_full = grad_q_groups.transpose(1, 0, 2, 3).reshape(rows, H, head_dim)
+    grad_q_proj = query_back(grad_q_full)[0].reshape(rows, H * head_dim).astype(low)
+    grad_q_lat_f, grad_gain_query = norm_q_back(outer_cols(grad_q_proj, qup))
+    grad_q_lat = grad_q_lat_f.astype(low)
+    grad_lat_c, grad_gain_latent = norm_l_back(grad_lat_own[:, :KR])
+    grad_lat_r = key_back(grad_lat_own[:, KR:])[0]
+    grad_lat = jnp.concatenate([grad_lat_c, grad_lat_r], axis=1).astype(low)
+    grad_normed = outer_cols(grad_q_lat, qdown) + outer_cols(grad_lat, ldown)
+    grad_in_norm, grad_gain_attn = norm_in_back(grad_normed)
+    tokens_grad = (grad_resid + grad_in_norm).astype(low)
+
+    qup_grad = inner_rows(query_low, grad_q_proj).astype(low)
+    lup_grad = inner_rows(latent_low, grad_kv).astype(low)
+
+    def scattered(grad):
+        grad = grad.reshape(8, 4, grad.shape[0] // 32, grad.shape[1])
+        part = lax.psum_scatter(grad, "rep", scatter_dimension=1, tiled=False)
+        part = lax.psum_scatter(part, "shard", scatter_dimension=0, tiled=False)
+        return lax.all_gather(part, "rep", axis=0, tiled=True).astype(wide)
+
+    qup_own, lup_own = scattered(qup_grad), scattered(lup_grad)
+    grad_lats = jnp.concatenate([grad_q_lat, grad_lat], axis=1)
+    cols = jnp.stack([mixed_low, normed_low]).reshape(2, rows, 8, width // 8).transpose(2, 0, 1, 3)
+    branch_all, lat_all, cols_all, out_sum, parts_all, down_all = late_exchange(
+        3, grad_branch, grad_lats, cols, out_part.reshape(8, rows, width), parts_own, down_own
+    )
+    layer_out = (residual + residual_scale * out_sum).astype(low)
+    down_grad = down_all.reshape(slice_ff, width).astype(wide)
+
+    def slices(which):
+        return jnp.concatenate(
+            [
+                parts_all[s, :, which, :, (slice_ff * s) % 128 : (slice_ff * s) % 128 + slice_ff]
+                for s in range(8)
+            ],
+            axis=-1,
+        ).reshape(-1, FF).astype(wide)
+
+    gate_grad, up_grad = slices(0), slices(1)
+    mixed_cols = cols_all[:, 0].reshape(8 * rows, width // 8)
+    normed_cols = cols_all[:, 1].reshape(8 * rows, width // 8)
+    aout_part = inner_rows(mixed_cols, branch_all).astype(low)
+    lat_part = inner_rows(normed_cols, lat_all).astype(low)
+    gains = jnp.concatenate(
+        [
+            v.reshape(8, -1)
+            for v in (grad_gain_attn, grad_gain_ffn, grad_gain_query, grad_gain_latent)
+        ]
+        + [jnp.zeros((8, 1024 - 768), wide)],
+        axis=1,
+    ).reshape(8, 8, 128)
+    aout_own, lat_own, gain_own = last_sums(
+        4, (aout_part.reshape(4, 80, width), lat_part.reshape(4, 80, -1)), gains
+    )
+    aout_own = aout_own.reshape(320, width).astype(wide)
+    lat_own = lat_own.reshape(320, -1).astype(wide)
+    gain_own = gain_own.reshape(1024)
+
+    return (
+        layer_out[None],
+        tokens_grad[None],
+        gain_own[:320],
+        lat_own[:, : query_down.shape[1]],
+        gain_own[640:736],
+        qup_own,
+        lat_own[:, query_down.shape[1] :],
+        gain_own[736:768],
+        lup_own,
+        aout_own,
+        gain_own[320:640],
+        gate_grad,
+        up_grad,
+        down_grad,
     )
 
 
@@ -400,8 +1408,9 @@
         P("shard", None),
         P("shard", None),
     )
+    fits = mesh.shape["rep"] == 4 and mesh.shape["shard"] == 8
     return jax.shard_map(
-        body,
+        column_body if fits else body,
         mesh=mesh,
         in_specs=placed,
         out_specs=(

time: 3030 us -> 1110 us (0.37)
  waiting for transfers between devices: 2580 us -> 209 us
  Pallas kernels: 0 us -> 503 us
  matrix products: 238 us -> 179 us
  blocking collectives: 74.5 us -> 22.2 us
    reduce_scatter x6 -> x2, waiting for transfers between devices: 1190 us -> 0.01 us  [scattered(): part = lax.psum_scatter(part, 'shard', scatter_dimension=0, tiled=False)]
    all_gather x9 -> x0, waiting for transfers between devices: 1070 us -> none  [the longest x1 275 us: body(): lax.all_gather(w_gate, 'shard', axis=0, tiled=True)]
    pallas_call x0 -> x5, Pallas kernels: none -> 503 us  [the longest x1 176 us: start_gather(): pl.pallas_call(start_kernel, out_shape=out, in_specs=[ANY] * 9, out_specs...]
    psum x1 -> x0, waiting for transfers between devices: 239 us -> none  [body(): lax.psum(owned_qdown.astype(jnp.bfloat16), 'rep').astype(jnp.float32)]
    unnamed x22 -> x10, waiting for transfers between devices: 83.7 us -> 209 us
    unnamed x2 -> x0, blocking collectives: 56.4 us -> none
  transfers between devices with their start and end apart: 19 -> 12, of which waited for: 17 -> 4; matrix products, arithmetic and copies ran while one was open for 7% -> 10% of each run, Pallas kernels for 0% -> 0%
where the time goes in v1:
time: 1110 us; the launch traced here: 1100 us
  Pallas kernels  503 us (45%)
  waiting for transfers between devices  209 us (19%)
  matrix products  179 us (16%)
  local copies, waits for them, and re-layouts  88.9 us (8%)
  other arithmetic  72.9 us (7%)
  blocking collectives  22.2 us (2%)
  between operations  15.7 us (1%)
    unnamed x10, waiting for transfers between devices  209 us
    pallas_call x1, Pallas kernels, start_gather(): pl.pallas_call(start_kernel, out_shape=out, in_specs=[ANY] * 9, out_specs...  176 us
    pallas_call x1, Pallas kernels, late_exchange(): pl.pallas_call(late_kernel, out_shape=out, in_specs=[ANY] * 6, out_specs=...  162 us
    pallas_call x1, Pallas kernels, last_sums(): pl.pallas_call(functools.partial(last_kernel, n), out_shape=out, in_specs...  59.4 us
    pallas_call x1, Pallas kernels, chain_sum(): pl.pallas_call(chain_sum_kernel, out_shape=jax.ShapeDtypeStruct(term.shap...  55.6 us
    dot_general x8, matrix products, outer_cols(): lax.dot_general(leading, trailing, (((1,), (1,)), ((), ())), preferred_el...  50 us
    pallas_call x1, Pallas kernels, chain_gather(): pl.pallas_call(functools.partial(chain_gather_kernel, n), out_shape=out,...  49.2 us
    dot_general x7, matrix products, inner_rows(): lax.dot_general(leading, trailing, (((0,), (0,)), ((), ())), preferred_el...  40.8 us
  transfers between devices with their start and end apart: 12, of which 4 were waited for; matrix products, arithmetic and copies ran while one was open for 10% of the time, Pallas kernels for 0%

profile of v1, /device:TPU:0, one launch (start us, length us, event | category | flops | bytes accessed | tf_op | source)
XLA Modules:
  0.0 1100.0 jit_solution(2736154632272790035)
XLA Ops:
  14.4 176.5 %shard_map.254 = (bf16[2560,2560]{1,0:T(8,128)(2,1)}, bf16[2560,768]{1,0:T(8,128)(2,1)}, bf16[2560,288]{1,0:T(8,128)(2,1)}, bf16[768,3840]{1,0:T(8,128)(2,1)}, b...) custom-call(bf16[320,2560]{1,0:T(8,128)(2,1)} %refs_0_.1, ...), custom_call_target="tpu_custom_call" | custom-call | tf_op jit(solution)/shard_map/pallas_call | solution.py:780
  214.2 10.6 fusion.103
  232.7 8.0 copy.133
  240.7 23.4 %while.28 = (s32[]{:T(128)}, bf16[5,128,8,64]{1,3,2,0:T(8,128)(2,1)S(1)}, f32[5,8,128,1]{2,1,3,0:T(8,128)}, bf16[5,512,8,128]{1,3,2,0:T(8,128)(2,1)}, bf16[5,128...) while((s32[]{:T(128)}, ...), condition=%wide.region_10.11_spmd.clone, body=%wide.region_7.10_spmd.clone.sunk | while | flops 172686336 | bytes 14685817 | solution.py:899
  264.2 7.0 multiply_reduce_fusion.3
  272.4 49.2 %shard_map.255 = bf16[1024,2560]{1,0:T(8,128)(2,1)} custom-call(bf16[128,2560]{1,0:T(8,128)(2,1)} %multiply_convert_fusion.4.refs_0_), custom_call_target="tpu_custom_call" | custom-call | tf_op jit(solution)/shard_map/pallas_call | solution.py:309
  321.7 9.5 fusion.104
  331.2 8.7 multiply_convert_fusion.1
  339.9 7.1 fusion.105
  347.0 8.9 add_convert_fusion
  355.9 55.6 %shard_map.256 = f32[128,2560]{1,0:T(8,128)} custom-call(bf16[8,128,2560]{2,1,0:T(8,128)(2,1)} %bitcast.308), custom_call_target="tpu_custom_call" | custom-call | tf_op jit(solution)/shard_map/pallas_call | solution.py:326
  414.7 9.2 convolution_convert_fusion.7
  425.0 49.7 %while.29 = (s32[]{:T(128)}, f32[512,32]{0,1:T(8,128)S(1)}, f32[5,128,8,96]{1,3,2,0:T(8,128)}, bf16[5,512,8,128]{1,3,2,0:T(8,128)(2,1)}, bf16[5,128,8,96]{1,3,2,...) while((s32[]{:T(128)}, f32[512,32]{0,1:T(8,128)S(1)}, ...), condition=%wide.region_15.16_spmd.clone, body=%wide.region_13.15_spmd.clone.sunk | while | flops 444513280 | bytes 31419552 | solution.py:986
  489.3 28.7 %reduce-scatter.25.cloned.1.call-done = bf16[8,1,8,5120]{3,2,0,1:T(8,128)(2,1)} async-done(((bf16[8,4,8,5120]{3,2,0,1:T(8,128)(2,1)}), bf16[8,1,8,5120]{3,2,0,1:T(8,128)(2,1)}) %reduce-scatter.25.cloned.1.call-update) | async-done | bytes 655376
  518.1 70.5 %reduce-scatter.23.cloned.1.call-done = bf16[8,1,24,3840]{3,2,0,1:T(8,128)(2,1)} async-done(((bf16[8,4,24,3840]{3,2,0,1:T(8,128)(2,1)}), bf16[8,1,24,3840]{3,2,0,1:T(8,128)(2,1)}) %reduce-scatter.23.cloned.1.call-update) | async-done | bytes 1474576
  589.0 8.0 fusion.106
  599.4 9.7 convolution_convert_fusion.5
  609.0 9.8 convolution_convert_fusion.4
  618.8 8.2 maximum_bitcast_fusion.1
  627.0 8.2 copy.126
  655.3 9.8 convolution_convert_fusion.3
  675.0 11.7 %all-gather.1 = bf16[1,32,5120]{2,1,0:T(8,128)(2,1)S(1)} all-gather(bf16[1,8,5120]{2,1,0:T(8,128)(2,1)} %reduce-scatter.17.cloned.1.call-done), channel_id=3, replica_groups=mesh['rep'=4,'shard'=8] {'rep'}, dimensions={1}, use_global_device_ids=true | all-gather | bytes 409600 | tf_op jit(solution)/shard_map/all_gather | solution.py:1016
  687.5 10.6 all-gather
  699.3 13.6 %reduce-scatter.21.cloned.1.call-done = bf16[1,200,2560]{2,1,0:T(8,128)(2,1)} async-done(((bf16[4,200,2560]{2,1,0:T(8,128)(2,1)}), bf16[1,200,2560]{2,1,0:T(8,128)(2,1)}) %reduce-scatter.21.cloned.1.call-update) | async-done | bytes 1024016
  712.9 95.9 %reduce-scatter.19.cloned.1.call-done = bf16[1,8,2,80,896]{4,3,2,1,0:T(8,128)(2,1)} async-done(((bf16[4,8,2,80,896]{4,3,2,1,0:T(8,128)(2,1)}), bf16[1,8,2,80,896]{4,3,2,1,0:T(8,128)(2,1)}) %reduce-scatter.19.cloned.1.call-update) | async-done | bytes 2293776
  808.8 162.1 %shard_map.257 = (bf16[1024,2560]{1,0:T(8,128)(2,1)}, bf16[1024,1056]{1,0:T(8,128)(2,1)}, bf16[8,2,128,320]{3,2,1,0:T(8,128)(2,1)}, f32[128,2560]{1,0:T(8,128)},...) custom-call(bf16[128,2560]{1,0:T(8,128)(2,1)} %copy-done.9, ...), custom_call_target="tpu_custom_call" | custom-call | tf_op jit(solution)/shard_map/pallas_call | solution.py:452
  980.5 59.4 %shard_map.258 = (bf16[4,80,2560]{2,1,0:T(8,128)(2,1)}, bf16[4,80,1056]{2,1,0:T(8,128)(2,1)}, f32[8,128]{1,0:T(8,128)}) custom-call(bf16[4,80,2560]{2,1,0:T(8,128)(2,1)} %bitcast.336, bf16[4,80,1056]{2,1,0:T(8,128)(2,1)} %bitcast.315, f32[8,8,128]{2,1,0:T(8,128)} %bitcast.343), custom_call_target="tpu_custom_call" | custom-call | tf_op jit(solution)/shard_map/pallas_call | solution.py:524
  1043.9 7.9 fusion.99
  1051.9 8.3 concatenate.128
  1066.3 8.1 concatenate.119
  1074.4 6.1 convert_element_type.259
  1083.8 6.8 bitcast_convert_fusion
  (417 shorter events, 190.1 us)
Async XLA Ops:
  7.2 510.8 %reduce-scatter.25.cloned.1.call-start = ((), (), s32[]{:S(2)}) async-start(), calls=%async_computation.11 | async-start | bytes 3276800
  14.4 177.5 %copy-start.2 = (bf16[1,128,2560]{2,1,0:T(8,128)(2,1)S(1)}, bf16[1,128,2560]{2,1,0:T(8,128)(2,1)}, u32[]{:S(2)}) copy-start(bf16[1,128,2560]{2,1,0:T(8,128)(2,1)} %param.19) | copy-start | bytes 1966084
  191.7 10.3 copy-start.40
  192.0 10.1 copy-start.36
  192.2 12.8 %copy-start.52 = (f32[128]{0:T(128)}, f32[128]{0:T(128)S(1)}, u32[]{:S(2)}) copy-start(f32[128]{0:T(128)S(1)} %fusion.92) | copy-start | bytes 1540
  197.2 27.8 %collective-permute-start = (bf16[128,288]{1,0:T(8,128)(2,1)}, bf16[128,288]{1,0:T(8,128)(2,1)S(1)}, u32[]{:S(2)}, u32[]{:S(2)}) collective-permute-start(bf16[128,288]{1,0:T(8,128)(2,1)} %pad_maximum_fusion.4), channel_id=1, source_target_pairs={{0,8},{8,0},{16,24},{24,16},{1,9},{9,1},{17,25},{25,17},{2,10},{10... | collective-permute-start | bytes 221192 | tf_op jit(solution)/shard_map/ppermute | solution.py:789
  199.8 25.2 %collective-permute-start.1 = (bf16[128,288]{1,0:T(8,128)(2,1)}, bf16[128,288]{1,0:T(8,128)(2,1)}, u32[]{:S(2)}, u32[]{:S(2)}) collective-permute-start(bf16[128,288]{1,0:T(8,128)(2,1)} %pad_maximum_fusion.4), channel_id=1, source_target_pairs={{0,16},{8,24},{16,0},{24,8},{1,17},{9,25},{17,1},{25,9},{2,18},{10... | collective-permute-start | bytes 221192 | tf_op jit(solution)/shard_map/ppermute | solution.py:789
  200.5 24.5 %collective-permute-start.2 = (bf16[128,288]{1,0:T(8,128)(2,1)}, bf16[128,288]{1,0:T(8,128)(2,1)}, u32[]{:S(2)}, u32[]{:S(2)}) collective-permute-start(bf16[128,288]{1,0:T(8,128)(2,1)} %pad_maximum_fusion.4), channel_id=1, source_target_pairs={{0,24},{8,16},{16,8},{24,0},{1,25},{9,17},{17,9},{25,1},{2,26},{10... | collective-permute-start | bytes 221192 | tf_op jit(solution)/shard_map/ppermute | solution.py:789
  211.4 202.6 %copy-start.34 = (f32[2560]{0:T(1024)}, f32[2560]{0:T(1024)S(1)}, u32[]{:S(2)}) copy-start(f32[2560]{0:T(1024)S(1)} %mul.453) | copy-start | bytes 30724
  214.2 10.6 copy-start.14
  214.2 10.6 copy-start.20
  271.2 142.8 %copy-start = (f32[128,2560]{1,0:T(8,128)}, f32[128,2560]{1,0:T(8,128)S(1)}, u32[]{:S(2)}) copy-start(f32[128,2560]{1,0:T(8,128)S(1)} %get-tuple-element.439) | copy-start | bytes 3932164
  271.2 142.8 %copy-start.55 = (f32[128]{0:T(128)}, f32[128]{0:T(128)S(1)}, u32[]{:S(2)}) copy-start(f32[128]{0:T(128)S(1)} %fusion.95) | copy-start | bytes 1540
  272.4 58.8 %slice-start.2 = ((s8[4587520]{0:T(1024)(128)(4,1)}), s8[4194304]{0:T(1024)(128)(4,1)S(1)}, s32[]{:S(2)}) async-start(s8[4587520]{0:T(1024)(128)(4,1)} %bitcast.351), calls=%async_computation.14 | async-start | bytes 8388608
  321.6 9.5 copy-start.13
  321.7 9.5 slice-start.3
  321.7 9.5 copy-start.76
  321.7 18.2 %slice-start.4 = ((s8[4587520]{0:T(1024)(128)(4,1)}), s8[4194304]{0:T(1024)(128)(4,1)S(1)}, s32[]{:S(2)}) async-start(s8[4587520]{0:T(1024)(128)(4,1)} %bitcast.353), calls=%async_computation.16 | async-start | bytes 8388608
  414.1 9.8 copy-start.65
  414.7 9.2 copy-start.9
  480.5 108.1 %reduce-scatter.23.cloned.1.call-start = ((), (), s32[]{:S(2)}) async-start(), calls=%async_computation.10 | async-start | bytes 7372800
  489.2 185.8 %reduce-scatter.17.cloned.1.call-start = ((), (), s32[]{:S(2)}) async-start(), calls=%async_computation.7 | async-start | bytes 737280 | tf_op jit(solution)/shard_map/reduce_scatter | solution.py:1015
  518.0 169.5 %reduce-scatter.15.cloned.1.call-start = ((), (), s32[]{:S(2)}) async-start(), calls=%async_computation.6 | async-start | bytes 1658880 | tf_op jit(solution)/shard_map/reduce_scatter | solution.py:1015
  588.5 124.3 %reduce-scatter.21.cloned.1.call-start = ((), (), s32[]{:S(2)}) async-start(), calls=%async_computation.9 | async-start | bytes 5120000
  599.3 209.5 %reduce-scatter.19.cloned.1.call-start = ((), (), s32[]{:S(2)}) async-start(), calls=%async_computation.8 | async-start | bytes 11468800
  599.3 9.7 copy-start.77
  638.0 9.3 copy-start.18
  643.8 23.5 %collective-permute-start.3 = (bf16[128,288]{1,0:T(8,128)(2,1)}, bf16[128,288]{1,0:T(8,128)(2,1)}, u32[]{:S(2)}, u32[]{:S(2)}) collective-permute-start(bf16[128,288]{1,0:T(8,128)(2,1)} %get-tuple-element.421), channel_id=1, source_target_pairs={{0,8},{8,0},{16,24},{24,16},{1,9},{9,1},{17,25},{25,17},{2,10},{10... | collective-permute-start | bytes 221192 | tf_op jit(solution)/shard_map/ppermute | solution.py:789
  645.1 22.2 %collective-permute-start.4 = (bf16[128,288]{1,0:T(8,128)(2,1)}, bf16[128,288]{1,0:T(8,128)(2,1)}, u32[]{:S(2)}, u32[]{:S(2)}) collective-permute-start(bf16[128,288]{1,0:T(8,128)(2,1)} %get-tuple-element.423), channel_id=1, source_target_pairs={{0,16},{8,24},{16,0},{24,8},{1,17},{9,25},{17,1},{25,9},{2,18},{10... | collective-permute-start | bytes 221192 | tf_op jit(solution)/shard_map/ppermute | solution.py:789
  645.8 21.5 %collective-permute-start.5 = (bf16[128,288]{1,0:T(8,128)(2,1)}, bf16[128,288]{1,0:T(8,128)(2,1)}, u32[]{:S(2)}, u32[]{:S(2)}) collective-permute-start(bf16[128,288]{1,0:T(8,128)(2,1)} %get-tuple-element.422), channel_id=1, source_target_pairs={{0,24},{8,16},{16,8},{24,0},{1,25},{9,17},{17,9},{25,1},{2,26},{10... | collective-permute-start | bytes 221192 | tf_op jit(solution)/shard_map/ppermute | solution.py:789
  655.3 9.8 copy-start.19
  1041.1 10.8 copy-start.12
  (64 other events, 253.4 us)
Sparse Core Ops, SparseCore 0:
  480.6 37.3 reduce-scatter.24
  521.6 66.8 reduce-scatter.22
  590.8 31.2 reduce-scatter.16
  624.3 31.9 reduce-scatter.14
  659.2 53.5 reduce-scatter.20
  715.9 92.8 reduce-scatter.18

commit v2 on v1

--- a/solution.py
+++ b/solution.py
@@ -125,6 +125,139 @@
 
 def dma_sems(*dims):
     return pltpu.SemaphoreType.DMA(dims)
+
+
+def head_tile(h):
+    return pl.ds(pl.multiple_of(h * 128, 128), 128)
+
+
+def turn(values, tables, back=False):
+    keep, high, low_part = tables
+    if back:
+        return values * keep + pltpu.roll(values * high, 112, 1) + pltpu.roll(values * low_part, 16, 1)
+    return values * keep + pltpu.roll(values, 16, 1) * high + pltpu.roll(values, 112, 1) * low_part
+
+
+def dot_nt(a, b):
+    return lax.dot_general(a, b, (((1,), (1,)), ((), ())), preferred_element_type=jnp.float32)
+
+
+def dot_tn(a, b):
+    return lax.dot_general(a, b, (((0,), (0,)), ((), ())), preferred_element_type=jnp.float32)
+
+
+def attend_kernel(scale, proj, kv, rope, bias, turns, query, mixed, logs):
+    low = jnp.bfloat16
+    heads = kv.shape[1] // 128
+    lane = lax.broadcasted_iota(jnp.int32, (1, 128), 1)
+    first = lane < 64
+    logs[...] = jnp.zeros_like(logs)
+
+    def one(h):
+        q = turn(proj[:, head_tile(h)], (turns[0], turns[1], turns[2])).astype(low)
+        query[:, head_tile(h)] = q
+        keyval = kv[:, head_tile(h)]
+        key = jnp.where(first, keyval, rope[...])
+        scores = dot_nt(q, key) * scale + bias[...]
+        top = jnp.max(scores, axis=1, keepdims=True)
+        grown = jnp.exp(scores - top)
+        total = jnp.sum(grown, axis=1, keepdims=True)
+        probs = (grown / total).astype(low)
+        logs[...] = jnp.where(lane == h, top + jnp.log(total), logs[...])
+        return jnp.dot(probs, keyval, preferred_element_type=jnp.float32)
+
+    def pair(i, carry):
+        even, odd = one(2 * i), one(2 * i + 1)
+        mixed[:, head_tile(i)] = jnp.where(first, pltpu.roll(even, 64, 1), odd).astype(low)
+        return carry
+
+    lax.fori_loop(0, heads // 2, pair, 0)
+
+
+def attend(scale, proj, kv, rope, bias, turns):
+    rows, cols = proj.shape
+    return pl.pallas_call(
+        functools.partial(attend_kernel, scale),
+        out_shape=[jax.ShapeDtypeStruct((rows, cols), jnp.bfloat16), jax.ShapeDtypeStruct((rows, cols // 2), jnp.bfloat16),
+                   jax.ShapeDtypeStruct((rows, 128), jnp.float32)],
+        in_specs=[VMEM] * 5, out_specs=[VMEM] * 3,
+        compiler_params=pltpu.CompilerParams(vmem_limit_bytes=56 * 2**20),
+    )(proj, kv, rope, bias, turns)
+
+
+def attend_back_heads(scale, query, kv, rope, bias, turns, logs, grad, grad_query, grad_packed, grad_kv, grad_rope, left):
+    low = jnp.bfloat16
+    rows = query.shape[0]
+    lane = lax.broadcasted_iota(jnp.int32, (1, 128), 1)
+    first = lane < 64
+
+    def one(h, grad_value):
+        q = query[:, head_tile(h)]
+        keyval = kv[:, head_tile(h)]
+        key = jnp.where(first, keyval, rope[...])
+        left[0:rows, 0:128] = q
+        left[rows:, 128:256] = grad_value
+        both = dot_nt(left[...], jnp.concatenate([key, keyval], axis=1))
+        log = jnp.sum(jnp.where(lane == h, logs[...], 0.0), axis=1, keepdims=True)
+        probs = jnp.exp(both[:rows] * scale + bias[...] - log)
+        weighed = probs * both[rows:]
+        delta = jnp.sum(weighed, axis=1, keepdims=True)
+        grad_scores = (weighed - probs * delta).astype(low)
+        grad_q = jnp.dot(grad_scores, key, preferred_element_type=jnp.float32) * scale
+        grad_q = turn(grad_q, (turns[0], turns[1], turns[2]), True)
+        grad_query[:, head_tile(h)] = grad_q.astype(low)
+        out = dot_tn(jnp.concatenate([grad_scores, probs.astype(low)], axis=0), left[...])
+        grad_key = out[:, :128] * scale
+        grad_rope[...] += grad_key
+        grad_kv[:, head_tile(h)] = jnp.where(first, grad_key, out[:, 128:]).astype(low)
+        return grad_q
+
+    def quarter(i, carry):
+        rotary = jnp.zeros((rows, 128), jnp.float32)
+        for j in range(5):
+            both = grad[:, head_tile(5 * i + j)].astype(jnp.float32)
+            even = one(10 * i + 2 * j, jnp.where(first, 0.0, pltpu.roll(both, 64, 1)).astype(low))
+            odd = one(10 * i + 2 * j + 1, jnp.where(first, 0.0, both).astype(low))
+            grad_packed[:, head_tile(8 * i + j)] = jnp.where(first, even, pltpu.roll(odd, 64, 1)).astype(low)
+            for k, got in ((2 * j, even), (2 * j + 1, odd)):
+                at = 32 * (k % 4)
+                moved = got if at == 64 else pltpu.roll(got, (at + 64) % 128, 1)
+                rotary = jnp.where((lane >= at) & (lane < at + 32), moved, rotary)
+                if k % 4 == 3 or k == 9:
+                    grad_packed[:, head_tile(8 * i + 5 + k // 4)] = rotary.astype(low)
+                    rotary = jnp.zeros((rows, 128), jnp.float32)
+        return carry
+
+    return quarter
+
+
+def widen_kernel(*refs):
+    n = len(refs) // 2
+    for strips, out in zip(refs[:n], refs[n:]):
+        each = out.shape[1] // 8
+        for s in range(8):
+            first, last = s * each // 128, (s + 1) * each // 128
+            tiles = strips[s, 0].astype(jnp.float32)
+            if s * each % 128:
+                shared = strips[s - 1, 0, :, (first - (s - 1) * each // 128) * 128 :][:, :128]
+                out[:, first * 128 : first * 128 + 128] = tiles[:, :128] + shared.astype(jnp.float32)
+                first_full = first + 1
+            else:
+                first_full = first
+            base = s * each // 128
+            out[:, first_full * 128 : last * 128] = tiles[:, (first_full - base) * 128 : (last - base) * 128]
+
+
+def widen(arrays, cols):
+    _, quarters, rows, strip = arrays[0].shape
+    n = len(arrays)
+    return pl.pallas_call(
+        widen_kernel, grid=(quarters,),
+        out_shape=[jax.ShapeDtypeStruct((quarters * rows, cols), jnp.float32)] * n,
+        in_specs=[pl.BlockSpec((8, 1, rows, strip), lambda q: (0, q, 0, 0))] * n,
+        out_specs=[pl.BlockSpec((rows, cols), lambda q: (q, 0))] * n,
+        compiler_params=pltpu.CompilerParams(vmem_limit_bytes=56 * 2**20),
+    )(*arrays)
 
 
 class Gather:
@@ -312,169 +445,439 @@
     )(*arrays)
 
 
-def chain_sum_kernel(term, out, *refs):
-    total = Total(term, out, refs[:4], refs[4:])
-    greet(*place())
+def ffn_gather_kernel(tokens, partial, grad, down, tokens_all, up, grad_hidden, *scratch):
+    del partial
+    rep, zpos, core = place()
+    gather = Gather((tokens,), (tokens_all,), scratch[:5])
+    piece = up.shape[0] // 32
+
+    def part(m):
+        first = column_place(zpos, core, m, True) * (4 * piece)
+        return lambda p: up.at[pl.ds(mult(first + p * piece, 16), piece)]
+
+    spread = PlaneGather([(None, part(m), m % 2) for m in ColumnSwap.near], scratch[5:8])
+    greet(rep, zpos, core, plane=2)
+    gather.start()
+    spread.start()
+    chunk = grad.shape[0] // 4
+
+    def product(i):
+        at = pl.ds(mult(i * chunk, chunk), chunk)
+        grad_hidden[at] = dot_nt(grad[at], down[...])
+
+    def step(i, carry):
+        product(i)
+
+        @pl.when(i == 1)
+        def _():
+            gather.hop(1)
+
+        @pl.when(i == 3)
+        def _():
+            gather.hop(2)
+        return carry
+
+    lax.fori_loop(0, 4, step, 0)
+    for i in range(7):
+        spread.middle(i)
+    gather.hop(3)
+    gather.finish()
+    spread.finish()
+
+
+def ffn_gather(cid, tokens, partial, grad, down):
+    return pl.pallas_call(
+        ffn_gather_kernel,
+        out_shape=[jax.ShapeDtypeStruct((8 * tokens.shape[0], tokens.shape[1]), tokens.dtype),
+                   jax.ShapeDtypeStruct(partial.shape, partial.dtype),
+                   jax.ShapeDtypeStruct((grad.shape[0], down.shape[0]), jnp.float32)],
+        in_specs=[ANY, ANY, VMEM, VMEM], out_specs=[ANY, ANY, VMEM], input_output_aliases={1: 1},
+        scratch_shapes=Gather.scratch(1) + PlaneGather.scratch(7),
+        compiler_params=kernel_params(cid),
+    )(tokens, partial, grad, down)
+
+
+class PlaneSum:
+    def __init__(self, items, bufs, sems):
+        self.items = items
+        self.landed, self.stage, self.last = bufs
+        self.asend, self.arecv, self.bsend, self.brecv = sems
+        self.rep, self.zpos, self.core = place()
+        self.shard = self.zpos * 2 + self.core
+
+    @staticmethod
+    def scratch(shapes, dtype):
+        n = len(shapes)
+        return ([pltpu.VMEM((2,) + s, dtype) for s in shapes] + [pltpu.VMEM(s, dtype) for s in shapes] * 2
+                + [dma_sems(n, 2), dma_sems(n, 2), dma_sems(n), dma_sems(n)])
+
+    @staticmethod
+    def split(refs, n):
+        return (refs[:n], refs[n : 2 * n], refs[2 * n : 3 * n]), refs[3 * n : 3 * n + 4], refs[3 * n + 4 :]
+
+    def ways(self, i):
+        xrep, yrep, drep = plane_places(self.rep)
+        return (xrep, yrep, drep) if self.items[i][2] == 0 else (yrep, xrep, drep)
+
+    def out(self, i, k):
+        near, _, far = self.ways(i)
+        return remote(self.items[i][0](far if k else near), self.landed[i].at[k], self.asend.at[i, k], self.arecv.at[i, k],
+                      near, self.shard)
+
+    def on(self, i):
+        return remote(self.stage[i], self.last[i], self.bsend.at[i], self.brecv.at[i], self.ways(i)[1], self.shard)
+
+    def start(self, which=None):
+        for i in range(len(self.items)) if which is None else which:
+            for k in (1, 0):
+                self.out(i, k).start()
+
+    def middle(self, i):
+        wide = jnp.float32
+        self.out(i, 1).wait_recv()
+        term = self.items[i][0](self.ways(i)[1])
+        self.stage[i][...] = (term[...].astype(wide) + self.landed[i][1].astype(wide)).astype(self.stage[i].dtype)
+        self.on(i).start()
+
+    def end(self, i):
+        wide = jnp.float32
+        self.out(i, 0).wait_recv()
+        self.on(i).wait_recv()
+        total = self.items[i][0](self.rep)[...].astype(wide) + self.landed[i][0].astype(wide)
+        own = self.items[i][1]
+        own[...] = (total + self.last[i][...].astype(wide)).astype(own.dtype)
+
+    def finish(self):
+        for i in range(len(self.items)):
+            for k in range(2):
+                self.out(i, k).wait_send()
+            self.on(i).wait_send()
+
+
+class PlaneGather:
+    def __init__(self, items, sems):
+        self.items = items
+        self.send, self.recv, self.own = sems
+        self.rep, self.zpos, self.core = place()
+        self.shard = self.zpos * 2 + self.core
+
+    @staticmethod
+    def scratch(n):
+        return [dma_sems(3, n), dma_sems(3, n), dma_sems(n)]
+
+    def copy(self, i, kind, quarter, to):
+        own, part, _ = self.items[i]
+        dst = part(quarter)
+        return remote(dst if kind == 2 or own is None else own, dst, self.send.at[kind, i], self.recv.at[kind, i], to, self.shard)
+
+    def keep(self, i):
+        return pltpu.make_async_copy(self.items[i][0], self.items[i][1](self.rep), self.own.at[i])
+
+    def start(self, which=None):
+        xrep, yrep, _ = plane_places(self.rep)
+        for i in range(len(self.items)) if which is None else which:
+            self.copy(i, 0, self.rep, xrep).start()
+            self.copy(i, 1, self.rep, yrep).start()
+            if self.items[i][0] is not None:
+                self.keep(i).start()
+
+    def middle(self, i):
+        xrep, yrep, _ = plane_places(self.rep)
+        self.copy(i, 0, xrep, xrep).wait_recv()
+        if self.items[i][2] == 0:
+            self.copy(i, 2, xrep, yrep).start()
+        self.copy(i, 1, yrep, yrep).wait_recv()
+        if self.items[i][2] == 1:
+            self.copy(i, 2, yrep, xrep).start()
+
+    def finish(self):
+        xrep, yrep, drep = plane_places(self.rep)
+        for i, (own, _, first) in enumerate(self.items):
+            self.copy(i, 0, self.rep, xrep).wait_send()
+            self.copy(i, 1, self.rep, yrep).wait_send()
+            self.copy(i, 2, *((xrep, yrep) if first == 0 else (yrep, xrep))).wait_send()
+            self.copy(i, 2, drep, drep).wait_recv()
+            if own is not None:
+                self.keep(i).wait()
+
+
+class ColumnSwap:
+    def __init__(self, items, sems, keeps=True):
+        self.items, self.keeps = items, keeps
+        self.send, self.recv, self.own = sems
+        self.rep, self.zpos, self.core = place()
+        self.shard = self.zpos * 2 + self.core
+
+    near = (1, 2, 6, 3, 7, 4, 5)
+
+    @staticmethod
+    def scratch(n):
+        return [dma_sems(7, n), dma_sems(7, n), dma_sems(n)]
+
+    def copy(self, i, m, back=False):
+        s2 = column_place(self.zpos, self.core, m, back)
+        block, there = self.items[i]
+        return remote(block(s2), there(s2 if back else self.shard), self.send.at[m - 1, i], self.recv.at[m - 1, i], self.rep, s2)
+
+    def keep(self, i):
+        return pltpu.make_async_copy(self.items[i][0](self.shard), self.items[i][1](self.shard), self.own.at[i])
+
+    def start(self):
+        for m in self.near:
+            for i in range(len(self.items)):
+                self.copy(i, m).start()
+        for i in range(len(self.items) if self.keeps else 0):
+            self.keep(i).start()
+
+    def arrive(self, m):
+        for i in range(len(self.items)):
+            self.copy(i, m, True).wait_recv()
+
+    def finish(self, arrive=True):
+        for i in range(len(self.items)):
+            if self.keeps:
+                self.keep(i).wait()
+            for m in self.near:
+                self.copy(i, m).wait_send()
+                if arrive:
+                    self.copy(i, m, True).wait_recv()
+
+
+def quarter_cols(ref, first, rows, p):
+    width = ref.shape[1] // 4
+    return ref.at[pl.ds(first, rows), pl.ds(mult(p * width, 128), width)]
+
+
+def back_kernel(shift_unit, *refs):
+    term, down, gate, out, down_own, gate_own = refs[:6]
+    scratch = list(refs[6:])
+    rep, zpos, core = place()
+    total = Total(term, out, scratch[:4], scratch[4:9])
+    bufs, sems, _ = PlaneSum.split(scratch[9:], 4)
+    half = down_own.shape[0] // 2
+    shift = mult((zpos * 2 + core) % 4 * shift_unit, 16)
+
+    def down_item(h):
+        return (lambda p: quarter_cols(down, mult(shift + h * half, 16), half, p), down_own.at[pl.ds(h * half, half)], h)
+
+    def gate_item(h):
+        return (lambda p: gate.at[pl.ds(4 * h, 4), p], gate_own.at[pl.ds(4 * h, 4)], h)
+
+    sums = PlaneSum([down_item(0), down_item(1), gate_item(0), gate_item(1)], bufs, sems)
+    greet(rep, zpos, core, plane=2)
     total.start()
-    total.pair()
-    for step in range(3):
-        total.step(step)
-    total.finish()
-
-
-def chain_sum(cid, term):
-    return pl.pallas_call(
-        chain_sum_kernel, out_shape=jax.ShapeDtypeStruct(term.shape[1:], jnp.float32), in_specs=[ANY], out_specs=VMEM,
-        scratch_shapes=Total.scratch(term), compiler_params=kernel_params(cid),
-    )(term)
-
-
-def late_kernel(*refs):
-    branch, lat, cols, term, parts, down = refs[:6]
-    branch_all, lat_all, cols_all, out, parts_all, down_all = refs[6:12]
-    scratch = list(refs[12:])
-    rep, zpos, core = place()
-    shard = zpos * 2 + core
-    xrep, yrep, drep = plane_places(rep)
-    gather = Gather((branch, lat), (branch_all, lat_all), scratch[:5])
-    total = Total(term, out, scratch[5:9], scratch[9:14])
-    asend, arecv, esend, erecv, psend, precv, dsend, drecv, own = scratch[14:]
-
-    def cols_copy(m, back=False):
-        s2 = column_place(zpos, core, m, back)
-        here = cols_all.at[s2 if back else shard]
-        return remote(cols.at[s2], here, asend.at[m - 1], arecv.at[m - 1], rep, s2)
-
-    def parts_copy(m, which, back=False):
-        s2 = column_place(zpos, core, m, back)
-        return remote(parts.at[s2, which], parts_all.at[s2 if back else shard, rep, which],
-                      esend.at[m - 1, which], erecv.at[m - 1, which], rep, s2)
-
-    def parts_plane(m, which, quarter, kind, r):
-        ref = parts_all.at[column_place(zpos, core, m, True), quarter, which]
-        src = parts.at[shard, which] if m == 0 and kind < 2 else ref
-        return remote(src, ref, psend.at[kind, m, which], precv.at[kind, m, which], r, shard)
-
-    def down_plane(half, quarter, kind, r):
-        width = down.shape[1] // 2
-        at = (slice(None), pl.ds(half * width, width))
-        dst = down_all.at[(quarter,) + at]
-        return remote(down.at[at] if kind < 2 else dst, dst, dsend.at[kind, half], drecv.at[kind, half], r, shard)
-
-    def own_copies():
-        return (pltpu.make_async_copy(cols.at[shard], cols_all.at[shard], own.at[0]),
-                pltpu.make_async_copy(parts.at[shard], parts_all.at[shard, rep], own.at[1]),
-                pltpu.make_async_copy(down, down_all.at[rep], own.at[2]))
-
-    greet(rep, zpos, core, plane=2, column=True)
-    near = (1, 2, 6, 3, 7, 4, 5)
-    for m in near:
-        for which in range(2):
-            parts_copy(m, which).start()
-    total.start()
-    for half in range(2):
-        down_plane(half, rep, 0, xrep).start()
-        down_plane(half, rep, 1, yrep).start()
-        parts_plane(0, half, rep, 0, xrep).start()
-        parts_plane(0, half, rep, 1, yrep).start()
-    gather.start()
-    for m in near:
-        cols_copy(m).start()
-    for copy in own_copies():
-        copy.start()
-
-    def onward(kind_of, half, *first):
-        kind_of(*first, half, xrep, 0, xrep).wait_recv()
-        kind_of(*first, half, yrep, 1, yrep).wait_recv()
-        if half == 0:
-            kind_of(*first, half, xrep, 2, yrep).start()
-        else:
-            kind_of(*first, half, yrep, 2, xrep).start()
-
-    def from_column(m):
-        for which in range(2):
-            parts_copy(m, which, True).wait_recv()
-            parts_plane(m, which, rep, 0, xrep).start()
-            parts_plane(m, which, rep, 1, yrep).start()
-
+    sums.start()
     total.pair()
     total.step(0)
-    for m in near[:3]:
-        from_column(m)
-    for half in range(2):
-        onward(down_plane, half)
-        onward(parts_plane, half, 0)
-    gather.hop(1)
+    sums.middle(0)
+    sums.middle(1)
     total.step(1)
-    for m in near[3:]:
-        from_column(m)
-    for m in near[:3]:
-        for half in range(2):
-            onward(parts_plane, half, m)
-    gather.hop(2)
+    sums.middle(2)
+    sums.middle(3)
     total.step(2)
-    for m in near[3:]:
-        for half in range(2):
-            onward(parts_plane, half, m)
+    for i in range(4):
+        sums.end(i)
+    total.finish()
+    sums.finish()
+
+
+def back_sums(cid, term, down, gate, rows):
+    width = down.shape[1] // 4
+    kind = down.dtype
+    return pl.pallas_call(
+        functools.partial(back_kernel, rows % 128),
+        out_shape=[jax.ShapeDtypeStruct(term.shape[1:], jnp.float32), jax.ShapeDtypeStruct((rows, width), kind),
+                   jax.ShapeDtypeStruct((8,) + gate.shape[2:], kind)],
+        in_specs=[ANY, VMEM, VMEM], out_specs=[VMEM] * 3,
+        scratch_shapes=Total.scratch(term) + PlaneSum.scratch([(rows // 2, width)] * 2 + [(4,) + gate.shape[2:]] * 2, kind),
+        compiler_params=kernel_params(cid),
+    )(term, down, gate)
+
+
+def middle_kernel(scale, *refs):
+    branch, cols, term, down, up = refs[:5]
+    attend_in = refs[5:12]
+    branch_all, cols_all, out, down_all, up_own = refs[12:17]
+    attend_out = refs[17:21]
+    scratch = list(refs[21:])
+    left, scratch = scratch[0], scratch[1:]
+    rep, zpos, core = place()
+    gather = Gather((branch,), (branch_all,), scratch[:5])
+    total = Total(term, out, scratch[5:9], scratch[9:14])
+    swap = ColumnSwap([(lambda s: cols.at[s], lambda s: cols_all.at[s])], scratch[14:17])
+    half = down.shape[0] // 2
+    downs = PlaneGather(
+        [(down.at[pl.ds(h * half, half)], functools.partial(quarter_cols, down_all, h * half, half), h) for h in range(2)],
+        scratch[17:20])
+    bufs, sems, _ = PlaneSum.split(scratch[20:], 2)
+    sums = PlaneSum([(lambda p, h=h: up.at[pl.ds(4 * h, 4), p], up_own.at[pl.ds(4 * h, 4)], h) for h in range(2)], bufs, sems)
+    greet(rep, zpos, core, plane=2, column=True)
+    total.start()
+    gather.start()
+    sums.start()
+    downs.start()
+    swap.start()
+    left[...] = jnp.zeros_like(left)
+    attend_out[3][...] = jnp.zeros_like(attend_out[3])
+    quarter = attend_back_heads(scale, *attend_in, *attend_out, left)
+
+    def after_first():
+        total.pair()
+        total.step(0)
+
+    def after_second():
+        gather.hop(1)
+        sums.middle(0)
+        sums.middle(1)
+
+    def after_third():
+        total.step(1)
+        downs.middle(0)
+        downs.middle(1)
+
+    def after_fourth():
+        gather.hop(2)
+        total.step(2)
+
+    def step(i, carry):
+        quarter(i, carry)
+        for k, service in enumerate((after_first, after_second, after_third, after_fourth)):
+            pl.when(i == k)(service)
+        return carry
+
+    lax.fori_loop(0, 4, step, 0)
+    sums.end(0)
+    sums.end(1)
     gather.hop(3)
     total.finish()
     gather.finish()
-    for m in near:
-        cols_copy(m).wait_send()
-        cols_copy(m, True).wait_recv()
-        for which in range(2):
-            parts_copy(m, which).wait_send()
-
-    def settle(kind_of, half, *first):
-        kind_of(*first, half, rep, 0, xrep).wait_send()
-        kind_of(*first, half, rep, 1, yrep).wait_send()
-        if half == 0:
-            kind_of(*first, half, xrep, 2, yrep).wait_send()
-        else:
-            kind_of(*first, half, yrep, 2, xrep).wait_send()
-        kind_of(*first, half, drep, 2, drep).wait_recv()
-
-    for half in range(2):
-        settle(down_plane, half)
-        for m in range(8):
-            settle(parts_plane, half, m)
-    for copy in own_copies():
-        copy.wait()
-
-
-def late_exchange(cid, branch, lat, cols, term, parts, down):
-    out = [jax.ShapeDtypeStruct((8 * branch.shape[0], branch.shape[1]), branch.dtype),
-           jax.ShapeDtypeStruct((8 * lat.shape[0], lat.shape[1]), lat.dtype),
-           jax.ShapeDtypeStruct(cols.shape, cols.dtype),
-           jax.ShapeDtypeStruct(term.shape[1:], jnp.float32),
-           jax.ShapeDtypeStruct((8, 4) + parts.shape[1:], parts.dtype),
-           jax.ShapeDtypeStruct((4,) + down.shape, down.dtype)]
+    swap.finish()
+    downs.finish()
+    sums.finish()
+
+
+def middle_exchange(cid, scale, branch, cols, term, down, up, attend_in):
+    kind = branch.dtype
+    query, kv, rope = attend_in[:3]
+    rows = query.shape[0]
     return pl.pallas_call(
-        late_kernel, out_shape=out, in_specs=[ANY] * 6, out_specs=[ANY, ANY, ANY, VMEM, ANY, ANY],
-        scratch_shapes=Gather.scratch(2) + Total.scratch(term) + [
-            dma_sems(7), dma_sems(7), dma_sems(7, 2), dma_sems(7, 2), dma_sems(3, 8, 2), dma_sems(3, 8, 2),
-            dma_sems(3, 2), dma_sems(3, 2), dma_sems(3)],
+        functools.partial(middle_kernel, scale),
+        out_shape=[jax.ShapeDtypeStruct((8 * branch.shape[0], branch.shape[1]), kind), jax.ShapeDtypeStruct(cols.shape, kind),
+                   jax.ShapeDtypeStruct(term.shape[1:], jnp.float32),
+                   jax.ShapeDtypeStruct((down.shape[0], 4 * down.shape[1]), kind), jax.ShapeDtypeStruct((8,) + up.shape[2:], kind),
+                   jax.ShapeDtypeStruct(query.shape, kind), jax.ShapeDtypeStruct((rows, 4096), kind),
+                   jax.ShapeDtypeStruct(kv.shape, kind), jax.ShapeDtypeStruct(rope.shape, jnp.float32)],
+        in_specs=[ANY] * 4 + [VMEM] * 8, out_specs=[ANY, ANY, VMEM, ANY] + [VMEM] * 5,
+        scratch_shapes=[pltpu.VMEM((2 * rows, 256), kind)]
+        + Gather.scratch(1) + Total.scratch(term) + ColumnSwap.scratch(1) + PlaneGather.scratch(2)
+        + PlaneSum.scratch([(4,) + up.shape[2:]] * 2, kind),
         compiler_params=kernel_params(cid),
-    )(branch, lat, cols, term, parts, down)
+    )(branch, cols, term, down, up, *attend_in)
+
+
+def late_kernel(lat, gate, up, query_up, latent_up, lat_all, gate_all, up_all, query_sum, latent_sum, *scratch):
+    rep, zpos, core = place()
+    shard = zpos * 2 + core
+    gather = Gather((lat,), (lat_all,), scratch[:5])
+    pairs = ((gate, gate_all), (up, up_all))
+    swap = ColumnSwap([(lambda s, a=a: a.at[s], lambda s, b=b: b.at[s, rep]) for a, b in pairs], scratch[5:8], keeps=False)
+
+    def part(m, b):
+        return lambda p: b.at[shard if m == 0 else column_place(zpos, core, m, True), p]
+
+    spread = PlaneGather(
+        [(a.at[shard] if m == 0 else None, part(m, b), h) for m in range(8) for h, (a, b) in enumerate(pairs)], scratch[8:11])
+    bufs, sems, rest = PlaneSum.split(scratch[11:], 2)
+    query_part = rest[0]
+    width = query_up.shape[2] // 4
+
+    def query_item(h):
+        return (lambda p: query_up.at[pl.ds(4 * h, 4), :, pl.ds(mult(p * width, 128), width)], query_part.at[pl.ds(4 * h, 4)], h)
+
+    sums = PlaneSum([query_item(0), query_item(1)], bufs, sems)
+    query_total = Total(query_part, query_sum, rest[1:5], rest[5:10])
+    latent_total = Total(latent_up, latent_sum, rest[10:14], rest[14:19])
+    greet(rep, zpos, core, plane=2, column=True)
+    sums.start()
+    spread.start((0, 1))
+    swap.start()
+    latent_total.start()
+    gather.start()
+    near = ColumnSwap.near
+    for i, m in enumerate(near):
+        swap.arrive(m)
+        spread.start((2 * m, 2 * m + 1))
+        if i == 0:
+            sums.middle(0)
+            sums.middle(1)
+        before = 0 if i == 0 else near[i - 1]
+        spread.middle(2 * before)
+        spread.middle(2 * before + 1)
+        if i == 2:
+            latent_total.pair()
+            latent_total.step(0)
+            sums.end(0)
+            sums.end(1)
+            query_total.start()
+        if i in (1, 3, 5):
+            gather.hop((i + 1) // 2)
+        if i == 4:
+            latent_total.step(1)
+            query_total.pair()
+            query_total.step(0)
+        if i == 6:
+            latent_total.step(2)
+            query_total.step(1)
+    query_total.step(2)
+    spread.middle(2 * near[-1])
+    spread.middle(2 * near[-1] + 1)
+    latent_total.finish()
+    query_total.finish()
+    gather.finish()
+    swap.finish(arrive=False)
+    spread.finish()
+    sums.finish()
+
+
+def late_exchange(cid, lat, gate, up, query_up, latent_up):
+    kind = gate.dtype
+    part = jax.ShapeDtypeStruct((8, query_up.shape[1], query_up.shape[2] // 4), kind)
+    half = (4,) + part.shape[1:]
+    return pl.pallas_call(
+        late_kernel,
+        out_shape=[jax.ShapeDtypeStruct((8 * lat.shape[0], lat.shape[1]), lat.dtype)]
+        + [jax.ShapeDtypeStruct((8, 4) + gate.shape[1:], kind)] * 2
+        + [jax.ShapeDtypeStruct(part.shape[1:], jnp.float32), jax.ShapeDtypeStruct(latent_up.shape[1:], jnp.float32)],
+        in_specs=[ANY] * 3 + [VMEM, ANY], out_specs=[ANY] * 3 + [VMEM] * 2,
+        scratch_shapes=Gather.scratch(1) + ColumnSwap.scratch(2) + PlaneGather.scratch(16)
+        + PlaneSum.scratch([half] * 2, kind) + [pltpu.VMEM(part.shape, kind)] + Total.scratch(part) + Total.scratch(latent_up),
+        compiler_params=kernel_params(cid),
+    )(lat, gate, up, query_up, latent_up)
 
 
 def last_kernel(n, *refs):
-    terms, gain = refs[:n], refs[n]
-    outs, gain_out = refs[n + 1 : 2 * n + 1], refs[2 * n + 1]
-    scratch = list(refs[2 * n + 2 :])
-    landed, sums = scratch[:n], scratch[n : 2 * n]
-    gain_landed, gain_sum, gain_plane, ssend, srecv, tsend, trecv, gsend, grecv, hsend, hrecv = scratch[2 * n :]
+    terms, done, gain = refs[:n], refs[n], refs[n + 1]
+    outs, done_out, gain_out = refs[n + 2 : 2 * n + 2], refs[2 * n + 2], refs[2 * n + 3]
+    scratch = list(refs[2 * n + 4 :])
+    landed, sums = scratch[:n], scratch[n : 2 * n + 1]
+    gain_landed, gain_sum, gain_plane, ssend, srecv, tsend, trecv, gsend, grecv, hsend, hrecv = scratch[2 * n + 1 :]
     rep, zpos, core = place()
     shard = zpos * 2 + core
     places = plane_places(rep)
     wide = jnp.float32
     greet(rep, zpos, core, plane=3, column=True)
 
+    def quarter(ref, p):
+        if len(ref.shape) == 3:
+            return ref.at[p]
+        return quarter_cols(ref, 0, ref.shape[0], p)
+
     def term_copy(a, k):
-        return remote(terms[a].at[places[k]], landed[a].at[k], ssend.at[k, a], srecv.at[k, a], places[k], shard)
+        return remote(quarter(terms[a], places[k]), landed[a].at[k], ssend.at[k, a], srecv.at[k, a], places[k], shard)
 
     def sum_copy(a, k, back=False):
-        return remote(sums[a], outs[a].at[places[k] if back else rep], tsend.at[k, a], trecv.at[k, a], places[k], shard)
+        out = quarter((*outs, done_out)[a], places[k] if back else rep)
+        return remote(sums[a], out, tsend.at[k, a], trecv.at[k, a], places[k], shard)
 
     def gain_copy(m):
         s2 = column_place(zpos, core, m)
@@ -482,12 +885,19 @@
 
     def gain_on(k):
         return remote(gain_sum, gain_plane.at[k], hsend.at[k], hrecv.at[k], places[k], shard)
+
+    def hand_on(a):
+        for k in range(3):
+            sum_copy(a, k).start()
+        quarter((*outs, done_out)[a], rep)[...] = sums[a][...]
 
     for m in range(1, 8):
         gain_copy(m).start()
     for a in range(n):
         for k in range(3):
             term_copy(a, k).start()
+    sums[n][...] = done[...].astype(sums[n].dtype)
+    hand_on(n)
     gain_sum[...] = gain[shard]
     for m in range(1, 8):
         gain_copy(m).wait_recv()
@@ -495,40 +905,41 @@
     for k in range(3):
         gain_on(k).start()
     for a in range(n):
-        total = terms[a][rep].astype(wide)
+        total = quarter(terms[a], rep)[...].astype(wide)
         for k in range(3):
             term_copy(a, k).wait_recv()
             total = total + landed[a][k].astype(wide)
         sums[a][...] = total.astype(jnp.bfloat16)
-        for k in range(3):
-            sum_copy(a, k).start()
-        outs[a][rep] = sums[a][...]
+        hand_on(a)
     gain_out[...] = gain_sum[...]
     for k in range(3):
         gain_on(k).wait_recv()
         gain_out[...] += gain_plane[k]
     for k in range(3):
         gain_on(k).wait_send()
-        for a in range(n):
-            term_copy(a, k).wait_send()
+        for a in range(n + 1):
+            if a < n:
+                term_copy(a, k).wait_send()
             sum_copy(a, k).wait_send()
             sum_copy(a, k, True).wait_recv()
     for m in range(1, 8):
         gain_copy(m).wait_send()
 
 
-def last_sums(cid, terms, gain):
+def last_sums(cid, terms, done, gain):
     n = len(terms)
-    out = [jax.ShapeDtypeStruct(t.shape, jnp.bfloat16) for t in terms] + [jax.ShapeDtypeStruct(gain.shape[1:], gain.dtype)]
+    low = jnp.bfloat16
+    out = [jax.ShapeDtypeStruct(t.shape, low) for t in terms]
+    out += [jax.ShapeDtypeStruct((done.shape[0], 4 * done.shape[1]), low), jax.ShapeDtypeStruct(gain.shape[1:], gain.dtype)]
+    cut = [t.shape[1:] if len(t.shape) == 3 else (t.shape[0], t.shape[1] // 4) for t in terms]
     block = pltpu.VMEM(gain.shape[1:], gain.dtype)
     return pl.pallas_call(
-        functools.partial(last_kernel, n), out_shape=out, in_specs=[VMEM] * (n + 1), out_specs=[VMEM] * (n + 1),
-        scratch_shapes=[pltpu.VMEM((3,) + t.shape[1:], t.dtype) for t in terms]
-        + [pltpu.VMEM(t.shape[1:], t.dtype) for t in terms]
+        functools.partial(last_kernel, n), out_shape=out, in_specs=[VMEM] * (n + 2), out_specs=[VMEM] * (n + 2),
+        scratch_shapes=[pltpu.VMEM((3,) + c, low) for c in cut] + [pltpu.VMEM(c, low) for c in cut] + [pltpu.VMEM(done.shape, low)]
         + [pltpu.VMEM((7,) + gain.shape[1:], gain.dtype), block, pltpu.VMEM((3,) + gain.shape[1:], gain.dtype)]
-        + [dma_sems(3, n)] * 4 + [dma_sems(7)] * 2 + [dma_sems(3)] * 2,
+        + [dma_sems(3, n + 1)] * 4 + [dma_sems(7)] * 2 + [dma_sems(3)] * 2,
         compiler_params=kernel_params(cid),
-    )(*terms, gain)
+    )(*terms, done, gain)
 
 def start_kernel(*refs):
     ins, (gate, up) = refs[:7], refs[7:9]
@@ -633,9 +1044,9 @@
         return remote(slice_of(which, s2, rep * quarter_rows, quarter_rows), rows_of(which, shard, rep),
                       gsend.at[m - 1, which], grecv.at[m - 1, which], rep, s2)
 
-    def slice_plane(m, which, quarter, kind, r):
-        ref = rows_of(which, column_place(zpos, core, m, back=True), quarter)
-        return remote(ref, ref, psend.at[kind, m - 1, which], precv.at[kind, m - 1, which], r, shard)
+    def slice_plane(m, quarter, kind, r):
+        ref = rows_of(0, column_place(zpos, core, m, back=True), quarter)
+        return remote(ref, ref, psend.at[kind, m - 1], precv.at[kind, m - 1], r, shard)
 
     def own_slice(which, half):
         if half == 0:
@@ -661,17 +1072,16 @@
             s2 = column_place(zpos, core, m, back=True)
             ref = rows_of(which, s2, rep)
             remote(ref, ref, gsend.at[m - 1, which], grecv.at[m - 1, which], rep, s2).wait_recv()
-            slice_plane(m, which, rep, 0, xrep).start()
-            slice_plane(m, which, rep, 1, yrep).start()
+        slice_plane(m, rep, 0, xrep).start()
+        slice_plane(m, rep, 1, yrep).start()
 
     def slices_from_plane(m):
-        for which in range(2):
-            slice_plane(m, which, xrep, 0, xrep).wait_recv()
-            slice_plane(m, which, yrep, 1, yrep).wait_recv()
-            if which == 0:
-                slice_plane(m, which, xrep, 2, yrep).start()
-            else:
-                slice_plane(m, which, yrep, 2, xrep).start()
+        slice_plane(m, xrep, 0, xrep).wait_recv()
+        slice_plane(m, yrep, 1, yrep).wait_recv()
+        slice_plane(m, *onward(m)).start()
+
+    def onward(m):
+        return (xrep, 2, yrep) if m % 2 else (yrep, 2, xrep)
 
     def from_column(h, way, z, slots=range(4)):
         for a in slots:
@@ -744,13 +1154,11 @@
         own_slice(which, 1).wait()
         for m in near:
             slice_copy(m, which).wait_send()
-            slice_plane(m, which, rep, 0, xrep).wait_send()
-            slice_plane(m, which, rep, 1, yrep).wait_send()
-            if which == 0:
-                slice_plane(m, which, xrep, 2, yrep).wait_send()
-            else:
-                slice_plane(m, which, yrep, 2, xrep).wait_send()
-            slice_plane(m, which, drep, 2, drep).wait_recv()
+    for m in near:
+        slice_plane(m, rep, 0, xrep).wait_send()
+        slice_plane(m, rep, 1, yrep).wait_send()
+        slice_plane(m, *onward(m)).wait_send()
+        slice_plane(m, drep, 2, drep).wait_recv()
     for way in range(2):
         for h in range(3):
             z = zpos - h if way == 0 else zpos + h
@@ -780,7 +1188,7 @@
     return pl.pallas_call(
         start_kernel, out_shape=out, in_specs=[ANY] * 9, out_specs=[ANY] * 9,
         scratch_shapes=[dma_sems(2, 3, 6), dma_sems(2, 3, 6)] + [dma_sems(6, 4)] * 6
-        + [dma_sems(7, 7), dma_sems(7, 7), dma_sems(2, 9), dma_sems(7, 2), dma_sems(7, 2), dma_sems(3, 7, 2), dma_sems(3, 7, 2)]
+        + [dma_sems(7, 7), dma_sems(7, 7), dma_sems(2, 9), dma_sems(7, 2), dma_sems(7, 2), dma_sems(3, 7), dma_sems(3, 7)]
         + [pltpu.VMEM(a.shape, a.dtype) for a in weights] + [pltpu.VMEM((gate.shape[0], strip), gate.dtype)] * 2,
         compiler_params=kernel_params(cid),
     )(*weights, gate, up)
@@ -811,8 +1219,6 @@
     rows, width = tokens.shape[1], tokens.shape[2]
     seq_len = rows * 4
     head_dim = ND + RD
-    group = 8
-    groups = H // group
     scale = head_dim ** (-0.5)
     rep, shard = lax.axis_index("rep"), lax.axis_index("shard")
     slice_ff = FF // 8
@@ -823,10 +1229,13 @@
         [v.astype(wide) for v in (gain_attn, gain_ffn, gain_query, gain_latent)]
         + [jnp.zeros((1024 - 768,), wide)]
     ).reshape(8, 128)
+    tile_up = jnp.pad(
+        query_up.reshape(-1, H, head_dim), ((0, 0), (0, 0), (0, 128 - head_dim))
+    ).reshape(-1, H * 128)
     grad_out = cotangent[0].astype(wide)
     grad_down_in = (residual_scale * grad_out).astype(low)
-    aout, qdown, ldown, qup, lup, gd_all, small_all, gate_w, up_w = start_gather(
-        0, (attn_out, query_down, latent_down, query_up, latent_up, grad_down_in, small), w_gate, w_up, strip
+    aout, qdown, ldown, qup, lup, gd_all, small_all, gate_w, up_quarter = start_gather(
+        0, (attn_out, query_down, latent_down, tile_up, latent_up, grad_down_in, small), w_gate, w_up, strip
     )
     small_all = small_all.reshape(8, 1024)
     gain_in = small_all[:, :320].reshape(-1)
@@ -843,7 +1252,18 @@
     query_seg, query_off = segment_of(doc_lengths[0], local_pos)
     key_seg = segment_of(doc_lengths[0], key_pos)[0]
     allowed = (query_seg[:, None] == key_seg[None, :]) & (key_pos[None, :] <= local_pos[:, None])
+    bias = jnp.where(allowed, 0.0, masked_score).astype(wide)
     cos_part, sin_part = rope_tables(query_off, RD)
+    none = jnp.zeros((rows, RD // 2), wide)
+    edge = jnp.zeros((rows, ND), wide)
+    tail = jnp.zeros((rows, 128 - head_dim), wide)
+    turns = jnp.stack(
+        [
+            jnp.concatenate([edge + 1.0, cos_part, cos_part, tail], axis=1),
+            jnp.concatenate([edge, none, sin_part, tail], axis=1),
+            jnp.concatenate([edge, -sin_part, none, tail], axis=1),
+        ]
+    )
     inputs = tokens[0].astype(wide)
     normed, norm_in_back = jax.vjp(rms_scale, inputs, gain_in)
     normed_low = normed.astype(low)
@@ -860,143 +1280,66 @@
     query_lat = jnp.dot(normed_low, qdown, preferred_element_type=wide)
     query_norm, norm_q_back = jax.vjp(rms_scale, query_lat, gain_q)
     query_low = query_norm.astype(low)
-    query_proj = jnp.dot(query_low, qup, preferred_element_type=wide).reshape(rows, H, head_dim)
-
-    def query_rope(values):
-        return jnp.concatenate(
-            [
-                values[..., :ND],
-                rotate(values[..., ND:], cos_part[:, None, :], sin_part[:, None, :]),
-            ],
-            axis=-1,
-        )
-
-    query_rot, query_back = jax.vjp(query_rope, query_proj)
-    query_used = query_rot.astype(low)
+    query_proj = jnp.dot(query_low, qup, preferred_element_type=wide)
     keyvals = jnp.dot(latent_low, lup, preferred_element_type=wide).astype(low)
-    queries = query_used.reshape(rows, groups, group, head_dim).transpose(1, 0, 2, 3)
-    key_groups = keyvals.reshape(seq_len, groups, group, ND + VD).transpose(1, 0, 2, 3)
-
-    def scores_of(query_blk, key_blk):
-        nope_part = jnp.einsum(
-            "thd,shd->hts", query_blk[..., :ND], key_blk[..., :ND], preferred_element_type=wide
-        )
-        rope_part = jnp.einsum(
-            "thd,sd->hts", query_blk[..., ND:], all_rope, preferred_element_type=wide
-        )
-        return jnp.where(allowed[None], (nope_part + rope_part) * scale, masked_score)
-
-    def forward_group(carry, blocks):
-        query_blk, key_blk = blocks
-        scores = scores_of(query_blk, key_blk)
-        row_max = jnp.max(scores, axis=-1, keepdims=True)
-        exp_scores = jnp.exp(scores - row_max)
-        totals = jnp.sum(exp_scores, axis=-1, keepdims=True)
-        probs = (exp_scores / totals).astype(low)
-        mixed = jnp.einsum("hts,shd->thd", probs, key_blk[..., ND:], preferred_element_type=wide)
-        return (carry, (mixed, row_max + jnp.log(totals)))
-
-    _, (mixed_groups, log_totals) = lax.scan(
-        forward_group, jnp.zeros((), wide), (queries, key_groups)
-    )
-    mixed_low = mixed_groups.transpose(1, 0, 2, 3).reshape(rows, H * VD).astype(low)
+    rope_tile = jnp.pad(all_rope, ((0, 0), (ND, 128 - head_dim)))
+    queries, mixed_low, logs = attend(scale, query_proj, keyvals, rope_tile, bias, turns)
     branch = jnp.dot(mixed_low, aout, preferred_element_type=wide)
     residual = inputs + residual_scale * branch
     normed_ffn, norm_f_back = jax.vjp(rms_scale, residual, gain_f)
     ffn_low = normed_ffn.astype(low)
 
-    (ffn_all,) = chain_gather(1, ffn_low)
+    ffn_all, up_w, grad_hidden = ffn_gather(1, ffn_low, up_quarter, gd_all, down_w)
     gate_pre = jnp.dot(ffn_all, gate_w, preferred_element_type=wide)
     up_pre = jnp.dot(ffn_all, up_w, preferred_element_type=wide)
     hidden, act_back = jax.vjp(swiglu, gate_pre, up_pre)
     hidden_low = hidden.astype(low)
-    grad_hidden = outer_cols(gd_all, down_w)
     grad_gate_f, grad_up_f = act_back(grad_hidden)
     grad_gate = grad_gate_f.astype(low)
     grad_up = grad_up_f.astype(low)
     ffn_in_part = (outer_cols(grad_gate, gate_w) + outer_cols(grad_up, up_w)).astype(low)
-    grad_ffn_in = chain_sum(2, ffn_in_part.reshape(8, rows, width))
     out_part = jnp.dot(hidden_low, down_w, preferred_element_type=wide).astype(low)
-    down_part = lax.dynamic_slice(
-        inner_rows(hidden_low, gd_all).astype(low), (shift, 0), (slice_ff, width)
-    )
-    gate_part = inner_rows(ffn_all, grad_gate).astype(low)
-    up_part = inner_rows(ffn_all, grad_up).astype(low)
-    down_own = lax.psum_scatter(
-        down_part.reshape(4, slice_ff // 4, width), "rep", scatter_dimension=0, tiled=False
-    )
-    parts_own = lax.psum_scatter(
-        jnp.stack([gate_part.reshape(8, 4, 80, strip), up_part.reshape(8, 4, 80, strip)])
-        .transpose(2, 1, 0, 3, 4),
-        "rep",
-        scatter_dimension=0,
-        tiled=False,
+    down_part = inner_rows(hidden_low, gd_all).astype(low)
+    gate_part = inner_rows(ffn_all, grad_gate).astype(low).reshape(8, 4, -1, strip)
+    up_part = inner_rows(ffn_all, grad_up).astype(low).reshape(8, 4, -1, strip)
+    grad_ffn_in, down_own, gate_own = back_sums(
+        2, ffn_in_part.reshape(8, rows, width), down_part, gate_part, slice_ff
     )
 
     grad_res_norm, grad_gain_ffn = norm_f_back(grad_ffn_in)
     grad_resid = grad_out + grad_res_norm
     grad_branch = (residual_scale * grad_resid).astype(low)
     grad_mixed = outer_cols(grad_branch, aout).astype(low)
-    grad_groups = grad_mixed.reshape(rows, groups, group, VD).transpose(1, 0, 2, 3)
-
-    def backward_group(rope_acc, blocks):
-        query_blk, key_blk, grad_blk, log_blk = blocks
-        scores = scores_of(query_blk, key_blk)
-        probs = jnp.exp(scores - log_blk)
-        grad_probs = jnp.einsum(
-            "thd,shd->hts", grad_blk, key_blk[..., ND:], preferred_element_type=wide
-        )
-        delta = jnp.sum(probs * grad_probs, axis=-1, keepdims=True)
-        grad_scores = (probs * (grad_probs - delta)).astype(low)
-        grad_query = (
-            jnp.concatenate(
-                [
-                    jnp.einsum(
-                        "hts,shd->thd",
-                        grad_scores,
-                        key_blk[..., :ND],
-                        preferred_element_type=wide,
-                    ),
-                    jnp.einsum(
-                        "hts,sd->thd", grad_scores, all_rope, preferred_element_type=wide
-                    ),
-                ],
-                axis=-1,
-            )
-            * scale
-        )
-        grad_key = (
-            jnp.einsum(
-                "hts,thd->shd", grad_scores, query_blk[..., :ND], preferred_element_type=wide
-            )
-            * scale
-        )
-        grad_value = jnp.einsum(
-            "hts,thd->shd", probs.astype(low), grad_blk, preferred_element_type=wide
-        )
-        rope_acc = (
-            rope_acc
-            + jnp.einsum(
-                "hts,thd->sd", grad_scores, query_blk[..., ND:], preferred_element_type=wide
-            )
-            * scale
-        )
-        return (rope_acc, (grad_query, jnp.concatenate([grad_key, grad_value], axis=-1)))
-
-    rope_sum, (grad_q_groups, grad_kv_groups) = lax.scan(
-        backward_group,
-        jnp.zeros((seq_len, RD), wide),
-        (queries, key_groups, grad_groups, log_totals),
-    )
-    grad_kv = grad_kv_groups.transpose(1, 0, 2, 3).reshape(seq_len, H * (ND + VD)).astype(low)
+    cols = jnp.stack([mixed_low, normed_low]).reshape(2, rows, 8, width // 8).transpose(2, 0, 1, 3)
+    (
+        branch_all,
+        cols_all,
+        out_sum,
+        down_all,
+        up_own,
+        grad_q_proj,
+        grad_q_packed,
+        grad_kv,
+        grad_rope,
+    ) = middle_exchange(
+        3,
+        scale,
+        grad_branch,
+        cols,
+        out_part.reshape(8, rows, width),
+        down_own,
+        up_part,
+        (queries, keyvals, rope_tile, bias, turns, logs, grad_mixed),
+    )
+    layer_out = (residual + residual_scale * out_sum).astype(low)
+    down_grad = down_all.astype(wide)
+    rope_sum = grad_rope[:, ND:head_dim]
     grad_lat_part = jnp.concatenate([outer_cols(grad_kv, lup), rope_sum], axis=1).astype(low)
     grad_lat_own = grad_lat_part[:rows].astype(wide)
     for j in range(1, 4):
         grad_lat_own = grad_lat_own + plane_swap(
             grad_lat_part[j * rows : (j + 1) * rows], j
         ).astype(wide)
-    grad_q_full = grad_q_groups.transpose(1, 0, 2, 3).reshape(rows, H, head_dim)
-    grad_q_proj = query_back(grad_q_full)[0].reshape(rows, H * head_dim).astype(low)
     grad_q_lat_f, grad_gain_query = norm_q_back(outer_cols(grad_q_proj, qup))
     grad_q_lat = grad_q_lat_f.astype(low)
     grad_lat_c, grad_gain_latent = norm_l_back(grad_lat_own[:, :KR])
@@ -1006,34 +1349,14 @@
     grad_in_norm, grad_gain_attn = norm_in_back(grad_normed)
     tokens_grad = (grad_resid + grad_in_norm).astype(low)
 
-    qup_grad = inner_rows(query_low, grad_q_proj).astype(low)
-    lup_grad = inner_rows(latent_low, grad_kv).astype(low)
-
-    def scattered(grad):
-        grad = grad.reshape(8, 4, grad.shape[0] // 32, grad.shape[1])
-        part = lax.psum_scatter(grad, "rep", scatter_dimension=1, tiled=False)
-        part = lax.psum_scatter(part, "shard", scatter_dimension=0, tiled=False)
-        return lax.all_gather(part, "rep", axis=0, tiled=True).astype(wide)
-
-    qup_own, lup_own = scattered(qup_grad), scattered(lup_grad)
+    qup_part = inner_rows(query_low, grad_q_packed).astype(low)
+    lup_part = inner_rows(latent_low, grad_kv).astype(low)
     grad_lats = jnp.concatenate([grad_q_lat, grad_lat], axis=1)
-    cols = jnp.stack([mixed_low, normed_low]).reshape(2, rows, 8, width // 8).transpose(2, 0, 1, 3)
-    branch_all, lat_all, cols_all, out_sum, parts_all, down_all = late_exchange(
-        3, grad_branch, grad_lats, cols, out_part.reshape(8, rows, width), parts_own, down_own
-    )
-    layer_out = (residual + residual_scale * out_sum).astype(low)
-    down_grad = down_all.reshape(slice_ff, width).astype(wide)
-
-    def slices(which):
-        return jnp.concatenate(
-            [
-                parts_all[s, :, which, :, (slice_ff * s) % 128 : (slice_ff * s) % 128 + slice_ff]
-                for s in range(8)
-            ],
-            axis=-1,
-        ).reshape(-1, FF).astype(wide)
-
-    gate_grad, up_grad = slices(0), slices(1)
+    lat_all, gate_all, up_all, qup_sum, lup_sum = late_exchange(
+        4, grad_lats, gate_own, up_own,
+        qup_part.reshape(8, -1, qup_part.shape[1]), lup_part.reshape(8, -1, lup_part.shape[1]),
+    )
+    gate_grad, up_grad = widen((gate_all, up_all), FF)
     mixed_cols = cols_all[:, 0].reshape(8 * rows, width // 8)
     normed_cols = cols_all[:, 1].reshape(8 * rows, width // 8)
     aout_part = inner_rows(mixed_cols, branch_all).astype(low)
@@ -1046,11 +1369,21 @@
         + [jnp.zeros((8, 1024 - 768), wide)],
         axis=1,
     ).reshape(8, 8, 128)
-    aout_own, lat_own, gain_own = last_sums(
-        4, (aout_part.reshape(4, 80, width), lat_part.reshape(4, 80, -1)), gains
-    )
-    aout_own = aout_own.reshape(320, width).astype(wide)
+    aout_own, lat_own, lup_own, qup_own, gain_own = last_sums(
+        5, (aout_part, lat_part.reshape(4, 80, -1), lup_sum.astype(low)), qup_sum, gains
+    )
+    aout_own = aout_own.astype(wide)
     lat_own = lat_own.reshape(320, -1).astype(wide)
+    lup_own = lup_own.astype(wide)
+    qup_own = qup_own.reshape(-1, 4, 1024)
+    quarter_heads = H // 4
+    qup_own = jnp.concatenate(
+        [
+            qup_own[:, :, : quarter_heads * ND].reshape(-1, H, ND),
+            qup_own[:, :, quarter_heads * ND : quarter_heads * head_dim].reshape(-1, H, RD),
+        ],
+        axis=-1,
+    ).reshape(-1, H * head_dim).astype(wide)
     gain_own = gain_own.reshape(1024)
 
     return (

time: 1110 us -> 842 us (0.76)
  waiting for transfers between devices: 209 us -> 0.02 us
  Pallas kernels: 503 us -> 642 us
  local copies, waits for them, and re-layouts: 88.9 us -> 29.7 us
  matrix products: 179 us -> 127 us
  other arithmetic: 72.9 us -> 30.2 us
  blocking collectives: 22.2 us -> 0 us
  between operations: 15.7 us -> 1.78 us
    unnamed x10 -> x0, waiting for transfers between devices: 209 us -> none
    pallas_call x3 -> x6, Pallas kernels: 267 us -> 412 us  [the longest x1 139 us: late_exchange(): pl.pallas_call(late_kernel, out_shape=[jax.ShapeDtypeStruct((8 * lat.shap...]
    dot_general x56 -> x1, matrix products: 42.8 us -> 7.67 us  [column_body(): query_proj = jnp.dot(query_low, qup, preferred_element_type=wide)]
    all_gather x2 -> x0, blocking collectives: 22.2 us -> none  [scattered(): return lax.all_gather(part, 'rep', axis=0, tiled=True).astype(wide)]
    pallas_call x1, Pallas kernels: 176 us -> 155 us  [start_gather(): pl.pallas_call(start_kernel, out_shape=out, in_specs=[ANY] * 9, out_specs...]
    concatenate x2 -> x3, local copies, waits for them, and re-layouts: 16.4 us -> 0.09 us  [the longest x2 0.08 us: column_body(): jnp.concatenate([edge + 1.0, cos_part, cos_part, tail], axis=1)]
    pallas_call x1, Pallas kernels: 59.4 us -> 74.8 us  [last_sums(): pl.pallas_call(functools.partial(last_kernel, n), out_shape=out, in_specs...]
    squeeze x20 -> x0, local copies, waits for them, and re-layouts: 13.2 us -> none  [column_body(): lax.scan(forward_group, jnp.zeros((), wide), (queries, key_groups))]
  transfers between devices with their start and end apart: 12 -> 6, of which waited for: 4 -> 0; matrix products, arithmetic and copies ran while one was open for 10% -> 4% of each run, Pallas kernels for 0% -> 0%
where the time goes in v2:
time: 842 us; the launch traced here: 837 us
  Pallas kernels  642 us (76%)
  matrix products  127 us (15%)
  other arithmetic  30.2 us (4%)
  local copies, waits for them, and re-layouts  29.7 us (4%)
    pallas_call x1, Pallas kernels, start_gather(): pl.pallas_call(start_kernel, out_shape=out, in_specs=[ANY] * 9, out_specs...  155 us
    pallas_call x1, Pallas kernels, late_exchange(): pl.pallas_call(late_kernel, out_shape=[jax.ShapeDtypeStruct((8 * lat.shap...  139 us
    pallas_call x1, Pallas kernels, middle_exchange(): pl.pallas_call(functools.partial(middle_kernel, scale), out_shape=[jax.Sh...  105 us
    pallas_call x1, Pallas kernels, back_sums(): pl.pallas_call(functools.partial(back_kernel, rows % 128), out_shape=[jax...  79.4 us
    pallas_call x1, Pallas kernels, last_sums(): pl.pallas_call(functools.partial(last_kernel, n), out_shape=out, in_specs...  74.8 us
    pallas_call x1, Pallas kernels, ffn_gather(): pl.pallas_call(ffn_gather_kernel, out_shape=[jax.ShapeDtypeStruct((8 * to...  55.3 us
    dot_general x7, matrix products, inner_rows(): lax.dot_general(leading, trailing, (((0,), (0,)), ((), ())), preferred_el...  39.3 us
    dot_general x7, matrix products, outer_cols(): lax.dot_general(leading, trailing, (((1,), (1,)), ((), ())), preferred_el...  38.4 us
  transfers between devices with their start and end apart: 6, of which 0 were waited for; matrix products, arithmetic and copies ran while one was open for 4% of the time, Pallas kernels for 0%

profile of v2, /device:TPU:0, one launch (start us, length us, event | category | flops | bytes accessed | tf_op | source)
XLA Modules:
  0.0 837.4 jit_solution(6234781856361580788)
XLA Ops:
  2.4 2.6 reshape.229
  8.1 154.5 %shard_map.254 = (bf16[2560,2560]{1,0:T(8,128)(2,1)}, bf16[2560,768]{1,0:T(8,128)(2,1)}, bf16[2560,288]{1,0:T(8,128)(2,1)}, bf16[768,5120]{1,0:T(8,128)(2,1)}, b...) custom-call(bf16[320,2560]{1,0:T(8,128)(2,1)} %refs_0_.1, ...), custom_call_target="tpu_custom_call" | custom-call | tf_op jit(solution)/shard_map/pallas_call | solution.py:1188
  171.4 2.9 multiply_reduce_fusion.5
  179.7 7.7 fusion.61.proj
  188.3 3.9 convolution_convert_fusion.kv.refs_6_
  193.0 22.9 %shard_map.255 = (bf16[128,5120]{1,0:T(8,128)(2,1)}, bf16[128,2560]{1,0:T(8,128)(2,1)}, f32[128,128]{1,0:T(8,128)}) custom-call(f32[128,5120]{1,0:T(8,128)} %fusion.61.proj, bf16[512,5120]{1,0:T(8,128)(2,1)} %convolution_convert_fusion.kv.refs_6_, bf16[512,128]{1,0:T(8,128)(2,1)} %select_maximum_fusion.rope.refs_7_, f32[128,512]{1,0:T(8,128)} %and_select_fusion.bias.refs_8_, ...), custom_call_target="tpu_custom_call" | custom-call | tf_op jit(solution)/shard_map/pallas_call | solution.py:179
  215.9 7.0 multiply_reduce_fusion.2
  223.9 55.3 %shard_map.256 = (bf16[1024,2560]{1,0:T(8,128)(2,1)}, bf16[2560,896]{1,0:T(8,128)(2,1)}, f32[1024,896]{1,0:T(8,128)}) custom-call(bf16[128,2560]{1,0:T(8,128)(2,1)} %multiply_convert_fusion.3.tokens, bf16[2560,896]{1,0:T(8,128)(2,1)} %get-tuple-element.60.partial, bf16[1024,2560]{1,0:T(8,128)(2,1)} %get-tuple-element.61.grad, ...), custom_call_target="tpu_custom_call", output_to_operand_aliasing={{1}: (1, {})} | custom-call | tf_op jit(solution)/shard_map/pallas_call | solution.py:489
  279.3 7.6 fusion.65
  286.9 8.3 multiply_convert_fusion
  295.2 8.2 fusion.66
  303.4 7.4 convolution_convert_fusion.5
  312.0 10.2 %convolution_convert_fusion.6.refs_1_ = bf16[896,2560]{1,0:T(8,128)(2,1)} fusion(bf16[1024,896]{1,0:T(8,128)(2,1)} %get-tuple-element.142, bf16[1024,2560]{1,0:T(8,128)(2,1)} %get-tuple-element.61.grad), kind=kOutput, calls=%fused_computation.8 | convolution fusion | flops 4699914240 | bytes 11665408 | tf_op jit(solution)/shard_map/dot_general | solution.py:58
  322.2 9.7 %convolution_convert_fusion.3 = bf16[1024,2560]{1,0:T(8,128)(2,1)} fusion(bf16[1024,896]{1,0:T(8,128)(2,1)S(1)} %copy-done.48, bf16[896,2560]{1,0:T(8,128)(2,1)} %copy-done.1), kind=kOutput, calls=%fused_computation.4 | convolution fusion | flops 4700241920 | bytes 11665408 | tf_op jit(solution)/shard_map/dot_general | solution.py:1301
  331.9 7.3 convolution_convert_fusion.4
  339.3 9.9 %add_convert_fusion = bf16[1024,2560]{1,0:T(8,128)(2,1)} fusion(f32[1024,2560]{1,0:T(8,128)} %fusion.66, bf16[1024,896]{1,0:T(8,128)(2,1)S(1)} %copy-done.49, bf16[2560,896]{1,0:T(8,128)(2,1)S(1)} %bitcast.138), kind=kOutput, calls=%fused_computation | convolution fusion | flops 4702863360 | bytes 22151168 | tf_op jit(solution)/shard_map/dot_general | solution.py:64
  349.2 79.4 %shard_map.257 = (f32[128,2560]{1,0:T(8,128)}, bf16[800,640]{1,0:T(8,128)(2,1)}, bf16[8,80,896]{2,1,0:T(8,128)(2,1)}) custom-call(bf16[8,128,2560]{2,1,0:T(8,128)(2,1)} %bitcast.135, bf16[896,2560]{1,0:T(8,128)(2,1)} %convolution_convert_fusion.6.refs_1_, bf16[8,4,80,896]{3,2,1,0:T(8,128)(2,1)} %bitcast.140), custom_call_target="tpu_custom_call" | custom-call | tf_op jit(solution)/shard_map/pallas_call | solution.py:687
  431.1 2.5 copy.69
  433.6 9.9 %convolution_convert_fusion.8.refs_11_ = bf16[128,2560]{1,0:T(8,128)(2,1)} fusion(bf16[128,2560]{1,0:T(8,128)(2,1)S(1)} %multiply_convert_fusion.2.refs_0_, bf16[2560,2560]{1,0:T(8,128)(2,1)} %get-tuple-element.59), kind=kOutput, calls=%fused_computation.20 | convolution fusion | flops 1678049280 | bytes 14417920 | tf_op jit(solution)/shard_map/dot_general | solution.py:64
  445.0 105.3 %shard_map.258 = (bf16[1024,2560]{1,0:T(8,128)(2,1)}, bf16[8,2,128,320]{3,2,1,0:T(8,128)(2,1)}, f32[128,2560]{1,0:T(8,128)}, bf16[800,2560]{1,0:T(8,128)(2,1)}, ...) custom-call(bf16[128,2560]{1,0:T(8,128)(2,1)} %copy-done.6, ...), custom_call_target="tpu_custom_call" | custom-call | tf_op jit(solution)/shard_map/pallas_call | solution.py:763
  550.3 4.2 convolution_convert_fusion.10
  554.5 3.1 convolution_convert_fusion.2
  557.6 2.8 multiply_reduce_fusion.3
  565.9 4.6 convolution_convert_fusion.1
  570.6 3.1 convolution_convert_fusion.7.refs_0_
  575.3 6.7 convert_element_type.202
  586.7 138.7 %shard_map.259 = (bf16[1024,1056]{1,0:T(8,128)(2,1)}, bf16[8,4,80,896]{3,2,1,0:T(8,128)(2,1)}, bf16[8,4,80,896]{3,2,1,0:T(8,128)(2,1)}, f32[96,1024]{1,0:T(8,128)}, f32[32,5120]{1,0:T(8,128)}) custom-call(bf16[128,1056]{1,0:T(8,128)(2,1)} %pad_maximum_fusion.2.lat, bf16[8,80,896]{2,1,0:T(8,128)(2,1)} %get-tuple-element.76.gate, ...), custom_call_target="tpu_custom_call" | custom-call | tf_op jit(solution)/shard_map/pallas_call | solution.py:846
  728.1 3.6 convolution_convert_fusion.9
  731.7 74.8 %shard_map.260 = (bf16[320,2560]{1,0:T(8,128)(2,1)}, bf16[4,80,1056]{2,1,0:T(8,128)(2,1)}, bf16[32,5120]{1,0:T(8,128)(2,1)}, bf16[96,4096]{1,0:T(8,128)(2,1)}, f32[8,128]{1,0:T(8,128)}) custom-call(bf16[320,2560]{1,0:T(8,128)(2,1)} %convolution_convert_fusion.7.refs_0_, bf16[4,80,1056]{2,1,0:T(8,128)(2,1)} %bitcast.145, ...), custom_call_target="tpu_custom_call" | custom-call | tf_op jit(solution)/shard_map/pallas_call | solution.py:936
  816.0 2.8 copy.75
  820.7 3.5 convert_element_type.201
  824.2 10.8 %shard_map.261 = (f32[320,6400]{1,0:T(8,128)}, f32[320,6400]{1,0:T(8,128)}) custom-call(bf16[8,4,80,896]{3,2,1,0:T(8,128)(2,1)} %get-tuple-element.87.refs_0_, bf16[8,4,80,896]{3,2,1,0:T(8,128)(2,1)} %get-tuple-element.88.refs_1_), custom_call_target="tpu_custom_call" | custom-call | tf_op jit(solution)/shard_map/pallas_call | solution.py:254
  (233 shorter events, 54.4 us)
Async XLA Ops:
  8.1 155.4 %copy-start = (bf16[1,128,2560]{2,1,0:T(8,128)(2,1)S(1)}, bf16[1,128,2560]{2,1,0:T(8,128)(2,1)}, u32[]{:S(2)}) copy-start(bf16[1,128,2560]{2,1,0:T(8,128)(2,1)} %param.15) | copy-start | bytes 1966084
  8.1 155.8 %copy-start.47 = (s32[1,4]{1,0:T(1,128)S(1)}, s32[1,4]{1,0:T(1,128)}, u32[]{:S(2)}) copy-start(s32[1,4]{1,0:T(1,128)} %param.17) | copy-start | bytes 52
  163.4 7.8 copy-start.33
  167.6 20.6 %collective-permute-start.2 = (bf16[128,288]{1,0:T(8,128)(2,1)S(1)}, bf16[128,288]{1,0:T(8,128)(2,1)S(1)}, u32[]{:S(2)}, u32[]{:S(2)}) collective-permute-start(bf16[128,288]{1,0:T(8,128)(2,1)S(1)} %pad_maximum_fusion.5), channel_id=1, source_target_pairs={{0,24},{8,16},{16,8},{24,0},{1,25},{9,17},{17,9},{25,1},{2,26},{10... | collective-permute-start | bytes 221192 | tf_op jit(solution)/shard_map/ppermute | solution.py:1197
  169.2 19.1 %collective-permute-start.1 = (bf16[128,288]{1,0:T(8,128)(2,1)S(1)}, bf16[128,288]{1,0:T(8,128)(2,1)S(1)}, u32[]{:S(2)}, u32[]{:S(2)}) collective-permute-start(bf16[128,288]{1,0:T(8,128)(2,1)S(1)} %pad_maximum_fusion.5), channel_id=1, source_target_pairs={{0,16},{8,24},{16,0},{24,8},{1,17},{9,25},{17,1},{25,9},{2,18},{10... | collective-permute-start | bytes 221192 | tf_op jit(solution)/shard_map/ppermute | solution.py:1197
  169.7 18.6 %collective-permute-start = (bf16[128,288]{1,0:T(8,128)(2,1)S(1)}, bf16[128,288]{1,0:T(8,128)(2,1)S(1)}, u32[]{:S(2)}, u32[]{:S(2)}) collective-permute-start(bf16[128,288]{1,0:T(8,128)(2,1)S(1)} %pad_maximum_fusion.5), channel_id=1, source_target_pairs={{0,8},{8,0},{16,24},{24,16},{1,9},{9,1},{17,25},{25,17},{2,10},{10... | collective-permute-start | bytes 221192 | tf_op jit(solution)/shard_map/ppermute | solution.py:1197
  179.6 7.7 copy-start.1
  179.7 8.7 %copy-start.18 = (bf16[256,5120]{1,0:T(8,128)(2,1)S(1)}, bf16[256,5120]{1,0:T(8,128)(2,1)}, u32[]{:S(2)}) copy-start(bf16[256,5120]{1,0:T(8,128)(2,1)} %get-tuple-element.57) | copy-start | bytes 7864324
  222.9 56.3 %slice-start.10 = ((s8[4587520]{0:T(1024)(128)(4,1)}), s8[4194304]{0:T(1024)(128)(4,1)S(1)}, s32[]{:S(2)}) async-start(s8[4587520]{0:T(1024)(128)(4,1)} %bitcast.164), calls=%async_computation.10 | async-start | bytes 8388608
  223.9 55.3 %slice-start.11 = ((s8[4587520]{0:T(1024)(128)(4,1)}), s8[393216]{0:T(1024)(128)(4,1)S(1)}, s32[]{:S(2)}) async-start(s8[4587520]{0:T(1024)(128)(4,1)} %bitcast.164), calls=%async_computation.11 | async-start | bytes 786432
  279.2 7.7 copy-start.12
  311.9 10.2 %copy-start.48 = (bf16[1024,896]{1,0:T(8,128)(2,1)S(1)}, bf16[1024,896]{1,0:T(8,128)(2,1)}, u32[]{:S(2)}) copy-start(bf16[1024,896]{1,0:T(8,128)(2,1)} %get-tuple-element.142) | copy-start | bytes 5505028
  311.9 19.9 %slice-start.8 = ((s8[5242880]{0:T(1024)(128)(4,1)}), s8[4194304]{0:T(1024)(128)(4,1)S(1)}, s32[]{:S(2)}) async-start(s8[5242880]{0:T(1024)(128)(4,1)} %bitcast.162), calls=%async_computation.8 | async-start | bytes 8388608
  322.2 9.7 %slice-start.9 = ((s8[5242880]{0:T(1024)(128)(4,1)}), s8[1048576]{0:T(1024)(128)(4,1)S(1)}, s32[]{:S(2)}) async-start(s8[5242880]{0:T(1024)(128)(4,1)} %bitcast.162), calls=%async_computation.9 | async-start | bytes 2097152
  322.2 9.7 %copy-start.49 = (bf16[1024,896]{1,0:T(8,128)(2,1)S(1)}, bf16[1024,896]{1,0:T(8,128)(2,1)}, u32[]{:S(2)}) copy-start(bf16[1024,896]{1,0:T(8,128)(2,1)} %get-tuple-element.144) | copy-start | bytes 5505028
  322.2 17.1 %slice-start.3 = ((s8[4587520]{0:T(1024)(128)(4,1)}), s8[4194304]{0:T(1024)(128)(4,1)S(1)}, s32[]{:S(2)}) async-start(s8[4587520]{0:T(1024)(128)(4,1)} %bitcast.137), calls=%async_computation.3 | async-start | bytes 8388608
  431.1 12.4 %copy-start.6 = (bf16[128,2560]{1,0:T(8,128)(2,1)}, bf16[128,2560]{1,0:T(8,128)(2,1)S(1)}, u32[]{:S(2)}) copy-start(bf16[128,2560]{1,0:T(8,128)(2,1)S(1)} %multiply_convert_fusion.2.refs_0_) | copy-start | bytes 1966084
  433.6 9.9 %copy-start.15 = (bf16[1,128,8,320]{3,1,0,2:T(8,128)(2,1)S(1)}, bf16[1,128,8,320]{3,1,0,2:T(8,128)(2,1)}, u32[]{:S(2)}) copy-start(bf16[1,128,8,320]{3,1,0,2:T(8,128)(2,1)} %copy.70) | copy-start | bytes 1966084
  433.6 9.9 %copy-start.16 = (bf16[1,128,8,320]{3,1,0,2:T(8,128)(2,1)S(1)}, bf16[1,128,8,320]{3,1,0,2:T(8,128)(2,1)}, u32[]{:S(2)}) copy-start(bf16[1,128,8,320]{3,1,0,2:T(8,128)(2,1)} %copy.69) | copy-start | bytes 1966084
  445.0 105.3 %copy-start.19 = (bf16[256,5120]{1,0:T(8,128)(2,1)S(1)}, bf16[256,5120]{1,0:T(8,128)(2,1)}, u32[]{:S(2)}) copy-start(bf16[256,5120]{1,0:T(8,128)(2,1)} %get-tuple-element.57) | copy-start | bytes 7864324
  560.6 9.9 %copy-start.26 = (bf16[512,32]{1,0:T(8,128)(2,1)}, bf16[512,32]{1,0:T(8,128)(2,1)S(1)}, u32[]{:S(2)}) copy-start(bf16[512,32]{1,0:T(8,128)(2,1)S(1)} %slice.167) | copy-start | bytes 98308
  561.3 20.6 %collective-permute-start.5 = (bf16[128,288]{1,0:T(8,128)(2,1)}, bf16[128,288]{1,0:T(8,128)(2,1)}, u32[]{:S(2)}, u32[]{:S(2)}) collective-permute-start(bf16[128,288]{1,0:T(8,128)(2,1)} %get-tuple-element.150), channel_id=1, source_target_pairs={{0,24},{8,16},{16,8},{24,0},{1,25},{9,17},{17,9},{25,1},{2,26},{10... | collective-permute-start | bytes 221192 | tf_op jit(solution)/shard_map/ppermute | solution.py:1197
  562.8 19.2 %collective-permute-start.4 = (bf16[128,288]{1,0:T(8,128)(2,1)}, bf16[128,288]{1,0:T(8,128)(2,1)}, u32[]{:S(2)}, u32[]{:S(2)}) collective-permute-start(bf16[128,288]{1,0:T(8,128)(2,1)} %get-tuple-element.151), channel_id=1, source_target_pairs={{0,16},{8,24},{16,0},{24,8},{1,17},{9,25},{17,1},{25,9},{2,18},{10... | collective-permute-start | bytes 221192 | tf_op jit(solution)/shard_map/ppermute | solution.py:1197
  563.8 18.2 %collective-permute-start.3 = (bf16[128,288]{1,0:T(8,128)(2,1)}, bf16[128,288]{1,0:T(8,128)(2,1)}, u32[]{:S(2)}, u32[]{:S(2)}) collective-permute-start(bf16[128,288]{1,0:T(8,128)(2,1)} %get-tuple-element.149), channel_id=1, source_target_pairs={{0,8},{8,0},{16,24},{24,16},{1,9},{9,1},{17,25},{25,17},{2,10},{10... | collective-permute-start | bytes 221192 | tf_op jit(solution)/shard_map/ppermute | solution.py:1197
  575.3 8.2 copy-start.21
  575.3 8.4 %copy-start.40 = (f32[128]{0:T(128)S(1)}, f32[128]{0:T(128)}, u32[]{:S(2)}) copy-start(f32[128]{0:T(128)} %copy-done.39) | copy-start | bytes 1540
  586.7 141.4 %copy-start.17 = (bf16[8,1,128,320]{3,2,1,0:T(8,128)(2,1)S(1)}, bf16[8,1,128,320]{3,2,1,0:T(8,128)(2,1)}, u32[]{:S(2)}) copy-start(bf16[8,1,128,320]{3,2,1,0:T(8,128)(2,1)} %get-tuple-element.145) | copy-start | bytes 1966084
  824.2 10.9 %copy-start.4 = (f32[128,2560]{1,0:T(8,128)S(1)}, f32[128,2560]{1,0:T(8,128)}, u32[]{:S(2)}) copy-start(f32[128,2560]{1,0:T(8,128)} %get-tuple-element.66) | copy-start | bytes 3932164
  824.2 10.9 %copy-start.9 = (bf16[1,128,2560]{2,1,0:T(8,128)(2,1)S(1)}, bf16[1,128,2560]{2,1,0:T(8,128)(2,1)}, u32[]{:S(2)}) copy-start(bf16[1,128,2560]{2,1,0:T(8,128)(2,1)} %param.16) | copy-start | bytes 1966084
  824.2 10.9 %copy-start.11 = (f32[128,2560]{1,0:T(8,128)S(1)}, f32[128,2560]{1,0:T(8,128)}, u32[]{:S(2)}) copy-start(f32[128,2560]{1,0:T(8,128)} %get-tuple-element.173) | copy-start | bytes 3932164
  824.2 10.9 %copy-start.24 = (f32[128,2560]{1,0:T(8,128)S(1)}, f32[128,2560]{1,0:T(8,128)}, u32[]{:S(2)}) copy-start(f32[128,2560]{1,0:T(8,128)} %get-tuple-element.70) | copy-start | bytes 3932164
  824.2 10.9 %copy-start.36 = (f32[128]{0:T(128)S(1)}, f32[128]{0:T(128)}, u32[]{:S(2)}) copy-start(f32[128]{0:T(128)} %copy-done.35) | copy-start | bytes 1540
  (36 other events, 139.9 us)

commit v3 on v2

--- a/solution.py
+++ b/solution.py
@@ -153,25 +153,24 @@
     first = lane < 64
     logs[...] = jnp.zeros_like(logs)
 
-    def one(h):
-        q = turn(proj[:, head_tile(h)], (turns[0], turns[1], turns[2])).astype(low)
-        query[:, head_tile(h)] = q
-        keyval = kv[:, head_tile(h)]
-        key = jnp.where(first, keyval, rope[...])
-        scores = dot_nt(q, key) * scale + bias[...]
-        top = jnp.max(scores, axis=1, keepdims=True)
-        grown = jnp.exp(scores - top)
-        total = jnp.sum(grown, axis=1, keepdims=True)
-        probs = (grown / total).astype(low)
-        logs[...] = jnp.where(lane == h, top + jnp.log(total), logs[...])
-        return jnp.dot(probs, keyval, preferred_element_type=jnp.float32)
-
-    def pair(i, carry):
-        even, odd = one(2 * i), one(2 * i + 1)
-        mixed[:, head_tile(i)] = jnp.where(first, pltpu.roll(even, 64, 1), odd).astype(low)
+    def group(i, carry):
+        heads_here = [4 * i + j for j in range(4)]
+        queries = [turn(proj[:, head_tile(h)], (turns[0], turns[1], turns[2])).astype(low) for h in heads_here]
+        keyvals = [kv[:, head_tile(h)] for h in heads_here]
+        scores = [dot_nt(q, jnp.where(first, keyval, rope[...])) * scale + bias[...] for q, keyval in zip(queries, keyvals)]
+        tops = [jnp.max(s, axis=1, keepdims=True) for s in scores]
+        grown = [jnp.exp(s - top) for s, top in zip(scores, tops)]
+        totals = [jnp.sum(g, axis=1, keepdims=True) for g in grown]
+        outs = [jnp.dot((g / total).astype(low), keyval, preferred_element_type=jnp.float32)
+                for g, total, keyval in zip(grown, totals, keyvals)]
+        for h, q, top, total in zip(heads_here, queries, tops, totals):
+            query[:, head_tile(h)] = q
+            logs[...] = jnp.where(lane == h, top + jnp.log(total), logs[...])
+        for j in range(2):
+            mixed[:, head_tile(2 * i + j)] = jnp.where(first, pltpu.roll(outs[2 * j], 64, 1), outs[2 * j + 1]).astype(low)
         return carry
 
-    lax.fori_loop(0, heads // 2, pair, 0)
+    lax.fori_loop(0, heads // 4, group, 0)
 
 
 def attend(scale, proj, kv, rope, bias, turns):
@@ -248,6 +247,22 @@
             out[:, first_full * 128 : last * 128] = tiles[:, (first_full - base) * 128 : (last - base) * 128]
 
 
+def unpack_kernel(heads, packed, out):
+    pieces = []
+    for h in range(heads):
+        first, k = h // 10 * 1024, h % 10
+        pieces.append(packed[:, first + 64 * k : first + 64 * k + 64])
+        pieces.append(packed[:, first + 640 + 32 * k : first + 672 + 32 * k])
+    out[...] = jnp.concatenate(pieces, axis=1).astype(jnp.float32)
+
+
+def unpack(packed, heads):
+    return pl.pallas_call(
+        functools.partial(unpack_kernel, heads),
+        out_shape=jax.ShapeDtypeStruct((packed.shape[0], heads * 96), jnp.float32), in_specs=[VMEM], out_specs=VMEM,
+    )(packed)
+
+
 def widen(arrays, cols):
     _, quarters, rows, strip = arrays[0].shape
     n = len(arrays)
@@ -349,25 +364,25 @@
 class Total:
     def __init__(self, term, out, bufs, sems):
         self.term, self.out = term, out
-        self.mine, self.theirs, self.stage, self.landed = bufs
-        self.zsend, self.zrecv, self.csend, self.crecv, self.own = sems
+        self.theirs, self.landed = bufs
+        self.zsend, self.zrecv, self.csend, self.crecv = sems
         self.rep, self.zpos, self.core = place()
 
     @staticmethod
     def scratch(term):
-        four = pltpu.VMEM((4,) + term.shape[1:], term.dtype)
-        return [four] * 3 + [pltpu.VMEM((2, 4) + term.shape[1:], term.dtype),
-                             dma_sems(2, 4), dma_sems(2, 4), dma_sems(4), dma_sems(4), dma_sems(4)]
+        return [pltpu.VMEM((4,) + term.shape[1:], term.dtype), pltpu.VMEM((5,) + term.shape[1:], term.dtype),
+                dma_sems(2, 4), dma_sems(2, 4), dma_sems(4), dma_sems(4)]
+
+    @staticmethod
+    def split(term, out, refs):
+        return Total(term, out, refs[:2], refs[2:6]), refs[6:]
 
     def pair_copy(self, z):
         return remote(self.term.at[z * 2 + 1 - self.core], self.theirs.at[z], self.csend.at[z], self.crecv.at[z],
                       self.rep, self.zpos * 2 + 1 - self.core)
 
-    def load(self, z):
-        return pltpu.make_async_copy(self.term.at[z * 2 + self.core], self.mine.at[z], self.own.at[z])
-
     def hop_copy(self, way, z):
-        return remote(self.stage.at[z], self.landed.at[way, z], self.zsend.at[way, z], self.zrecv.at[way, z],
+        return remote(self.theirs.at[z], self.landed.at[z + 1 - way], self.zsend.at[way, z], self.zrecv.at[way, z],
                       self.rep, (self.zpos + (1 - 2 * way)) * 2 + self.core)
 
     def each(self, step):
@@ -379,38 +394,37 @@
     def start(self):
         for z in (3, 0, 2, 1):
             self.pair_copy(z).start()
-            self.load(z).start()
 
     def pair(self):
         for z in (3, 0, 2, 1):
-            self.load(z).wait()
             self.pair_copy(z).wait_recv()
 
+    def both(self, z):
+        return self.term[z * 2 + self.core].astype(jnp.float32) + self.theirs[z].astype(jnp.float32)
+
     def step(self, step):
-        wide = jnp.float32
         for way, behind, target, there in self.each(step):
             @pl.when(there)
             def _():
-                total = self.mine[target].astype(wide) + self.theirs[target].astype(wide)
+                total = self.both(target)
 
                 @pl.when(behind == 0)
                 def _():
-                    self.stage[target] = total.astype(self.stage.dtype)
+                    self.theirs[target] = total.astype(self.theirs.dtype)
 
                 @pl.when(behind > 0)
                 def _():
                     self.hop_copy(way, target).wait_recv()
-                    self.stage[target] = (total + self.landed[way, target].astype(wide)).astype(self.stage.dtype)
+                    self.theirs[target] = (total + self.landed[target + 1 - way].astype(jnp.float32)).astype(self.theirs.dtype)
                 self.hop_copy(way, target).start()
 
     def finish(self):
-        wide = jnp.float32
-        self.out[...] = self.mine[self.zpos].astype(wide) + self.theirs[self.zpos].astype(wide)
+        self.out[...] = self.both(self.zpos)
         for way in range(2):
             @pl.when(self.zpos > 0 if way == 0 else self.zpos < 3)
             def _():
                 self.hop_copy(way, self.zpos).wait_recv()
-                self.out[...] += self.landed[way, self.zpos].astype(wide)
+                self.out[...] += self.landed[self.zpos + 1 - way].astype(jnp.float32)
         for step in range(3):
             for way, behind, target, there in self.each(step):
                 @pl.when(there)
@@ -425,24 +439,6 @@
 
 
 VMEM = pl.BlockSpec(memory_space=pltpu.VMEM)
-
-
-def chain_gather_kernel(n, *refs):
-    gather = Gather(refs[:n], refs[n : 2 * n], refs[2 * n :])
-    greet(*place())
-    gather.start()
-    for hop in range(1, 4):
-        gather.hop(hop)
-    gather.finish()
-
-
-def chain_gather(cid, *arrays):
-    n = len(arrays)
-    out = [jax.ShapeDtypeStruct((a.shape[0] * 8,) + a.shape[1:], a.dtype) for a in arrays]
-    return pl.pallas_call(
-        functools.partial(chain_gather_kernel, n), out_shape=out, in_specs=[ANY] * n, out_specs=[ANY] * n,
-        scratch_shapes=Gather.scratch(n), compiler_params=kernel_params(cid),
-    )(*arrays)
 
 
 def ffn_gather_kernel(tokens, partial, grad, down, tokens_all, up, grad_hidden, *scratch):
@@ -649,13 +645,14 @@
 
 
 def back_kernel(shift_unit, *refs):
-    term, down, gate, out, down_own, gate_own = refs[:6]
-    scratch = list(refs[6:])
+    down, tokens, grad_gate, grad_up, gate_w, up_w, out, down_own, gate_own, up = refs[:10]
+    term, gate, strips, strip_sems = refs[10:14]
     rep, zpos, core = place()
-    total = Total(term, out, scratch[:4], scratch[4:9])
-    bufs, sems, _ = PlaneSum.split(scratch[9:], 4)
+    total, rest = Total.split(term, out, refs[14:])
+    bufs, sems, _ = PlaneSum.split(rest, 4)
     half = down_own.shape[0] // 2
     shift = mult((zpos * 2 + core) % 4 * shift_unit, 16)
+    wide = jnp.float32
 
     def down_item(h):
         return (lambda p: quarter_cols(down, mult(shift + h * half, 16), half, p), down_own.at[pl.ds(h * half, half)], h)
@@ -664,220 +661,283 @@
         return (lambda p: gate.at[pl.ds(4 * h, 4), p], gate_own.at[pl.ds(4 * h, 4)], h)
 
     sums = PlaneSum([down_item(0), down_item(1), gate_item(0), gate_item(1)], bufs, sems)
+    chunk = strips.shape[2]
+    chunks = gate_w.shape[0] // chunk
+
+    def strip(i, which):
+        return pltpu.make_async_copy(
+            (gate_w, up_w)[which].at[pl.ds(mult(i * chunk, 128), chunk)], strips.at[i % 2, which], strip_sems.at[i % 2, which])
+
+    for which in range(2):
+        strip(0, which).start()
     greet(rep, zpos, core, plane=2)
+    sums.start((0, 1))
+
+    def back(i, carry):
+        for which in range(2):
+            strip(i, which).wait()
+
+        @pl.when(i < chunks - 1)
+        def _():
+            for which in range(2):
+                strip(i + 1, which).start()
+
+        part = dot_nt(grad_gate[...], strips[i % 2, 0]) + dot_nt(grad_up[...], strips[i % 2, 1])
+        term[:, :, pl.ds(mult(i * chunk, 128), chunk)] = part.astype(term.dtype).reshape(8, -1, chunk)
+        return carry
+
+    lax.fori_loop(0, chunks, back, 0)
     total.start()
-    sums.start()
-    total.pair()
-    total.step(0)
-    sums.middle(0)
-    sums.middle(1)
-    total.step(1)
+    wide_rows = tokens.shape[1] // 4
+
+    def weight(grad, to, i):
+        got = dot_tn(tokens[:, pl.ds(mult(i * wide_rows, 128), wide_rows)], grad[...])
+        to[pl.ds(2 * i, 2)] = got.astype(to.dtype).reshape((2,) + to.shape[1:])
+
+    def gate_step(i, carry):
+        weight(grad_gate, gate, i)
+
+        @pl.when(i == 2)
+        def _():
+            total.pair()
+            total.step(0)
+        return carry
+
+    lax.fori_loop(0, 4, gate_step, 0)
+    sums.start((2, 3))
+
+    def up_step(i, carry):
+        weight(grad_up, up, i)
+
+        @pl.when(i == 1)
+        def _():
+            sums.middle(0)
+            sums.middle(1)
+            total.step(1)
+        return carry
+
+    lax.fori_loop(0, 4, up_step, 0)
+    sums.end(0)
+    sums.end(1)
+    total.step(2)
     sums.middle(2)
     sums.middle(3)
-    total.step(2)
-    for i in range(4):
-        sums.end(i)
     total.finish()
+    sums.end(2)
+    sums.end(3)
     sums.finish()
 
 
-def back_sums(cid, term, down, gate, rows):
+def back_sums(cid, down, tokens, grad_gate, grad_up, gate_w, up_w, rows):
     width = down.shape[1] // 4
     kind = down.dtype
+    strip = gate_w.shape[1]
+    parts = (8, 4, gate_w.shape[0] // 32, strip)
+    term = jax.ShapeDtypeStruct((8, tokens.shape[0] // 8, tokens.shape[1]), kind)
     return pl.pallas_call(
         functools.partial(back_kernel, rows % 128),
         out_shape=[jax.ShapeDtypeStruct(term.shape[1:], jnp.float32), jax.ShapeDtypeStruct((rows, width), kind),
-                   jax.ShapeDtypeStruct((8,) + gate.shape[2:], kind)],
-        in_specs=[ANY, VMEM, VMEM], out_specs=[VMEM] * 3,
-        scratch_shapes=Total.scratch(term) + PlaneSum.scratch([(rows // 2, width)] * 2 + [(4,) + gate.shape[2:]] * 2, kind),
+                   jax.ShapeDtypeStruct((8,) + parts[2:], kind), jax.ShapeDtypeStruct(parts, kind)],
+        in_specs=[VMEM] * 4 + [ANY] * 2, out_specs=[VMEM] * 4,
+        scratch_shapes=[pltpu.VMEM(term.shape, kind), pltpu.VMEM(parts, kind),
+                        pltpu.VMEM((2, 2, gate_w.shape[0] // 5, strip), kind), dma_sems(2, 2)]
+        + Total.scratch(term) + PlaneSum.scratch([(rows // 2, width)] * 2 + [(4,) + parts[2:]] * 2, kind),
         compiler_params=kernel_params(cid),
-    )(term, down, gate)
+    )(down, tokens, grad_gate, grad_up, gate_w, up_w)
 
 
 def middle_kernel(scale, *refs):
-    branch, cols, term, down, up = refs[:5]
-    attend_in = refs[5:12]
-    branch_all, cols_all, out, down_all, up_own = refs[12:17]
-    attend_out = refs[17:21]
-    scratch = list(refs[21:])
-    left, scratch = scratch[0], scratch[1:]
+    branch, cols, down, up, attn_out, query_low, latent_low = refs[:7]
+    query, kv, rope, bias, turns, logs = refs[7:13]
+    branch_all, cols_all, down_all, up_own = refs[13:17]
+    grad_query, grad_kv, grad_rope, query_up, latent_up = refs[17:22]
+    scratch = list(refs[22:])
+    left, mixed, packed, strips, strip_sems = scratch[:5]
+    scratch = scratch[5:]
     rep, zpos, core = place()
+    shard = zpos * 2 + core
     gather = Gather((branch,), (branch_all,), scratch[:5])
-    total = Total(term, out, scratch[5:9], scratch[9:14])
-    swap = ColumnSwap([(lambda s: cols.at[s], lambda s: cols_all.at[s])], scratch[14:17])
+    swap = ColumnSwap([(lambda s: cols.at[s], lambda s: cols_all.at[s])], scratch[5:8])
     half = down.shape[0] // 2
     downs = PlaneGather(
         [(down.at[pl.ds(h * half, half)], functools.partial(quarter_cols, down_all, h * half, half), h) for h in range(2)],
-        scratch[17:20])
-    bufs, sems, _ = PlaneSum.split(scratch[20:], 2)
+        scratch[8:11])
+    bufs, sems, _ = PlaneSum.split(scratch[11:], 2)
     sums = PlaneSum([(lambda p, h=h: up.at[pl.ds(4 * h, 4), p], up_own.at[pl.ds(4 * h, 4)], h) for h in range(2)], bufs, sems)
+    rows = attn_out.shape[0] // 4
+
+    def strip(i):
+        return pltpu.make_async_copy(
+            attn_out.at[pl.ds(mult(i * rows, 128), rows)], strips.at[i % 2], strip_sems.at[i % 2])
+
+    strip(0).start()
     greet(rep, zpos, core, plane=2, column=True)
-    total.start()
     gather.start()
     sums.start()
     downs.start()
     swap.start()
     left[...] = jnp.zeros_like(left)
-    attend_out[3][...] = jnp.zeros_like(attend_out[3])
-    quarter = attend_back_heads(scale, *attend_in, *attend_out, left)
-
-    def after_first():
-        total.pair()
-        total.step(0)
+    grad_rope[...] = jnp.zeros_like(grad_rope)
+    quarter = attend_back_heads(
+        scale, query, kv, rope, bias, turns, logs, mixed, grad_query, packed, grad_kv, grad_rope, left)
 
     def after_second():
         gather.hop(1)
         sums.middle(0)
         sums.middle(1)
 
-    def after_third():
-        total.step(1)
+    def after_fourth():
+        gather.hop(2)
         downs.middle(0)
         downs.middle(1)
 
-    def after_fourth():
-        gather.hop(2)
-        total.step(2)
-
     def step(i, carry):
+        strip(i).wait()
+
+        @pl.when(i < 3)
+        def _():
+            strip(i + 1).start()
+
+        mixed[:, pl.ds(mult(i * rows, 128), rows)] = dot_nt(branch[...], strips[i % 2]).astype(mixed.dtype)
         quarter(i, carry)
-        for k, service in enumerate((after_first, after_second, after_third, after_fourth)):
-            pl.when(i == k)(service)
+        pl.when(i == 1)(after_second)
+        pl.when(i == 3)(after_fourth)
         return carry
 
     lax.fori_loop(0, 4, step, 0)
+
+    def terms(i, carry):
+        at = pl.ds(mult(i * 1024, 128), 1024)
+        query_up[:, at] = dot_tn(query_low[...], packed[:, at]).astype(query_up.dtype)
+        width = latent_up.shape[1] // 4
+        at = pl.ds(mult(i * width, 128), width)
+        latent_up[:, at] = dot_tn(latent_low[...], grad_kv[:, at]).astype(latent_up.dtype)
+        return carry
+
+    lax.fori_loop(0, 4, terms, 0)
     sums.end(0)
     sums.end(1)
     gather.hop(3)
-    total.finish()
     gather.finish()
     swap.finish()
     downs.finish()
     sums.finish()
 
 
-def middle_exchange(cid, scale, branch, cols, term, down, up, attend_in):
+def middle_exchange(cid, scale, branch, cols, down, up, attn_out, query_low, latent_low, attend_in):
     kind = branch.dtype
     query, kv, rope = attend_in[:3]
     rows = query.shape[0]
     return pl.pallas_call(
         functools.partial(middle_kernel, scale),
         out_shape=[jax.ShapeDtypeStruct((8 * branch.shape[0], branch.shape[1]), kind), jax.ShapeDtypeStruct(cols.shape, kind),
-                   jax.ShapeDtypeStruct(term.shape[1:], jnp.float32),
                    jax.ShapeDtypeStruct((down.shape[0], 4 * down.shape[1]), kind), jax.ShapeDtypeStruct((8,) + up.shape[2:], kind),
-                   jax.ShapeDtypeStruct(query.shape, kind), jax.ShapeDtypeStruct((rows, 4096), kind),
-                   jax.ShapeDtypeStruct(kv.shape, kind), jax.ShapeDtypeStruct(rope.shape, jnp.float32)],
-        in_specs=[ANY] * 4 + [VMEM] * 8, out_specs=[ANY, ANY, VMEM, ANY] + [VMEM] * 5,
-        scratch_shapes=[pltpu.VMEM((2 * rows, 256), kind)]
-        + Gather.scratch(1) + Total.scratch(term) + ColumnSwap.scratch(1) + PlaneGather.scratch(2)
+                   jax.ShapeDtypeStruct(query.shape, kind),
+                   jax.ShapeDtypeStruct(kv.shape, kind), jax.ShapeDtypeStruct(rope.shape, jnp.float32),
+                   jax.ShapeDtypeStruct((query_low.shape[1], 4096), kind),
+                   jax.ShapeDtypeStruct((latent_low.shape[1], kv.shape[1]), kind)],
+        in_specs=[VMEM] + [ANY] * 2 + [VMEM, ANY] + [VMEM] * 8, out_specs=[ANY] * 3 + [VMEM] * 6,
+        scratch_shapes=[pltpu.VMEM((2 * rows, 256), kind), pltpu.VMEM(branch.shape, kind), pltpu.VMEM((rows, 4096), kind),
+                        pltpu.VMEM((2, attn_out.shape[0] // 4, attn_out.shape[1]), kind), dma_sems(2)]
+        + Gather.scratch(1) + ColumnSwap.scratch(1) + PlaneGather.scratch(2)
         + PlaneSum.scratch([(4,) + up.shape[2:]] * 2, kind),
         compiler_params=kernel_params(cid),
-    )(branch, cols, term, down, up, *attend_in)
-
-
-def late_kernel(lat, gate, up, query_up, latent_up, lat_all, gate_all, up_all, query_sum, latent_sum, *scratch):
+    )(branch, cols, down, up, attn_out, query_low, latent_low, *attend_in)
+
+
+def latent_kernel(lat, query_up, latent_up, hidden, down, lat_all, query_part, latent_sum, out_term, *scratch):
     rep, zpos, core = place()
-    shard = zpos * 2 + core
     gather = Gather((lat,), (lat_all,), scratch[:5])
-    pairs = ((gate, gate_all), (up, up_all))
-    swap = ColumnSwap([(lambda s, a=a: a.at[s], lambda s, b=b: b.at[s, rep]) for a, b in pairs], scratch[5:8], keeps=False)
-
-    def part(m, b):
-        return lambda p: b.at[shard if m == 0 else column_place(zpos, core, m, True), p]
-
-    spread = PlaneGather(
-        [(a.at[shard] if m == 0 else None, part(m, b), h) for m in range(8) for h, (a, b) in enumerate(pairs)], scratch[8:11])
-    bufs, sems, rest = PlaneSum.split(scratch[11:], 2)
-    query_part = rest[0]
+    bufs, sems, rest = PlaneSum.split(scratch[5:], 2)
     width = query_up.shape[2] // 4
 
     def query_item(h):
         return (lambda p: query_up.at[pl.ds(4 * h, 4), :, pl.ds(mult(p * width, 128), width)], query_part.at[pl.ds(4 * h, 4)], h)
 
     sums = PlaneSum([query_item(0), query_item(1)], bufs, sems)
-    query_total = Total(query_part, query_sum, rest[1:5], rest[5:10])
-    latent_total = Total(latent_up, latent_sum, rest[10:14], rest[14:19])
-    greet(rep, zpos, core, plane=2, column=True)
+    latent_total, _ = Total.split(latent_up, latent_sum, rest)
+    greet(rep, zpos, core, plane=2)
     sums.start()
-    spread.start((0, 1))
-    swap.start()
     latent_total.start()
     gather.start()
-    near = ColumnSwap.near
-    for i, m in enumerate(near):
-        swap.arrive(m)
-        spread.start((2 * m, 2 * m + 1))
-        if i == 0:
-            sums.middle(0)
-            sums.middle(1)
-        before = 0 if i == 0 else near[i - 1]
-        spread.middle(2 * before)
-        spread.middle(2 * before + 1)
-        if i == 2:
-            latent_total.pair()
-            latent_total.step(0)
-            sums.end(0)
-            sums.end(1)
-            query_total.start()
-        if i in (1, 3, 5):
-            gather.hop((i + 1) // 2)
-        if i == 4:
-            latent_total.step(1)
-            query_total.pair()
-            query_total.step(0)
-        if i == 6:
-            latent_total.step(2)
-            query_total.step(1)
-    query_total.step(2)
-    spread.middle(2 * near[-1])
-    spread.middle(2 * near[-1] + 1)
+    rows = lat.shape[0]
+
+    def after_second():
+        latent_total.pair()
+        latent_total.step(0)
+
+    def after_fourth():
+        gather.hop(1)
+        latent_total.step(1)
+
+    def after_sixth():
+        gather.hop(2)
+        latent_total.step(2)
+
+    def step(i, carry):
+        out_term[i] = jnp.dot(hidden[pl.ds(mult(i * rows, rows), rows)], down[...],
+                              preferred_element_type=jnp.float32).astype(out_term.dtype)
+        pl.when(i == 1)(after_second)
+        pl.when(i == 3)(after_fourth)
+        pl.when(i == 5)(after_sixth)
+        return carry
+
+    lax.fori_loop(0, 8, step, 0)
+    sums.middle(0)
+    sums.middle(1)
+    gather.hop(3)
     latent_total.finish()
-    query_total.finish()
     gather.finish()
-    swap.finish(arrive=False)
-    spread.finish()
+    sums.end(0)
+    sums.end(1)
     sums.finish()
 
 
-def late_exchange(cid, lat, gate, up, query_up, latent_up):
-    kind = gate.dtype
+def latent_sums(cid, lat, query_up, latent_up, hidden, down):
+    kind = query_up.dtype
     part = jax.ShapeDtypeStruct((8, query_up.shape[1], query_up.shape[2] // 4), kind)
     half = (4,) + part.shape[1:]
     return pl.pallas_call(
-        late_kernel,
-        out_shape=[jax.ShapeDtypeStruct((8 * lat.shape[0], lat.shape[1]), lat.dtype)]
-        + [jax.ShapeDtypeStruct((8, 4) + gate.shape[1:], kind)] * 2
-        + [jax.ShapeDtypeStruct(part.shape[1:], jnp.float32), jax.ShapeDtypeStruct(latent_up.shape[1:], jnp.float32)],
-        in_specs=[ANY] * 3 + [VMEM, ANY], out_specs=[ANY] * 3 + [VMEM] * 2,
-        scratch_shapes=Gather.scratch(1) + ColumnSwap.scratch(2) + PlaneGather.scratch(16)
-        + PlaneSum.scratch([half] * 2, kind) + [pltpu.VMEM(part.shape, kind)] + Total.scratch(part) + Total.scratch(latent_up),
+        latent_kernel,
+        out_shape=[jax.ShapeDtypeStruct((8 * lat.shape[0], lat.shape[1]), lat.dtype), part,
+                   jax.ShapeDtypeStruct(latent_up.shape[1:], jnp.float32),
+                   jax.ShapeDtypeStruct((8, lat.shape[0], down.shape[1]), kind)],
+        in_specs=[ANY] + [VMEM] * 4, out_specs=[ANY] + [VMEM] * 3,
+        scratch_shapes=Gather.scratch(1) + PlaneSum.scratch([half] * 2, kind) + Total.scratch(latent_up),
         compiler_params=kernel_params(cid),
-    )(lat, gate, up, query_up, latent_up)
-
-
-def last_kernel(n, *refs):
-    terms, done, gain = refs[:n], refs[n], refs[n + 1]
-    outs, done_out, gain_out = refs[n + 2 : 2 * n + 2], refs[2 * n + 2], refs[2 * n + 3]
-    scratch = list(refs[2 * n + 4 :])
-    landed, sums = scratch[:n], scratch[n : 2 * n + 1]
-    gain_landed, gain_sum, gain_plane, ssend, srecv, tsend, trecv, gsend, grecv, hsend, hrecv = scratch[2 * n + 1 :]
+    )(lat, query_up, latent_up, hidden, down)
+
+
+def last_kernel(*refs):
+    gate, up, term, attn_out, lat, latent_up, query_up, gain = refs[:8]
+    gate_all, up_all, out, attn_sum, lat_sum, latent_sum, query_sum, gain_out = refs[8:16]
+    scratch = list(refs[16:])
     rep, zpos, core = place()
     shard = zpos * 2 + core
     places = plane_places(rep)
-    wide = jnp.float32
-    greet(rep, zpos, core, plane=3, column=True)
-
-    def quarter(ref, p):
-        if len(ref.shape) == 3:
-            return ref.at[p]
-        return quarter_cols(ref, 0, ref.shape[0], p)
-
-    def term_copy(a, k):
-        return remote(quarter(terms[a], places[k]), landed[a].at[k], ssend.at[k, a], srecv.at[k, a], places[k], shard)
-
-    def sum_copy(a, k, back=False):
-        out = quarter((*outs, done_out)[a], places[k] if back else rep)
-        return remote(sums[a], out, tsend.at[k, a], trecv.at[k, a], places[k], shard)
+    swap = ColumnSwap([(lambda s, a=a: a.at[s], lambda s, b=b: b.at[s, rep]) for a, b in ((gate, gate_all), (up, up_all))],
+                      scratch[:2] + [None], keeps=False)
+    spread_sems, scratch = scratch[2:5], scratch[5:]
+    total, scratch = Total.split(term, out, scratch)
+    owns = scratch[:5]
+    gain_landed, gain_sum, gain_plane, gsend, grecv, hsend, hrecv = scratch[5:12]
+    query_total, scratch = Total.split(query_up, scratch[12], scratch[13:])
+    bufs, sems, _ = PlaneSum.split(scratch, 4)
+
+    def part(m, b):
+        return lambda p: b.at[shard if m == 0 else column_place(zpos, core, m, True), p]
+
+    half = attn_out.shape[0] // 2
+    sums = PlaneSum(
+        [(functools.partial(quarter_cols, attn_out, h * half, half), owns[h], h) for h in range(2)]
+        + [(lambda p: lat.at[p], owns[2], 0), (functools.partial(quarter_cols, latent_up, 0, latent_up.shape[0]), owns[3], 1)],
+        bufs, sems)
+    spread = PlaneGather(
+        [(a.at[shard] if m == 0 else None, part(m, b), h) for m in range(8) for h, (a, b) in enumerate(((gate, gate_all), (up, up_all)))]
+        + [(owns[h], functools.partial(quarter_cols, attn_sum, h * half, half), h) for h in range(2)]
+        + [(owns[2], lambda p: lat_sum.at[p], 0),
+           (owns[3], functools.partial(quarter_cols, latent_sum, 0, latent_up.shape[0]), 1),
+           (owns[4], functools.partial(quarter_cols, query_sum, 0, query_up.shape[1]), 0)], spread_sems)
 
     def gain_copy(m):
         s2 = column_place(zpos, core, m)
@@ -886,60 +946,85 @@
     def gain_on(k):
         return remote(gain_sum, gain_plane.at[k], hsend.at[k], hrecv.at[k], places[k], shard)
 
-    def hand_on(a):
-        for k in range(3):
-            sum_copy(a, k).start()
-        quarter((*outs, done_out)[a], rep)[...] = sums[a][...]
-
+    greet(rep, zpos, core, plane=3, column=True)
     for m in range(1, 8):
         gain_copy(m).start()
-    for a in range(n):
-        for k in range(3):
-            term_copy(a, k).start()
-    sums[n][...] = done[...].astype(sums[n].dtype)
-    hand_on(n)
+    sums.start()
+    swap.start()
+    spread.start((0, 1))
+    query_total.start()
+    total.start()
     gain_sum[...] = gain[shard]
     for m in range(1, 8):
         gain_copy(m).wait_recv()
         gain_sum[...] += gain_landed[m - 1]
     for k in range(3):
         gain_on(k).start()
-    for a in range(n):
-        total = quarter(terms[a], rep)[...].astype(wide)
-        for k in range(3):
-            term_copy(a, k).wait_recv()
-            total = total + landed[a][k].astype(wide)
-        sums[a][...] = total.astype(jnp.bfloat16)
-        hand_on(a)
+    near = ColumnSwap.near
+    for i, m in enumerate(near):
+        swap.arrive(m)
+        spread.start((2 * m, 2 * m + 1))
+        if i in (1, 2):
+            for k in range(2):
+                sums.middle(2 * i - 2 + k)
+        if i == 1:
+            query_total.pair()
+        if i in (1, 2, 3):
+            query_total.step(i - 1)
+        if i == 4:
+            query_total.finish()
+            owns[4][...] = query_total.out[...].astype(owns[4].dtype)
+            spread.start((20,))
+        before = 0 if i == 0 else near[i - 1]
+        spread.middle(2 * before)
+        spread.middle(2 * before + 1)
+        if i == 3:
+            total.pair()
+            total.step(0)
+        if i in (3, 4):
+            for k in range(2):
+                sums.end(2 * i - 6 + k)
+                spread.start((2 * i + 10 + k,))
+    total.step(1)
+    for i in (2 * near[-1], 2 * near[-1] + 1, 20, 16, 17):
+        spread.middle(i)
+    total.step(2)
+    for i in (18, 19):
+        spread.middle(i)
     gain_out[...] = gain_sum[...]
     for k in range(3):
         gain_on(k).wait_recv()
         gain_out[...] += gain_plane[k]
     for k in range(3):
         gain_on(k).wait_send()
-        for a in range(n + 1):
-            if a < n:
-                term_copy(a, k).wait_send()
-            sum_copy(a, k).wait_send()
-            sum_copy(a, k, True).wait_recv()
     for m in range(1, 8):
         gain_copy(m).wait_send()
-
-
-def last_sums(cid, terms, done, gain):
-    n = len(terms)
-    low = jnp.bfloat16
-    out = [jax.ShapeDtypeStruct(t.shape, low) for t in terms]
-    out += [jax.ShapeDtypeStruct((done.shape[0], 4 * done.shape[1]), low), jax.ShapeDtypeStruct(gain.shape[1:], gain.dtype)]
-    cut = [t.shape[1:] if len(t.shape) == 3 else (t.shape[0], t.shape[1] // 4) for t in terms]
+    total.finish()
+    swap.finish(arrive=False)
+    sums.finish()
+    spread.finish()
+
+
+def last_sums(cid, gate, up, term, attn_out, lat, latent_up, query_up, gain):
+    kind = gate.dtype
+    shapes = [(attn_out.shape[0] // 2, attn_out.shape[1] // 4)] * 2 + [
+        lat.shape[1:], (latent_up.shape[0], latent_up.shape[1] // 4)]
     block = pltpu.VMEM(gain.shape[1:], gain.dtype)
     return pl.pallas_call(
-        functools.partial(last_kernel, n), out_shape=out, in_specs=[VMEM] * (n + 2), out_specs=[VMEM] * (n + 2),
-        scratch_shapes=[pltpu.VMEM((3,) + c, low) for c in cut] + [pltpu.VMEM(c, low) for c in cut] + [pltpu.VMEM(done.shape, low)]
+        last_kernel,
+        out_shape=[jax.ShapeDtypeStruct((8, 4) + gate.shape[1:], kind)] * 2
+        + [jax.ShapeDtypeStruct(term.shape[1:], jnp.float32)]
+        + [jax.ShapeDtypeStruct(a.shape, kind) for a in (attn_out, lat, latent_up)]
+        + [jax.ShapeDtypeStruct((query_up.shape[1], 4 * query_up.shape[2]), kind), jax.ShapeDtypeStruct(gain.shape[1:], gain.dtype)],
+        in_specs=[ANY] * 2 + [VMEM] * 6, out_specs=[ANY] * 2 + [VMEM] + [ANY] * 4 + [VMEM],
+        scratch_shapes=[dma_sems(7, 2), dma_sems(7, 2)] + PlaneGather.scratch(21) + Total.scratch(term)
+        + [pltpu.VMEM(s, kind) for s in shapes + [query_up.shape[1:]]]
         + [pltpu.VMEM((7,) + gain.shape[1:], gain.dtype), block, pltpu.VMEM((3,) + gain.shape[1:], gain.dtype)]
-        + [dma_sems(3, n + 1)] * 4 + [dma_sems(7)] * 2 + [dma_sems(3)] * 2,
+        + [dma_sems(7)] * 2 + [dma_sems(3)] * 2 + [pltpu.VMEM(query_up.shape[1:], jnp.float32)] + Total.scratch(query_up)
+        + PlaneSum.scratch(shapes, kind),
         compiler_params=kernel_params(cid),
-    )(*terms, done, gain)
+    )(gate, up, term, attn_out, lat, latent_up, query_up, gain)
+
 
 def start_kernel(*refs):
     ins, (gate, up) = refs[:7], refs[7:9]
@@ -1297,41 +1382,37 @@
     grad_gate_f, grad_up_f = act_back(grad_hidden)
     grad_gate = grad_gate_f.astype(low)
     grad_up = grad_up_f.astype(low)
-    ffn_in_part = (outer_cols(grad_gate, gate_w) + outer_cols(grad_up, up_w)).astype(low)
-    out_part = jnp.dot(hidden_low, down_w, preferred_element_type=wide).astype(low)
     down_part = inner_rows(hidden_low, gd_all).astype(low)
-    gate_part = inner_rows(ffn_all, grad_gate).astype(low).reshape(8, 4, -1, strip)
-    up_part = inner_rows(ffn_all, grad_up).astype(low).reshape(8, 4, -1, strip)
-    grad_ffn_in, down_own, gate_own = back_sums(
-        2, ffn_in_part.reshape(8, rows, width), down_part, gate_part, slice_ff
+    grad_ffn_in, down_own, gate_own, up_part = back_sums(
+        2, down_part, ffn_all, grad_gate, grad_up, gate_w, up_w, slice_ff
     )
 
     grad_res_norm, grad_gain_ffn = norm_f_back(grad_ffn_in)
     grad_resid = grad_out + grad_res_norm
     grad_branch = (residual_scale * grad_resid).astype(low)
-    grad_mixed = outer_cols(grad_branch, aout).astype(low)
     cols = jnp.stack([mixed_low, normed_low]).reshape(2, rows, 8, width // 8).transpose(2, 0, 1, 3)
     (
         branch_all,
         cols_all,
-        out_sum,
         down_all,
         up_own,
         grad_q_proj,
-        grad_q_packed,
         grad_kv,
         grad_rope,
+        qup_part,
+        lup_part,
     ) = middle_exchange(
         3,
         scale,
         grad_branch,
         cols,
-        out_part.reshape(8, rows, width),
         down_own,
         up_part,
-        (queries, keyvals, rope_tile, bias, turns, logs, grad_mixed),
-    )
-    layer_out = (residual + residual_scale * out_sum).astype(low)
+        aout,
+        query_low,
+        latent_low,
+        (queries, keyvals, rope_tile, bias, turns, logs),
+    )
     down_grad = down_all.astype(wide)
     rope_sum = grad_rope[:, ND:head_dim]
     grad_lat_part = jnp.concatenate([outer_cols(grad_kv, lup), rope_sum], axis=1).astype(low)
@@ -1349,14 +1430,15 @@
     grad_in_norm, grad_gain_attn = norm_in_back(grad_normed)
     tokens_grad = (grad_resid + grad_in_norm).astype(low)
 
-    qup_part = inner_rows(query_low, grad_q_packed).astype(low)
-    lup_part = inner_rows(latent_low, grad_kv).astype(low)
     grad_lats = jnp.concatenate([grad_q_lat, grad_lat], axis=1)
-    lat_all, gate_all, up_all, qup_sum, lup_sum = late_exchange(
-        4, grad_lats, gate_own, up_own,
-        qup_part.reshape(8, -1, qup_part.shape[1]), lup_part.reshape(8, -1, lup_part.shape[1]),
-    )
-    gate_grad, up_grad = widen((gate_all, up_all), FF)
+    lat_all, qup_own, lup_sum, out_part = latent_sums(
+        4,
+        grad_lats,
+        qup_part.reshape(8, -1, qup_part.shape[1]),
+        lup_part.reshape(8, -1, lup_part.shape[1]),
+        hidden_low,
+        down_w,
+    )
     mixed_cols = cols_all[:, 0].reshape(8 * rows, width // 8)
     normed_cols = cols_all[:, 1].reshape(8 * rows, width // 8)
     aout_part = inner_rows(mixed_cols, branch_all).astype(low)
@@ -1369,21 +1451,23 @@
         + [jnp.zeros((8, 1024 - 768), wide)],
         axis=1,
     ).reshape(8, 8, 128)
-    aout_own, lat_own, lup_own, qup_own, gain_own = last_sums(
-        5, (aout_part, lat_part.reshape(4, 80, -1), lup_sum.astype(low)), qup_sum, gains
-    )
+    gate_all, up_all, out_sum, aout_own, lat_own, lup_own, qup_own, gain_own = last_sums(
+        5,
+        gate_own,
+        up_own,
+        out_part,
+        aout_part,
+        lat_part.reshape(4, 80, -1),
+        lup_sum.astype(low),
+        qup_own,
+        gains,
+    )
+    layer_out = (residual + residual_scale * out_sum).astype(low)
+    gate_grad, up_grad = widen((gate_all, up_all), FF)
     aout_own = aout_own.astype(wide)
     lat_own = lat_own.reshape(320, -1).astype(wide)
     lup_own = lup_own.astype(wide)
-    qup_own = qup_own.reshape(-1, 4, 1024)
-    quarter_heads = H // 4
-    qup_own = jnp.concatenate(
-        [
-            qup_own[:, :, : quarter_heads * ND].reshape(-1, H, ND),
-            qup_own[:, :, quarter_heads * ND : quarter_heads * head_dim].reshape(-1, H, RD),
-        ],
-        axis=-1,
-    ).reshape(-1, H * head_dim).astype(wide)
+    qup_own = unpack(qup_own, H)
     gain_own = gain_own.reshape(1024)
 
     return (

time: 842 us -> 760 us (0.903)
  matrix products: 127 us -> 65.1 us
  Pallas kernels: 642 us -> 624 us
    dot_general x7 -> x4, matrix products: 38.4 us -> 10.2 us  [outer_cols(): lax.dot_general(leading, trailing, (((1,), (1,)), ((), ())), preferred_el...]
    dot_general x7 -> x3, matrix products: 39.3 us -> 13.3 us  [inner_rows(): lax.dot_general(leading, trailing, (((0,), (0,)), ((), ())), preferred_el...]
    pallas_call x1, Pallas kernels: 105 us -> 95.2 us  [middle_exchange(): pl.pallas_call(functools.partial(middle_kernel, scale), out_shape=[jax.Sh...]
    dot_general x1 -> x0, matrix products: 9.73 us -> none  [column_body(): jnp.dot(hidden_low, down_w, preferred_element_type=wide).astype(low)]
    pallas_call x1, Pallas kernels: 22.9 us -> 14.3 us  [attend(): pl.pallas_call(functools.partial(attend_kernel, scale), out_shape=[jax.Sh...]
    pallas_call x2 -> x3, Pallas kernels: 214 us -> 207 us  [the longest x1 143 us: last_sums(): pl.pallas_call(last_kernel, out_shape=[jax.ShapeDtypeStruct((8, 4) + gate...]
where the time goes in v3:
time: 760 us; the launch traced here: 756 us
  Pallas kernels  624 us (82%)
  matrix products  65.1 us (9%)
  other arithmetic  32.8 us (4%)
  local copies, waits for them, and re-layouts  24.9 us (3%)
    pallas_call x1, Pallas kernels, start_gather(): pl.pallas_call(start_kernel, out_shape=out, in_specs=[ANY] * 9, out_specs...  155 us
    pallas_call x1, Pallas kernels, last_sums(): pl.pallas_call(last_kernel, out_shape=[jax.ShapeDtypeStruct((8, 4) + gate...  143 us
    pallas_call x1, Pallas kernels, middle_exchange(): pl.pallas_call(functools.partial(middle_kernel, scale), out_shape=[jax.Sh...  95.2 us
    pallas_call x1, Pallas kernels, back_sums(): pl.pallas_call(functools.partial(back_kernel, rows % 128), out_shape=[jax...  87.7 us
    pallas_call x1, Pallas kernels, latent_sums(): pl.pallas_call(latent_kernel, out_shape=[jax.ShapeDtypeStruct((8 * lat.sh...  62.3 us
    pallas_call x1, Pallas kernels, ffn_gather(): pl.pallas_call(ffn_gather_kernel, out_shape=[jax.ShapeDtypeStruct((8 * to...  54.3 us
  transfers between devices with their start and end apart: 6, of which 0 were waited for; matrix products, arithmetic and copies ran while one was open for 4% of the time, Pallas kernels for 0%

profile of v3, /device:TPU:0, one launch (start us, length us, event | category | flops | bytes accessed | tf_op | source)
XLA Modules:
  0.0 755.8 jit_solution(3956161516716582448)
XLA Ops:
  0.7 2.6 reshape.205
  7.2 154.5 %shard_map.254 = (bf16[2560,2560]{1,0:T(8,128)(2,1)}, bf16[2560,768]{1,0:T(8,128)(2,1)}, bf16[2560,288]{1,0:T(8,128)(2,1)}, bf16[768,5120]{1,0:T(8,128)(2,1)}, b...) custom-call(bf16[320,2560]{1,0:T(8,128)(2,1)} %refs_0_.1, ...), custom_call_target="tpu_custom_call" | custom-call | tf_op jit(solution)/shard_map/pallas_call | solution.py:1273
  163.6 2.1 fusion.24
  173.5 2.9 multiply_reduce_fusion.5
  179.3 6.0 fusion.63.proj
  185.6 1.9 copy-done.11
  191.4 3.9 convolution_convert_fusion.kv.refs_8_
  195.3 1.7 select_maximum_fusion.rope.refs_9_
  197.0 14.3 %shard_map.255 = (bf16[128,5120]{1,0:T(8,128)(2,1)}, bf16[128,2560]{1,0:T(8,128)(2,1)}, f32[128,128]{1,0:T(8,128)}) custom-call(f32[128,5120]{1,0:T(8,128)} %fusion.63.proj, bf16[512,5120]{1,0:T(8,128)(2,1)} %convolution_convert_fusion.kv.refs_8_, bf16[512,128]{1,0:T(8,128)(2,1)} %select_maximum_fusion.rope.refs_9_, ...), custom_call_target="tpu_custom_call" | custom-call | tf_op jit(solution)/shard_map/pallas_call | solution.py:178
  211.3 2.2 copy.62
  213.5 2.2 copy.64
  215.8 6.7 multiply_reduce_fusion.2
  223.7 54.3 %shard_map.256 = (bf16[1024,2560]{1,0:T(8,128)(2,1)}, bf16[2560,896]{1,0:T(8,128)(2,1)}, f32[1024,896]{1,0:T(8,128)}) custom-call(bf16[128,2560]{1,0:T(8,128)(2,1)} %multiply_convert_fusion.3.tokens, bf16[2560,896]{1,0:T(8,128)(2,1)} %get-tuple-element.63.partial, bf16[1024,2560]{1,0:T(8,128)(2,1)} %get-tuple-element.64.grad, ...), custom_call_target="tpu_custom_call", output_to_operand_aliasing={{1}: (1, {})} | custom-call | tf_op jit(solution)/shard_map/pallas_call | solution.py:485
  278.0 9.0 %fusion.64 = f32[1024,896]{1,0:T(8,128)S(1)} fusion(bf16[1024,2560]{1,0:T(8,128)(2,1)} %get-tuple-element.65.refs_1_, bf16[2560,896]{1,0:T(8,128)(2,1)} %get-tuple-element.67.refs_5_), kind=kOutput, calls=%fused_computation.147 | convolution fusion | flops 4697620480 | bytes 13500416 | tf_op jit(solution)/shard_map/dot_general | solution.py:1379
  287.1 10.9 %multiply_convert_fusion = (bf16[1024,896]{1,0:T(8,128)(2,1)}, bf16[1024,896]{1,0:T(8,128)(2,1)}, bf16[1024,896]{1,0:T(8,128)(2,1)S(1)}) fusion(f32[1024,896]{1,0:T(8,128)S(1)} %copy-done.55, f32[1024,896]{1,0:T(8,128)S(1)} %fusion.64, bf16[1024,2560]{1,0:T(8,128)(2,1)S(1)} %copy-done.10, bf16[2560,896]{1,0:T(8,128)(2,1)} %get-tuple-element.66.refs_4_), kind=kOutput, calls=%fused_computation.9 | convolution fusion | flops 4712300544 | bytes 22675456 | tf_op jit(solution)/shard_map/dot_general | solution.py:1378
  298.0 6.6 convolution_convert_fusion.1.refs_0_
  304.6 87.7 %shard_map.257 = (f32[128,2560]{1,0:T(8,128)}, bf16[800,640]{1,0:T(8,128)(2,1)}, bf16[8,80,896]{2,1,0:T(8,128)(2,1)}, bf16[8,4,80,896]{3,2,1,0:T(8,128)(2,1)}) custom-call(bf16[896,2560]{1,0:T(8,128)(2,1)} %convolution_convert_fusion.1.refs_0_, bf16[1024,2560]{1,0:T(8,128)(2,1)} %get-tuple-element.65.refs_1_, bf16[1024,896]{1,0:T(8,128)(2,1)} %get-tuple-element.107.refs_2_, ...), custom_call_target="tpu_custom_call" | custom-call | tf_op jit(solution)/shard_map/pallas_call | solution.py:737
  392.4 1.8 multiply_reduce_fusion
  397.1 95.2 %shard_map.258 = (bf16[1024,2560]{1,0:T(8,128)(2,1)}, bf16[8,2,128,320]{3,2,1,0:T(8,128)(2,1)}, bf16[800,2560]{1,0:T(8,128)(2,1)}, bf16[8,80,896]{2,1,0:T(8,128)...) custom-call(bf16[128,2560]{1,0:T(8,128)(2,1)} %multiply_convert_fusi, ...), custom_call_target="tpu_custom_call" | custom-call | tf_op jit(solution)/shard_map/pallas_call | solution.py:831
  492.3 5.0 convolution_convert_fusion.4
  498.3 1.8 collective-permute-start.4
  501.8 2.8 multiply_reduce_fusion.3
  505.8 3.1 convolution_convert_fusion.2.refs_3_
  510.6 6.8 convert_element_type.166
  521.8 62.3 %shard_map.259 = (bf16[1024,1056]{1,0:T(8,128)(2,1)}, bf16[8,96,1024]{2,1,0:T(8,128)(2,1)}, f32[32,5120]{1,0:T(8,128)}, bf16[8,128,2560]{2,1,0:T(8,128)(2,1)}) custom-call(bf16[128,1056]{1,0:T(8,128)(2,1)} %pad_maximum_fusion.1.lat, bf16[8,96,4096]{2,1,0:T(8,128)(2,1)} %bitcast.110, bf16[8,32,5120]{2,1,0:T(8,128)(2,1)} %bitcast.119, ...), custom_call_target="tpu_custom_call" | custom-call | tf_op jit(solution)/shard_map/pallas_call | solution.py:900
  584.1 1.8 convert_element_type.159.refs_5_
  585.9 3.6 convolution_convert_fusion.3
  589.5 142.6 %shard_map.260 = (bf16[8,4,80,896]{3,2,1,0:T(8,128)(2,1)}, bf16[8,4,80,896]{3,2,1,0:T(8,128)(2,1)}, f32[128,2560]{1,0:T(8,128)}, bf16[320,2560]{1,0:T(8,128)(2,1...) custom-call(bf16[8,80,896]{2,1,0:T(8,128)(2,1)} %get-tuple-element.69., ...), custom_call_target="tpu_custom_call" | custom-call | tf_op jit(solution)/shard_map/pallas_call | solution.py:1013
  736.1 2.1 convert_element_type.165
  739.2 2.6 shard_map.261
  742.7 10.8 %shard_map.262 = (f32[320,6400]{1,0:T(8,128)}, f32[320,6400]{1,0:T(8,128)}) custom-call(bf16[8,4,80,896]{3,2,1,0:T(8,128)(2,1)} %get-tuple-element.93.refs_0_, bf16[8,4,80,896]{3,2,1,0:T(8,128)(2,1)} %get-tuple-element.94.refs_1_), custom_call_target="tpu_custom_call" | custom-call | tf_op jit(solution)/shard_map/pallas_call | solution.py:269
  753.6 2.1 fusion.21
  (225 shorter events, 40.0 us)
Async XLA Ops:
  0.7 165.2 %copy-start.37 = (f32[16]{0:T(128)}, f32[16]{0:T(128)S(1)}, u32[]{:S(2)}) copy-start(f32[16]{0:T(128)S(1)} %negate_power_fusion) | copy-start | bytes 196
  7.2 155.5 %copy-start.3 = (bf16[1,128,2560]{2,1,0:T(8,128)(2,1)S(1)}, bf16[1,128,2560]{2,1,0:T(8,128)(2,1)}, u32[]{:S(2)}) copy-start(bf16[1,128,2560]{2,1,0:T(8,128)(2,1)} %param.15) | copy-start | bytes 1966084
  7.2 155.8 %copy-start.56 = (s32[1,4]{1,0:T(1,128)S(1)}, s32[1,4]{1,0:T(1,128)}, u32[]{:S(2)}) copy-start(s32[1,4]{1,0:T(1,128)} %param.17) | copy-start | bytes 52
  162.5 8.8 %copy-start.34 = (f32[8,1024]{1,0:T(8,128)}, f32[8,1024]{1,0:T(8,128)S(1)}, u32[]{:S(2)}) copy-start(f32[8,1024]{1,0:T(8,128)S(1)} %reshape.208) | copy-start | bytes 98308
  167.7 21.5 %collective-permute-start = (bf16[128,288]{1,0:T(8,128)(2,1)}, bf16[128,288]{1,0:T(8,128)(2,1)}, u32[]{:S(2)}, u32[]{:S(2)}) collective-permute-start(bf16[128,288]{1,0:T(8,128)(2,1)} %pad_maximum_fusion.4), channel_id=1, source_target_pairs={{0,8},{8,0},{16,24},{24,16},{1,9},{9,1},{17,25},{25,17},{2,10},{10... | collective-permute-start | bytes 221192 | tf_op jit(solution)/shard_map/ppermute | solution.py:1282
  168.3 20.9 %collective-permute-start.1 = (bf16[128,288]{1,0:T(8,128)(2,1)}, bf16[128,288]{1,0:T(8,128)(2,1)}, u32[]{:S(2)}, u32[]{:S(2)}) collective-permute-start(bf16[128,288]{1,0:T(8,128)(2,1)} %pad_maximum_fusion.4), channel_id=1, source_target_pairs={{0,16},{8,24},{16,0},{24,8},{1,17},{9,25},{17,1},{25,9},{2,18},{10... | collective-permute-start | bytes 221192 | tf_op jit(solution)/shard_map/ppermute | solution.py:1282
  169.8 19.4 %collective-permute-start.2 = (bf16[128,288]{1,0:T(8,128)(2,1)}, bf16[128,288]{1,0:T(8,128)(2,1)}, u32[]{:S(2)}, u32[]{:S(2)}) collective-permute-start(bf16[128,288]{1,0:T(8,128)(2,1)} %pad_maximum_fusion.4), channel_id=1, source_target_pairs={{0,24},{8,16},{16,8},{24,0},{1,25},{9,17},{17,9},{25,1},{2,26},{10... | collective-permute-start | bytes 221192 | tf_op jit(solution)/shard_map/ppermute | solution.py:1282
  176.5 8.8 %copy-start.47 = (f32[128]{0:T(128)}, f32[128]{0:T(128)S(1)}, u32[]{:S(2)}) copy-start(f32[128]{0:T(128)S(1)} %get-tuple-element.132) | copy-start | bytes 1540
  188.0 7.3 copy-start
  222.5 171.7 %copy-start.1 = (f32[128,2560]{1,0:T(8,128)}, f32[128,2560]{1,0:T(8,128)S(1)}, u32[]{:S(2)}) copy-start(f32[128,2560]{1,0:T(8,128)S(1)} %get-tuple-element.135) | copy-start | bytes 3932164
  278.0 9.0 %copy-start.10 = (bf16[1024,2560]{1,0:T(8,128)(2,1)S(1)}, bf16[1024,2560]{1,0:T(8,128)(2,1)}, u32[]{:S(2)}) copy-start(bf16[1024,2560]{1,0:T(8,128)(2,1)} %get-tuple-element.65.refs_1_) | copy-start | bytes 15728644
  278.0 9.0 %copy-start.55 = (f32[1024,896]{1,0:T(8,128)S(1)}, f32[1024,896]{1,0:T(8,128)}, u32[]{:S(2)}) copy-start(f32[1024,896]{1,0:T(8,128)} %get-tuple-element.68) | copy-start | bytes 11010052
  278.0 20.0 %slice-start.2 = ((s8[5242880]{0:T(1024)(128)(4,1)}), s8[4194304]{0:T(1024)(128)(4,1)S(1)}, s32[]{:S(2)}) async-start(s8[5242880]{0:T(1024)(128)(4,1)} %bitcast.111), calls=%async_computation.2 | async-start | bytes 8388608
  287.1 11.0 %slice-start.3 = ((s8[5242880]{0:T(1024)(128)(4,1)}), s8[1048576]{0:T(1024)(128)(4,1)S(1)}, s32[]{:S(2)}) async-start(s8[5242880]{0:T(1024)(128)(4,1)} %bitcast.111), calls=%async_computation.3 | async-start | bytes 2097152
  395.7 106.0 %slice-start = ((s8[7864320]{0:T(1024)(128)(4,1)}), s8[4194304]{0:T(1024)(128)(4,1)S(1)}, s32[]{:S(2)}) async-start(s8[7864320]{0:T(1024)(128)(4,1)} %bitcast.108), calls=%async_computation | async-start | bytes 8388608
  397.1 104.6 %slice-start.1 = ((s8[7864320]{0:T(1024)(128)(4,1)}), s8[3670016]{0:T(1024)(128)(4,1)S(1)}, s32[]{:S(2)}) async-start(s8[7864320]{0:T(1024)(128)(4,1)} %bitcast.108), calls=%async_computation.1 | async-start | bytes 7340032
  492.3 9.4 %copy-start.24 = (bf16[128,5120]{1,0:T(8,128)(2,1)S(1)}, bf16[128,5120]{1,0:T(8,128)(2,1)}, u32[]{:S(2)}) copy-start(bf16[128,5120]{1,0:T(8,128)(2,1)} %get-tuple-element.76) | copy-start | bytes 3932164
  497.5 8.3 %slice-start.5 = ((s8[5242880]{0:T(1024)(128)(4,1)}), s8[4194304]{0:T(1024)(128)(4,1)S(1)}, s32[]{:S(2)}) async-start(s8[5242880]{0:T(1024)(128)(4,1)} %bitcast.129), calls=%async_computation.5 | async-start | bytes 8388608
  498.2 19.1 %collective-permute-start.3 = (bf16[128,288]{1,0:T(8,128)(2,1)}, bf16[128,288]{1,0:T(8,128)(2,1)}, u32[]{:S(2)}, u32[]{:S(2)}) collective-permute-start(bf16[128,288]{1,0:T(8,128)(2,1)} %get-tuple-element.113), channel_id=1, source_target_pairs={{0,8},{8,0},{16,24},{24,16},{1,9},{9,1},{17,25},{25,17},{2,10},{10... | collective-permute-start | bytes 221192 | tf_op jit(solution)/shard_map/ppermute | solution.py:1282
  498.3 19.1 %collective-permute-start.4 = (bf16[128,288]{1,0:T(8,128)(2,1)}, bf16[128,288]{1,0:T(8,128)(2,1)}, u32[]{:S(2)}, u32[]{:S(2)}) collective-permute-start(bf16[128,288]{1,0:T(8,128)(2,1)} %get-tuple-element.115), channel_id=1, source_target_pairs={{0,16},{8,24},{16,0},{24,8},{1,17},{9,25},{17,1},{25,9},{2,18},{10... | collective-permute-start | bytes 221192 | tf_op jit(solution)/shard_map/ppermute | solution.py:1282
  500.1 17.3 %collective-permute-start.5 = (bf16[128,288]{1,0:T(8,128)(2,1)}, bf16[128,288]{1,0:T(8,128)(2,1)}, u32[]{:S(2)}, u32[]{:S(2)}) collective-permute-start(bf16[128,288]{1,0:T(8,128)(2,1)} %get-tuple-element.114), channel_id=1, source_target_pairs={{0,24},{8,16},{16,8},{24,0},{1,25},{9,17},{17,9},{25,1},{2,26},{10... | collective-permute-start | bytes 221192 | tf_op jit(solution)/shard_map/ppermute | solution.py:1282
  510.5 7.9 %copy-start.18 = (f32[128,288]{1,0:T(8,128)S(1)}, f32[128,288]{1,0:T(8,128)}, u32[]{:S(2)}) copy-start(f32[128,288]{1,0:T(8,128)} %copy-done.17) | copy-start | bytes 442372
  510.5 8.1 %copy-start.38 = (f32[16]{0:T(128)S(1)}, f32[16]{0:T(128)}, u32[]{:S(2)}) copy-start(f32[16]{0:T(128)} %copy-done.37) | copy-start | bytes 196
  510.5 8.1 %copy-start.40 = (f32[128]{0:T(128)S(1)}, f32[128]{0:T(128)}, u32[]{:S(2)}) copy-start(f32[128]{0:T(128)} %copy-done.39) | copy-start | bytes 1540
  510.5 8.4 %copy-start.46 = (f32[128]{0:T(128)S(1)}, f32[128]{0:T(128)}, u32[]{:S(2)}) copy-start(f32[128]{0:T(128)} %copy-done.45) | copy-start | bytes 1540
  510.5 9.4 %copy-start.19 = (bf16[2560,288]{1,0:T(8,128)(2,1)S(1)}, bf16[2560,288]{1,0:T(8,128)(2,1)}, u32[]{:S(2)}) copy-start(bf16[2560,288]{1,0:T(8,128)(2,1)} %get-tuple-element.59) | copy-start | bytes 4423684
  521.8 64.2 %copy-start.14 = (bf16[8,1,128,320]{3,2,1,0:T(8,128)(2,1)S(1)}, bf16[8,1,128,320]{3,2,1,0:T(8,128)(2,1)}, u32[]{:S(2)}) copy-start(bf16[8,1,128,320]{3,2,1,0:T(8,128)(2,1)} %get-tuple-element.109) | copy-start | bytes 1966084
  742.7 10.9 %copy-start.2 = (f32[128,2560]{1,0:T(8,128)S(1)}, f32[128,2560]{1,0:T(8,128)}, u32[]{:S(2)}) copy-start(f32[128,2560]{1,0:T(8,128)} %copy-done.1) | copy-start | bytes 3932164
  742.7 10.9 %copy-start.7 = (f32[128,2560]{1,0:T(8,128)S(1)}, f32[128,2560]{1,0:T(8,128)}, u32[]{:S(2)}) copy-start(f32[128,2560]{1,0:T(8,128)} %get-tuple-element.70) | copy-start | bytes 3932164
  742.7 10.9 %copy-start.9 = (bf16[1,128,2560]{2,1,0:T(8,128)(2,1)S(1)}, bf16[1,128,2560]{2,1,0:T(8,128)(2,1)}, u32[]{:S(2)}) copy-start(bf16[1,128,2560]{2,1,0:T(8,128)(2,1)} %param.16) | copy-start | bytes 1966084
  742.7 10.9 %copy-start.23 = (f32[128,2560]{1,0:T(8,128)S(1)}, f32[128,2560]{1,0:T(8,128)}, u32[]{:S(2)}) copy-start(f32[128,2560]{1,0:T(8,128)} %get-tuple-element.87) | copy-start | bytes 3932164
  742.7 10.9 %copy-start.42 = (f32[128]{0:T(128)S(1)}, f32[128]{0:T(128)}, u32[]{:S(2)}) copy-start(f32[128]{0:T(128)} %copy-done.41) | copy-start | bytes 1540
  (38 other events, 124.5 us)

commit v4 on v3

--- a/solution.py
+++ b/solution.py
@@ -146,12 +146,10 @@
     return lax.dot_general(a, b, (((0,), (0,)), ((), ())), preferred_element_type=jnp.float32)
 
 
-def attend_kernel(scale, proj, kv, rope, bias, turns, query, mixed, logs):
+def attend_heads(scale, proj, kv, rope, bias, turns, query, mixed, logs):
     low = jnp.bfloat16
-    heads = kv.shape[1] // 128
     lane = lax.broadcasted_iota(jnp.int32, (1, 128), 1)
     first = lane < 64
-    logs[...] = jnp.zeros_like(logs)
 
     def group(i, carry):
         heads_here = [4 * i + j for j in range(4)]
@@ -170,18 +168,7 @@
             mixed[:, head_tile(2 * i + j)] = jnp.where(first, pltpu.roll(outs[2 * j], 64, 1), outs[2 * j + 1]).astype(low)
         return carry
 
-    lax.fori_loop(0, heads // 4, group, 0)
-
-
-def attend(scale, proj, kv, rope, bias, turns):
-    rows, cols = proj.shape
-    return pl.pallas_call(
-        functools.partial(attend_kernel, scale),
-        out_shape=[jax.ShapeDtypeStruct((rows, cols), jnp.bfloat16), jax.ShapeDtypeStruct((rows, cols // 2), jnp.bfloat16),
-                   jax.ShapeDtypeStruct((rows, 128), jnp.float32)],
-        in_specs=[VMEM] * 5, out_specs=[VMEM] * 3,
-        compiler_params=pltpu.CompilerParams(vmem_limit_bytes=56 * 2**20),
-    )(proj, kv, rope, bias, turns)
+    return group
 
 
 def attend_back_heads(scale, query, kv, rope, bias, turns, logs, grad, grad_query, grad_packed, grad_kv, grad_rope, left):
@@ -441,58 +428,6 @@
 VMEM = pl.BlockSpec(memory_space=pltpu.VMEM)
 
 
-def ffn_gather_kernel(tokens, partial, grad, down, tokens_all, up, grad_hidden, *scratch):
-    del partial
-    rep, zpos, core = place()
-    gather = Gather((tokens,), (tokens_all,), scratch[:5])
-    piece = up.shape[0] // 32
-
-    def part(m):
-        first = column_place(zpos, core, m, True) * (4 * piece)
-        return lambda p: up.at[pl.ds(mult(first + p * piece, 16), piece)]
-
-    spread = PlaneGather([(None, part(m), m % 2) for m in ColumnSwap.near], scratch[5:8])
-    greet(rep, zpos, core, plane=2)
-    gather.start()
-    spread.start()
-    chunk = grad.shape[0] // 4
-
-    def product(i):
-        at = pl.ds(mult(i * chunk, chunk), chunk)
-        grad_hidden[at] = dot_nt(grad[at], down[...])
-
-    def step(i, carry):
-        product(i)
-
-        @pl.when(i == 1)
-        def _():
-            gather.hop(1)
-
-        @pl.when(i == 3)
-        def _():
-            gather.hop(2)
-        return carry
-
-    lax.fori_loop(0, 4, step, 0)
-    for i in range(7):
-        spread.middle(i)
-    gather.hop(3)
-    gather.finish()
-    spread.finish()
-
-
-def ffn_gather(cid, tokens, partial, grad, down):
-    return pl.pallas_call(
-        ffn_gather_kernel,
-        out_shape=[jax.ShapeDtypeStruct((8 * tokens.shape[0], tokens.shape[1]), tokens.dtype),
-                   jax.ShapeDtypeStruct(partial.shape, partial.dtype),
-                   jax.ShapeDtypeStruct((grad.shape[0], down.shape[0]), jnp.float32)],
-        in_specs=[ANY, ANY, VMEM, VMEM], out_specs=[ANY, ANY, VMEM], input_output_aliases={1: 1},
-        scratch_shapes=Gather.scratch(1) + PlaneGather.scratch(7),
-        compiler_params=kernel_params(cid),
-    )(tokens, partial, grad, down)
-
-
 class PlaneSum:
     def __init__(self, items, bufs, sems):
         self.items = items
@@ -845,98 +780,51 @@
     )(branch, cols, down, up, attn_out, query_low, latent_low, *attend_in)
 
 
-def latent_kernel(lat, query_up, latent_up, hidden, down, lat_all, query_part, latent_sum, out_term, *scratch):
-    rep, zpos, core = place()
-    gather = Gather((lat,), (lat_all,), scratch[:5])
-    bufs, sems, rest = PlaneSum.split(scratch[5:], 2)
-    width = query_up.shape[2] // 4
-
-    def query_item(h):
-        return (lambda p: query_up.at[pl.ds(4 * h, 4), :, pl.ds(mult(p * width, 128), width)], query_part.at[pl.ds(4 * h, 4)], h)
-
-    sums = PlaneSum([query_item(0), query_item(1)], bufs, sems)
-    latent_total, _ = Total.split(latent_up, latent_sum, rest)
-    greet(rep, zpos, core, plane=2)
-    sums.start()
-    latent_total.start()
-    gather.start()
-    rows = lat.shape[0]
-
-    def after_second():
-        latent_total.pair()
-        latent_total.step(0)
-
-    def after_fourth():
-        gather.hop(1)
-        latent_total.step(1)
-
-    def after_sixth():
-        gather.hop(2)
-        latent_total.step(2)
-
-    def step(i, carry):
-        out_term[i] = jnp.dot(hidden[pl.ds(mult(i * rows, rows), rows)], down[...],
-                              preferred_element_type=jnp.float32).astype(out_term.dtype)
-        pl.when(i == 1)(after_second)
-        pl.when(i == 3)(after_fourth)
-        pl.when(i == 5)(after_sixth)
-        return carry
-
-    lax.fori_loop(0, 8, step, 0)
-    sums.middle(0)
-    sums.middle(1)
-    gather.hop(3)
-    latent_total.finish()
-    gather.finish()
-    sums.end(0)
-    sums.end(1)
-    sums.finish()
-
-
-def latent_sums(cid, lat, query_up, latent_up, hidden, down):
-    kind = query_up.dtype
-    part = jax.ShapeDtypeStruct((8, query_up.shape[1], query_up.shape[2] // 4), kind)
-    half = (4,) + part.shape[1:]
-    return pl.pallas_call(
-        latent_kernel,
-        out_shape=[jax.ShapeDtypeStruct((8 * lat.shape[0], lat.shape[1]), lat.dtype), part,
-                   jax.ShapeDtypeStruct(latent_up.shape[1:], jnp.float32),
-                   jax.ShapeDtypeStruct((8, lat.shape[0], down.shape[1]), kind)],
-        in_specs=[ANY] + [VMEM] * 4, out_specs=[ANY] + [VMEM] * 3,
-        scratch_shapes=Gather.scratch(1) + PlaneSum.scratch([half] * 2, kind) + Total.scratch(latent_up),
-        compiler_params=kernel_params(cid),
-    )(lat, query_up, latent_up, hidden, down)
-
-
 def last_kernel(*refs):
-    gate, up, term, attn_out, lat, latent_up, query_up, gain = refs[:8]
-    gate_all, up_all, out, attn_sum, lat_sum, latent_sum, query_sum, gain_out = refs[8:16]
-    scratch = list(refs[16:])
+    gate, up, lat, query_up, latent_up, hidden, down, attn_out, cols, gain = refs[:10]
+    gate_all, up_all, out, attn_sum, lat_sum, latent_sum, query_sum, gain_out = refs[10:18]
+    scratch = list(refs[18:])
     rep, zpos, core = place()
     shard = zpos * 2 + core
     places = plane_places(rep)
+
+    def take(n):
+        nonlocal scratch
+        got, scratch = scratch[:n], scratch[n:]
+        return got
+
     swap = ColumnSwap([(lambda s, a=a: a.at[s], lambda s, b=b: b.at[s, rep]) for a, b in ((gate, gate_all), (up, up_all))],
-                      scratch[:2] + [None], keeps=False)
-    spread_sems, scratch = scratch[2:5], scratch[5:]
-    total, scratch = Total.split(term, out, scratch)
-    owns = scratch[:5]
-    gain_landed, gain_sum, gain_plane, gsend, grecv, hsend, hrecv = scratch[5:12]
-    query_total, scratch = Total.split(query_up, scratch[12], scratch[13:])
-    bufs, sems, _ = PlaneSum.split(scratch, 4)
+                      take(2) + [None], keeps=False)
+    spread_sems = take(3)
+    lat_all, out_term, lat_term, query_part, latent_own, query_own = take(6)
+    gather = Gather((lat,), (lat_all,), take(5))
+    owns = take(5)
+    gain_landed, gain_sum, gain_plane, gsend, grecv, hsend, hrecv = take(7)
+    total, scratch = Total.split(out_term, out, scratch)
+    query_total, scratch = Total.split(query_part, query_own, scratch)
+    latent_total, scratch = Total.split(latent_up, latent_own, scratch)
+    bufs, sems, _ = PlaneSum.split(scratch, 6)
+    width = query_up.shape[2] // 4
+    half = attn_out.shape[0] // 2
 
     def part(m, b):
         return lambda p: b.at[shard if m == 0 else column_place(zpos, core, m, True), p]
 
-    half = attn_out.shape[0] // 2
+    def query_item(h):
+        return (lambda p: query_up.at[pl.ds(4 * h, 4), :, pl.ds(mult(p * width, 128), width)], query_part.at[pl.ds(4 * h, 4)], h)
+
+    latent_low = scratch[-1]
     sums = PlaneSum(
-        [(functools.partial(quarter_cols, attn_out, h * half, half), owns[h], h) for h in range(2)]
-        + [(lambda p: lat.at[p], owns[2], 0), (functools.partial(quarter_cols, latent_up, 0, latent_up.shape[0]), owns[3], 1)],
+        [query_item(0), query_item(1)]
+        + [(functools.partial(quarter_cols, attn_out, h * half, half), owns[h], h) for h in range(2)]
+        + [(lambda p: lat_term.at[p], owns[2], 0),
+           (functools.partial(quarter_cols, latent_low, 0, latent_low.shape[0]), owns[3], 1)],
         bufs, sems)
     spread = PlaneGather(
         [(a.at[shard] if m == 0 else None, part(m, b), h) for m in range(8) for h, (a, b) in enumerate(((gate, gate_all), (up, up_all)))]
         + [(owns[h], functools.partial(quarter_cols, attn_sum, h * half, half), h) for h in range(2)]
         + [(owns[2], lambda p: lat_sum.at[p], 0),
-           (owns[3], functools.partial(quarter_cols, latent_sum, 0, latent_up.shape[0]), 1),
+           (owns[3], functools.partial(quarter_cols, latent_sum, 0, latent_low.shape[0]), 1),
            (owns[4], functools.partial(quarter_cols, query_sum, 0, query_up.shape[1]), 0)], spread_sems)
 
     def gain_copy(m):
@@ -949,88 +837,146 @@
     greet(rep, zpos, core, plane=3, column=True)
     for m in range(1, 8):
         gain_copy(m).start()
-    sums.start()
     swap.start()
+    sums.start((0, 1))
     spread.start((0, 1))
-    query_total.start()
-    total.start()
+    latent_total.start()
+    gather.start()
+    sums.start((2, 3))
+    rows = lat.shape[0]
+
+    def term(i, carry):
+        out_term[i] = jnp.dot(hidden[pl.ds(mult(i * rows, rows), rows)], down[...],
+                              preferred_element_type=jnp.float32).astype(out_term.dtype)
+        return carry
+
+    def arrive(m):
+        swap.arrive(m)
+        spread.start((2 * m, 2 * m + 1))
+
+    def onward(*ms):
+        for m in ms:
+            spread.middle(2 * m)
+            spread.middle(2 * m + 1)
+
+    lax.fori_loop(0, 3, term, 0)
+    arrive(1)
+    latent_total.pair()
+    latent_total.step(0)
+    lax.fori_loop(3, 6, term, 0)
+    onward(0)
+    gather.hop(1)
+    arrive(2)
+    arrive(6)
+    lax.fori_loop(6, 8, term, 0)
+    latent_total.step(1)
     gain_sum[...] = gain[shard]
     for m in range(1, 8):
         gain_copy(m).wait_recv()
         gain_sum[...] += gain_landed[m - 1]
     for k in range(3):
         gain_on(k).start()
-    near = ColumnSwap.near
-    for i, m in enumerate(near):
-        swap.arrive(m)
-        spread.start((2 * m, 2 * m + 1))
-        if i in (1, 2):
-            for k in range(2):
-                sums.middle(2 * i - 2 + k)
-        if i == 1:
-            query_total.pair()
-        if i in (1, 2, 3):
-            query_total.step(i - 1)
-        if i == 4:
-            query_total.finish()
-            owns[4][...] = query_total.out[...].astype(owns[4].dtype)
-            spread.start((20,))
-        before = 0 if i == 0 else near[i - 1]
-        spread.middle(2 * before)
-        spread.middle(2 * before + 1)
-        if i == 3:
-            total.pair()
-            total.step(0)
-        if i in (3, 4):
-            for k in range(2):
-                sums.end(2 * i - 6 + k)
-                spread.start((2 * i + 10 + k,))
+    total.start()
+    onward(1)
+    arrive(3)
+    arrive(7)
+    gather.hop(2)
+    sums.middle(0)
+    sums.middle(1)
+    latent_total.step(2)
+    onward(2, 6)
+    arrive(4)
+    arrive(5)
+    gather.hop(3)
+    total.pair()
+    total.step(0)
+    sums.middle(2)
+    sums.middle(3)
+    latent_total.finish()
+    latent_low[...] = latent_own[...].astype(latent_low.dtype)
+    sums.start((5,))
+    sums.end(0)
+    sums.end(1)
+    query_total.start()
+    gather.finish()
+    lat_term[...] = dot_tn(cols[...], lat_all[...]).astype(lat_term.dtype).reshape(lat_term.shape)
+    sums.start((4,))
+    query_total.pair()
+    query_total.step(0)
+    onward(3, 7)
     total.step(1)
-    for i in (2 * near[-1], 2 * near[-1] + 1, 20, 16, 17):
-        spread.middle(i)
+    sums.end(2)
+    sums.end(3)
+    spread.start((16, 17))
+    query_total.step(1)
+    onward(4, 5)
+    sums.middle(5)
+    sums.middle(4)
+    query_total.step(2)
     total.step(2)
-    for i in (18, 19):
+    query_total.finish()
+    owns[4][...] = query_own[...].astype(owns[4].dtype)
+    spread.start((20,))
+    sums.end(5)
+    spread.start((19,))
+    sums.end(4)
+    spread.start((18,))
+    for i in (16, 17, 20, 19, 18):
         spread.middle(i)
     gain_out[...] = gain_sum[...]
     for k in range(3):
         gain_on(k).wait_recv()
         gain_out[...] += gain_plane[k]
+    total.finish()
     for k in range(3):
         gain_on(k).wait_send()
     for m in range(1, 8):
         gain_copy(m).wait_send()
-    total.finish()
     swap.finish(arrive=False)
     sums.finish()
     spread.finish()
 
 
-def last_sums(cid, gate, up, term, attn_out, lat, latent_up, query_up, gain):
+def last_sums(cid, gate, up, lat, query_up, latent_up, hidden, down, attn_out, cols, gain):
     kind = gate.dtype
+    wide = jnp.float32
+    rows = lat.shape[0]
+    lat_shape = (4, cols.shape[1] // 4, lat.shape[1])
+    query_shape = (query_up.shape[1], query_up.shape[2] // 4)
     shapes = [(attn_out.shape[0] // 2, attn_out.shape[1] // 4)] * 2 + [
-        lat.shape[1:], (latent_up.shape[0], latent_up.shape[1] // 4)]
-    block = pltpu.VMEM(gain.shape[1:], gain.dtype)
+        lat_shape[1:], (latent_up.shape[1], latent_up.shape[2] // 4)]
+    out_term = jax.ShapeDtypeStruct((8, rows, down.shape[1]), kind)
+    query_part = jax.ShapeDtypeStruct((8,) + query_shape, kind)
     return pl.pallas_call(
         last_kernel,
         out_shape=[jax.ShapeDtypeStruct((8, 4) + gate.shape[1:], kind)] * 2
-        + [jax.ShapeDtypeStruct(term.shape[1:], jnp.float32)]
-        + [jax.ShapeDtypeStruct(a.shape, kind) for a in (attn_out, lat, latent_up)]
-        + [jax.ShapeDtypeStruct((query_up.shape[1], 4 * query_up.shape[2]), kind), jax.ShapeDtypeStruct(gain.shape[1:], gain.dtype)],
-        in_specs=[ANY] * 2 + [VMEM] * 6, out_specs=[ANY] * 2 + [VMEM] + [ANY] * 4 + [VMEM],
-        scratch_shapes=[dma_sems(7, 2), dma_sems(7, 2)] + PlaneGather.scratch(21) + Total.scratch(term)
-        + [pltpu.VMEM(s, kind) for s in shapes + [query_up.shape[1:]]]
-        + [pltpu.VMEM((7,) + gain.shape[1:], gain.dtype), block, pltpu.VMEM((3,) + gain.shape[1:], gain.dtype)]
-        + [dma_sems(7)] * 2 + [dma_sems(3)] * 2 + [pltpu.VMEM(query_up.shape[1:], jnp.float32)] + Total.scratch(query_up)
-        + PlaneSum.scratch(shapes, kind),
+        + [jax.ShapeDtypeStruct(out_term.shape[1:], wide)]
+        + [jax.ShapeDtypeStruct(s, kind) for s in (attn_out.shape, lat_shape, latent_up.shape[1:])]
+        + [jax.ShapeDtypeStruct((query_up.shape[1], query_up.shape[2]), kind), jax.ShapeDtypeStruct(gain.shape[1:], gain.dtype)],
+        in_specs=[ANY] * 3 + [VMEM] * 7, out_specs=[ANY] * 2 + [VMEM] + [ANY] * 4 + [VMEM],
+        scratch_shapes=[dma_sems(7, 2), dma_sems(7, 2)] + PlaneGather.scratch(21)
+        + [pltpu.VMEM((8 * rows, lat.shape[1]), kind), pltpu.VMEM(out_term.shape, kind), pltpu.VMEM(lat_shape, kind),
+           pltpu.VMEM(query_part.shape, kind), pltpu.VMEM(latent_up.shape[1:], wide), pltpu.VMEM(query_shape, wide)]
+        + Gather.scratch(1) + [pltpu.VMEM(s, kind) for s in shapes + [query_shape]]
+        + [pltpu.VMEM((7,) + gain.shape[1:], wide), pltpu.VMEM(gain.shape[1:], wide), pltpu.VMEM((3,) + gain.shape[1:], wide)]
+        + [dma_sems(7)] * 2 + [dma_sems(3)] * 2
+        + Total.scratch(out_term) + Total.scratch(query_part) + Total.scratch(latent_up)
+        + PlaneSum.scratch([(4,) + query_shape] * 2 + shapes, kind) + [pltpu.VMEM(latent_up.shape[1:], kind)],
         compiler_params=kernel_params(cid),
-    )(gate, up, term, attn_out, lat, latent_up, query_up, gain)
-
-
-def start_kernel(*refs):
-    ins, (gate, up) = refs[:7], refs[7:9]
-    outs, cols = refs[9:16], refs[16:18]
-    (zsend, zrecv, xsend, xrecv, ysend, yrecv, dsend, drecv, csend, crecv, own, gsend, grecv, psend, precv) = refs[18:33]
-    held, strips = refs[33:40], refs[40:42]
+    )(gate, up, lat, query_up, latent_up, hidden, down, attn_out, cols, gain)
+
+
+def start_kernel(scale, *refs):
+    ins, (gate, up), (tokens, bias, turns, down) = refs[:7], refs[7:9], refs[9:13]
+    outs, cols, refs = refs[13:20], refs[20:22], refs[22:]
+    (normed, query_low, latent, rope, kv, query, mixed, logs, query_lat, latent_proj, residual, ffn_all,
+     grad_hidden) = refs[:13]
+    refs = refs[13:]
+    (zsend, zrecv, xsend, xrecv, ysend, yrecv, dsend, drecv, csend, crecv, own, gsend, grecv, psend, precv) = refs[:15]
+    held, strips = refs[15:22], refs[22:24]
+    (small, gains, w_query, w_latent, w_query_up, w_latent_up, w_out, proj, ffn, lsend, lrecv, load_sems,
+     grad_sems) = refs[24:37]
+    gather = Gather((ffn,), (ffn_all,), refs[37:])
     rep, zpos, core = place()
     xrep, yrep, drep = plane_places(rep)
     shard = zpos * 2 + core
@@ -1077,7 +1023,7 @@
         ref = whole(a, z, c)
         getattr(copy(ref if src is None else src, ref, csend.at[slot, a], crecv.at[slot, a], rep, zpos * 2 + 1 - core), what)()
 
-    greet(rep, zpos, core, plane=2, column=True)
+    greet(rep, zpos, core, plane=3, column=True)
     def send_own(a):
         def first(way):
             def go(src):
@@ -1111,7 +1057,7 @@
             return pltpu.make_async_copy(ins[a], held[a], own.at[0, a])
         return pltpu.make_async_copy(held[a], whole(a, zpos, core), own.at[1, a])
 
-    for a in range(4):
+    for a in (5, 1, 2, 3, 0):
         send_own(a)
 
     strip = cols[0].shape[1]
@@ -1129,9 +1075,9 @@
         return remote(slice_of(which, s2, rep * quarter_rows, quarter_rows), rows_of(which, shard, rep),
                       gsend.at[m - 1, which], grecv.at[m - 1, which], rep, s2)
 
-    def slice_plane(m, quarter, kind, r):
-        ref = rows_of(0, column_place(zpos, core, m, back=True), quarter)
-        return remote(ref, ref, psend.at[kind, m - 1], precv.at[kind, m - 1], r, shard)
+    def slice_plane(m, which, quarter, kind, r):
+        ref = rows_of(which, column_place(zpos, core, m, back=True), quarter)
+        return remote(ref, ref, psend.at[kind, m - 1, which], precv.at[kind, m - 1, which], r, shard)
 
     def own_slice(which, half):
         if half == 0:
@@ -1157,18 +1103,21 @@
             s2 = column_place(zpos, core, m, back=True)
             ref = rows_of(which, s2, rep)
             remote(ref, ref, gsend.at[m - 1, which], grecv.at[m - 1, which], rep, s2).wait_recv()
-        slice_plane(m, rep, 0, xrep).start()
-        slice_plane(m, rep, 1, yrep).start()
-
-    def slices_from_plane(m):
-        slice_plane(m, xrep, 0, xrep).wait_recv()
-        slice_plane(m, yrep, 1, yrep).wait_recv()
-        slice_plane(m, *onward(m)).start()
+        slices_to_plane(m, 0)
+
+    def slices_to_plane(m, which):
+        slice_plane(m, which, rep, 0, xrep).start()
+        slice_plane(m, which, rep, 1, yrep).start()
+
+    def slices_from_plane(m, which=0):
+        slice_plane(m, which, xrep, 0, xrep).wait_recv()
+        slice_plane(m, which, yrep, 1, yrep).wait_recv()
+        slice_plane(m, which, *onward(m)).start()
 
     def onward(m):
-        return (xrep, 2, yrep) if m % 2 else (yrep, 2, xrep)
-
-    def from_column(h, way, z, slots=range(4)):
+        return (yrep, 2, xrep) if m % 2 else (xrep, 2, yrep)
+
+    def from_column(h, way, z, slots):
         for a in slots:
             hop(a, way, h - 1, z, "wait_recv")
             if h < 3:
@@ -1181,9 +1130,9 @@
             else:
                 to_core(a + 1, way * 3 + h, z, core, "start")
 
-    def from_plane(h, way, z):
+    def from_plane(h, way, z, slots):
         k = way * 3 + h - 1
-        for a in range(4):
+        for a in slots:
             to_plane(a, k, z, xrep, "wait_recv", (xsend, xrecv), xrep)
             if a == 0:
                 to_plane(a, k, z, xrep, "start", (dsend, drecv), yrep)
@@ -1191,12 +1140,12 @@
             if a > 0:
                 to_plane(a, k, z, yrep, "start", (dsend, drecv), xrep)
 
-    def from_corner(h, way, z):
+    def from_corner(h, way, z, slots):
         k = way * 3 + h - 1
-        for a in range(4):
+        for a in slots:
             to_plane(a, k, z, drep, "wait_recv", (dsend, drecv), drep)
-        for a in range(5):
-            to_core(a, k + 1, z, core, "start")
+            for b in (a,) if a < 3 else (3, 4):
+                to_core(b, k + 1, z, core, "start")
 
     def by_hop(stage, h, *more):
         for way in range(2):
@@ -1206,44 +1155,194 @@
             def _():
                 stage(h, way, z, *more)
 
-    by_hop(from_column, 1)
-    by_hop(from_column, 2)
+    def arrived(arrays):
+        for b in arrays:
+            keep(b, 1).wait()
+            to_core(b, 0, zpos, 1 - core, "wait_recv")
+
+            def theirs(h, way, z):
+                to_core(b, way * 3 + h, z, 1 - core, "wait_recv")
+
+            for h in range(1, 4):
+                by_hop(theirs, h)
+
+    wide, low = jnp.float32, jnp.bfloat16
+
+    def tile(t):
+        return slice(128 * t, 128 * t + 128)
+
+    def normalize(src, dst, tiles, first):
+        square = sum(jnp.sum(jnp.square(src(t)), axis=1, keepdims=True) for t in range(tiles))
+        factor = lax.rsqrt(square / (128 * tiles) + epsilon)
+        for t in range(tiles):
+            dst[:, tile(t)] = (src(t) * factor * gains[first + t : first + t + 1, :]).astype(low)
+
+    def load(b, to, i):
+        return pltpu.make_async_copy(outs[b], to, load_sems.at[i])
+
+    def share(k, what):
+        rows = tokens.shape[0]
+        for i, ref in enumerate((latent, rope)):
+            copy_ = remote(ref.at[pl.ds(0, rows)], ref.at[pl.ds((k + 1) * rows, rows)], lsend.at[k, i], lrecv.at[k, i],
+                           plane_places(rep)[k], shard)
+            getattr(copy_, what)()
+
+    def down_products():
+        arrived((1, 2))
+        load(1, w_query, 1).start()
+        load(2, w_latent, 2).start()
+        load(2, w_latent, 2).wait()
+        latent_proj[...] = jnp.dot(normed[...], w_latent[...], preferred_element_type=wide)
+        normalize(lambda t: latent_proj[:, tile(t)], latent.at[pl.ds(0, tokens.shape[0])], 2, 46)
+        edge = jnp.zeros((tokens.shape[0], 64), wide)
+        key = jnp.concatenate([edge, latent_proj[:, 256:288], edge[:, :32]], axis=1)
+        rope[0 : tokens.shape[0]] = turn(key, (turns[0], turns[1], turns[2])).astype(low)
+        for k in range(3):
+            share(k, "start")
+        load(1, w_query, 1).wait()
+        query_lat[...] = jnp.dot(normed[...], w_query[...], preferred_element_type=wide)
+        normalize(lambda t: query_lat[:, tile(t)], query_low, 6, 40)
+
+    def chunk_loop(count, body):
+        lax.fori_loop(0, count, lambda i, c: (body(i), c)[1], 0)
+
+    def query_chunk(i):
+        at = pl.ds(mult(i * 1024, 128), 1024)
+        proj[:, at] = jnp.dot(query_low[...], w_query_up[:, at], preferred_element_type=wide)
+
+    def key_chunk(i):
+        at = pl.ds(mult(i * 1024, 128), 1024)
+        kv[:, at] = jnp.dot(latent[...], w_latent_up[:, at], preferred_element_type=wide).astype(low)
+
+    out_rows = w_out.shape[1]
+
+    def out_strip(i):
+        return pltpu.make_async_copy(outs[0].at[pl.ds(mult(i * out_rows, 128), out_rows)], w_out.at[i % 2], load_sems.at[4 + i % 2])
+
+    by_hop(from_column, 1, (5, 1, 2))
+    by_hop(from_column, 1, (3, 0))
+    by_hop(from_column, 2, (5, 1, 2))
+    by_hop(from_plane, 1, (1, 2))
+    by_hop(from_column, 2, (3, 0))
+    by_hop(from_plane, 1, (3, 0))
+    by_hop(from_column, 3, (5, 1, 2))
+    by_hop(from_plane, 2, (1, 2))
+    by_hop(from_corner, 1, (1, 2))
+    by_hop(from_column, 3, (3, 0))
     for m in near:
         for which in range(2):
             slice_copy(m, which).start()
-    by_hop(from_plane, 1)
-    by_hop(from_column, 3)
-    by_hop(from_plane, 2)
-    by_hop(from_corner, 1)
+    by_hop(from_plane, 3, (1, 2))
+    by_hop(from_corner, 2, (1, 2))
+    by_hop(from_plane, 2, (3, 0))
+    arrived((6,))
+    load(6, small, 0).start()
+    load(6, small, 0).wait()
+    gains[...] = sum(small[48 * s : 48 * s + 48, :] for s in range(8))
+    normalize(lambda t: tokens[:, tile(t)].astype(wide), normed, 20, 0)
+    by_hop(from_corner, 3, (1, 2))
+    by_hop(from_corner, 1, (3, 0))
+    down_products()
+    by_hop(from_plane, 3, (3, 0))
+    by_hop(from_corner, 2, (3, 0))
     for m in near[:3]:
         slices_from_column(m)
     send_own(4)
-    send_own(5)
-    by_hop(from_plane, 3)
+    by_hop(from_corner, 3, (3, 0))
+    arrived((3, 4))
+    load(3, w_query_up, 3).start()
+    load(4, w_latent_up, 0).start()
     for m in near[3:]:
         slices_from_column(m)
-    by_hop(from_corner, 2)
+    load(3, w_query_up, 3).wait()
+    chunk_loop(5, query_chunk)
     for m in near[:3]:
         slices_from_plane(m)
-    by_hop(from_column, 1, (5, 4))
-    by_hop(from_corner, 3)
+    for k in range(3):
+        share(k, "wait_recv")
+    load(4, w_latent_up, 0).wait()
+    chunk_loop(5, key_chunk)
+    logs[...] = jnp.zeros_like(logs)
+    group = attend_heads(scale, proj, kv, rope, bias, turns, query, mixed, logs)
+
+    def attend_step(i, carry):
+        group(i, carry)
+
+        @pl.when(i == 3)
+        def _():
+            by_hop(from_column, 1, (4,))
+
+        @pl.when(i == 8)
+        def _():
+            by_hop(from_column, 2, (4,))
+        return carry
+
+    lax.fori_loop(0, kv.shape[1] // 512, attend_step, 0)
+    arrived((0,))
+    out_strip(0).start()
+    residual[...] = tokens[...].astype(wide)
+
+    def out_step(i, carry):
+        out_strip(i).wait()
+
+        @pl.when(i < 3)
+        def _():
+            out_strip(i + 1).start()
+
+        residual[...] += residual_scale * jnp.dot(
+            mixed[:, pl.ds(mult(i * out_rows, 128), out_rows)], w_out[i % 2], preferred_element_type=wide)
+        return carry
+
+    lax.fori_loop(0, 4, out_step, 0)
+    normalize(lambda t: residual[:, tile(t)], ffn, 20, 20)
+    gather.start()
+    for m in near:
+        slices_to_plane(m, 1)
+    by_hop(from_column, 3, (4,))
     for m in near[3:]:
         slices_from_plane(m)
-    by_hop(from_column, 2, (5, 4))
-    by_hop(from_column, 3, (5, 4))
+    gather.hop(1)
+    arrived((5,))
+    chunk = 2 * tokens.shape[0]
+
+    def grad_chunk(i):
+        return pltpu.make_async_copy(
+            outs[5].at[pl.ds(mult(i * chunk, chunk), chunk)], w_out.at[i % 2, pl.ds(0, chunk)], grad_sems.at[i % 2])
+
+    def hidden_step(i, carry):
+        grad_chunk(i).wait()
+
+        @pl.when(i < 3)
+        def _():
+            grad_chunk(i + 1).start()
+
+        grad_hidden[pl.ds(mult(i * chunk, chunk), chunk)] = dot_nt(w_out[i % 2, :chunk], down[...])
+
+        @pl.when(i == 2)
+        def _():
+            gather.hop(2)
+        return carry
+
+    grad_chunk(0).start()
+    lax.fori_loop(0, 4, hidden_step, 0)
+    for m in near:
+        slices_from_plane(m, 1)
+    for k in range(3):
+        share(k, "wait_send")
+    gather.hop(3)
+    gather.finish()
     for a in range(7):
         to_core(a, 0, zpos, core, "wait_send", src=ins[a])
-        to_core(a, 0, zpos, 1 - core, "wait_recv")
-        keep(a, 1).wait()
     for which in range(2):
         own_slice(which, 1).wait()
         for m in near:
             slice_copy(m, which).wait_send()
     for m in near:
-        slice_plane(m, rep, 0, xrep).wait_send()
-        slice_plane(m, rep, 1, yrep).wait_send()
-        slice_plane(m, *onward(m)).wait_send()
-        slice_plane(m, drep, 2, drep).wait_recv()
+        for which in range(2):
+            slice_plane(m, which, rep, 0, xrep).wait_send()
+            slice_plane(m, which, rep, 1, yrep).wait_send()
+            slice_plane(m, which, *onward(m)).wait_send()
+            slice_plane(m, which, drep, 2, drep).wait_recv()
     for way in range(2):
         for h in range(3):
             z = zpos - h if way == 0 else zpos + h
@@ -1265,18 +1364,34 @@
                     to_plane(a, k, z, xrep if a == 0 else yrep, "wait_send", (dsend, drecv), yrep)
                 for a in range(7):
                     to_core(a, k + 1, z, core, "wait_send")
-                    to_core(a, k + 1, z, 1 - core, "wait_recv")
-
-def start_gather(cid, weights, gate, up, strip):
+
+def start_gather(cid, scale, weights, gate, up, tokens, bias, turns, down):
+    low, wide = jnp.bfloat16, jnp.float32
+    rows, width = tokens.shape
+    strip = down.shape[0]
+    attn_out, query_down, latent_down, query_up, latent_up = weights[:5]
+    tiles = query_up.shape[1]
+    keys = bias.shape[1]
     out = [jax.ShapeDtypeStruct((a.shape[0] * 8,) + a.shape[1:], a.dtype) for a in weights]
     out += [jax.ShapeDtypeStruct((gate.shape[0] * 8, strip), gate.dtype)] * 2
+    latent_rank = 8 * latent_up.shape[0]
+    found = [((rows, width), low), ((rows, query_down.shape[1]), low), ((keys, latent_rank), low), ((keys, 128), low),
+             ((keys, tiles), low), ((rows, tiles), low), ((rows, tiles // 2), low), ((rows, 128), wide),
+             ((rows, query_down.shape[1]), wide), ((rows, latent_down.shape[1]), wide), ((rows, width), wide),
+             ((8 * rows, width), low), ((8 * rows, strip), wide)]
+    out += [jax.ShapeDtypeStruct(s, d) for s, d in found]
+    whole = [pltpu.VMEM((a.shape[0] * 8, a.shape[1]), a.dtype) for a in (query_down, latent_down, query_up, latent_up)]
     return pl.pallas_call(
-        start_kernel, out_shape=out, in_specs=[ANY] * 9, out_specs=[ANY] * 9,
+        functools.partial(start_kernel, scale), out_shape=out,
+        in_specs=[ANY] * 9 + [VMEM] * 4, out_specs=[ANY] * 9 + [VMEM] * 11 + [ANY, VMEM],
         scratch_shapes=[dma_sems(2, 3, 6), dma_sems(2, 3, 6)] + [dma_sems(6, 4)] * 6
-        + [dma_sems(7, 7), dma_sems(7, 7), dma_sems(2, 9), dma_sems(7, 2), dma_sems(7, 2), dma_sems(3, 7), dma_sems(3, 7)]
-        + [pltpu.VMEM(a.shape, a.dtype) for a in weights] + [pltpu.VMEM((gate.shape[0], strip), gate.dtype)] * 2,
+        + [dma_sems(7, 7), dma_sems(7, 7), dma_sems(2, 9), dma_sems(7, 2), dma_sems(7, 2), dma_sems(3, 7, 2), dma_sems(3, 7, 2)]
+        + [pltpu.VMEM(a.shape, a.dtype) for a in weights] + [pltpu.VMEM((gate.shape[0], strip), gate.dtype)] * 2
+        + [pltpu.VMEM((8 * weights[6].shape[0], 128), wide), pltpu.VMEM(weights[6].shape, wide)] + whole
+        + [pltpu.VMEM((2, 2 * attn_out.shape[0], width), low), pltpu.VMEM((rows, tiles), wide),
+           pltpu.VMEM((rows, width), low), dma_sems(3, 2), dma_sems(3, 2), dma_sems(6), dma_sems(2)] + Gather.scratch(1),
         compiler_params=kernel_params(cid),
-    )(*weights, gate, up)
+    )(*weights, gate, up, tokens, bias, turns, down)
 
 def plane_swap(values, j):
     return lax.ppermute(values, "rep", [(i, i ^ j) for i in range(4)])
@@ -1310,24 +1425,20 @@
     strip = 896
     shift = (slice_ff * shard) % 128
 
+    gain_list = (gain_attn, gain_ffn, gain_query, gain_latent)
     small = jnp.concatenate(
-        [v.astype(wide) for v in (gain_attn, gain_ffn, gain_query, gain_latent)]
-        + [jnp.zeros((1024 - 768,), wide)]
-    ).reshape(8, 128)
+        [
+            lax.dynamic_update_slice(
+                jnp.zeros((8 * v.shape[0],), wide), v.astype(wide), (shard * v.shape[0],)
+            )
+            for v in gain_list
+        ]
+    ).reshape(-1, 128)
     tile_up = jnp.pad(
         query_up.reshape(-1, H, head_dim), ((0, 0), (0, 0), (0, 128 - head_dim))
     ).reshape(-1, H * 128)
     grad_out = cotangent[0].astype(wide)
     grad_down_in = (residual_scale * grad_out).astype(low)
-    aout, qdown, ldown, qup, lup, gd_all, small_all, gate_w, up_quarter = start_gather(
-        0, (attn_out, query_down, latent_down, tile_up, latent_up, grad_down_in, small), w_gate, w_up, strip
-    )
-    small_all = small_all.reshape(8, 1024)
-    gain_in = small_all[:, :320].reshape(-1)
-    gain_f = small_all[:, 320:640].reshape(-1)
-    gain_q = small_all[:, 640:736].reshape(-1)
-    gain_l = small_all[:, 736:768].reshape(-1)
-
     down_w = lax.dynamic_update_slice(jnp.zeros((strip, width), low), w_down, (shift, 0))
 
     local_pos = rep * rows + jnp.arange(rows, dtype=jnp.int32)
@@ -1349,32 +1460,55 @@
             jnp.concatenate([edge, -sin_part, none, tail], axis=1),
         ]
     )
-    inputs = tokens[0].astype(wide)
-    normed, norm_in_back = jax.vjp(rms_scale, inputs, gain_in)
-    normed_low = normed.astype(low)
-    latent_proj = jnp.dot(normed_low, ldown, preferred_element_type=wide)
-    latent_norm, norm_l_back = jax.vjp(rms_scale, latent_proj[:, :KR], gain_l)
+    (
+        aout,
+        qdown,
+        ldown,
+        qup,
+        lup,
+        gd_all,
+        small_all,
+        gate_w,
+        up_w,
+        normed_low,
+        query_low,
+        latent_low,
+        rope_tile,
+        keyvals,
+        queries,
+        mixed_low,
+        logs,
+        query_lat,
+        latent_proj,
+        residual,
+        ffn_all,
+        grad_hidden,
+    ) = start_gather(
+        0,
+        scale,
+        (attn_out, query_down, latent_down, tile_up, latent_up, grad_down_in, small),
+        w_gate,
+        w_up,
+        tokens[0],
+        bias,
+        turns,
+        down_w,
+    )
+    gains_all = jnp.sum(small_all.reshape(8, -1), axis=0)
+    gain_in, gain_f = gains_all[:width], gains_all[width : 2 * width]
+    gain_q = gains_all[2 * width : 2 * width + query_down.shape[1]]
+    gain_l = gains_all[2 * width + query_down.shape[1] :]
 
     def key_rotate(values):
         return rotate(values, cos_part, sin_part)
 
-    key_rot, key_back = jax.vjp(key_rotate, latent_proj[:, KR:])
-    latents = jnp.concatenate([latent_norm.astype(low), key_rot.astype(low)], axis=1)
-    latents = jnp.concatenate([latents] + [plane_swap(latents, j) for j in range(1, 4)], axis=0)
-    latent_low, all_rope = latents[:, :KR], latents[:, KR:]
-    query_lat = jnp.dot(normed_low, qdown, preferred_element_type=wide)
-    query_norm, norm_q_back = jax.vjp(rms_scale, query_lat, gain_q)
-    query_low = query_norm.astype(low)
-    query_proj = jnp.dot(query_low, qup, preferred_element_type=wide)
-    keyvals = jnp.dot(latent_low, lup, preferred_element_type=wide).astype(low)
-    rope_tile = jnp.pad(all_rope, ((0, 0), (ND, 128 - head_dim)))
-    queries, mixed_low, logs = attend(scale, query_proj, keyvals, rope_tile, bias, turns)
-    branch = jnp.dot(mixed_low, aout, preferred_element_type=wide)
-    residual = inputs + residual_scale * branch
-    normed_ffn, norm_f_back = jax.vjp(rms_scale, residual, gain_f)
-    ffn_low = normed_ffn.astype(low)
-
-    ffn_all, up_w, grad_hidden = ffn_gather(1, ffn_low, up_quarter, gd_all, down_w)
+    inputs = tokens[0].astype(wide)
+    norm_in_back = jax.vjp(rms_scale, inputs, gain_in)[1]
+    norm_q_back = jax.vjp(rms_scale, query_lat, gain_q)[1]
+    norm_l_back = jax.vjp(rms_scale, latent_proj[:, :KR], gain_l)[1]
+    key_back = jax.vjp(key_rotate, latent_proj[:, KR:])[1]
+    norm_f_back = jax.vjp(rms_scale, residual, gain_f)[1]
+
     gate_pre = jnp.dot(ffn_all, gate_w, preferred_element_type=wide)
     up_pre = jnp.dot(ffn_all, up_w, preferred_element_type=wide)
     hidden, act_back = jax.vjp(swiglu, gate_pre, up_pre)
@@ -1431,18 +1565,9 @@
     tokens_grad = (grad_resid + grad_in_norm).astype(low)
 
     grad_lats = jnp.concatenate([grad_q_lat, grad_lat], axis=1)
-    lat_all, qup_own, lup_sum, out_part = latent_sums(
-        4,
-        grad_lats,
-        qup_part.reshape(8, -1, qup_part.shape[1]),
-        lup_part.reshape(8, -1, lup_part.shape[1]),
-        hidden_low,
-        down_w,
-    )
     mixed_cols = cols_all[:, 0].reshape(8 * rows, width // 8)
     normed_cols = cols_all[:, 1].reshape(8 * rows, width // 8)
     aout_part = inner_rows(mixed_cols, branch_all).astype(low)
-    lat_part = inner_rows(normed_cols, lat_all).astype(low)
     gains = jnp.concatenate(
         [
             v.reshape(8, -1)
@@ -1452,14 +1577,16 @@
         axis=1,
     ).reshape(8, 8, 128)
     gate_all, up_all, out_sum, aout_own, lat_own, lup_own, qup_own, gain_own = last_sums(
-        5,
+        4,
         gate_own,
         up_own,
-        out_part,
+        grad_lats,
+        qup_part.reshape(8, -1, qup_part.shape[1]),
+        lup_part.reshape(8, -1, lup_part.shape[1]),
+        hidden_low,
+        down_w,
         aout_part,
-        lat_part.reshape(4, 80, -1),
-        lup_sum.astype(low),
-        qup_own,
+        normed_cols,
         gains,
     )
     layer_out = (residual + residual_scale * out_sum).astype(low)

time: 760 us -> 721 us (0.949)
  Pallas kernels: 624 us -> 600 us
  matrix products: 65.1 us -> 46.6 us
    pallas_call x4 -> x1, Pallas kernels: 285 us -> 215 us  [start_gather(): pl.pallas_call(functools.partial(start_kernel, scale), out_shape=out, in_...]
    pallas_call x1, Pallas kernels: 143 us -> 190 us  [last_sums(): pl.pallas_call(last_kernel, out_shape=[jax.ShapeDtypeStruct((8, 4) + gate...]
    dot_general x5 -> x0, matrix products: 21.7 us -> none  [the longest x1 6.73 us: column_body(): branch = jnp.dot(mixed_low, aout, preferred_element_type=wide)]
  transfers between devices with their start and end apart: 6 -> 3, of which waited for: 0 -> 0; matrix products, arithmetic and copies ran while one was open for 4% -> 3% of each run, Pallas kernels for 0% -> 0%
where the time goes in v4:
time: 721 us; the launch traced here: 713 us
  Pallas kernels  600 us (83%)
  matrix products  46.6 us (6%)
  other arithmetic  34.7 us (5%)
  local copies, waits for them, and re-layouts  26.6 us (4%)
    pallas_call x1, Pallas kernels, start_gather(): pl.pallas_call(functools.partial(start_kernel, scale), out_shape=out, in_...  215 us
    pallas_call x1, Pallas kernels, last_sums(): pl.pallas_call(last_kernel, out_shape=[jax.ShapeDtypeStruct((8, 4) + gate...  190 us
    pallas_call x1, Pallas kernels, middle_exchange(): pl.pallas_call(functools.partial(middle_kernel, scale), out_shape=[jax.Sh...  95.2 us
    pallas_call x1, Pallas kernels, back_sums(): pl.pallas_call(functools.partial(back_kernel, rows % 128), out_shape=[jax...  86.5 us
    dot_general x4, matrix products, outer_cols(): lax.dot_general(leading, trailing, (((1,), (1,)), ((), ())), preferred_el...  16.7 us
  transfers between devices with their start and end apart: 3, of which 0 were waited for; matrix products, arithmetic and copies ran while one was open for 3% of the time, Pallas kernels for 0%

profile of v4, /device:TPU:0, one launch (start us, length us, event | category | flops | bytes accessed | tf_op | source)
XLA Modules:
  0.0 713.3 jit_solution(16091455419365832988)
XLA Ops:
  2.6 1.8 copy.47.refs_2_
  5.2 2.0 fusion.4.refs_5_
  7.3 1.5 reshape.188
  12.1 1.9 copy-done.7
  15.1 1.5 copy-done
  16.6 215.4 %shard_map.254 = (bf16[2560,2560]{1,0:T(8,128)(2,1)}, bf16[2560,768]{1,0:T(8,128)(2,1)}, bf16[2560,288]{1,0:T(8,128)(2,1)}, bf16[768,5120]{1,0:T(8,128)(2,1)}, b...) custom-call(bf16[320,2560]{1,0:T(8,128)(2,1)} %refs_0_.1, ...), custom_call_target="tpu_custom_call" | custom-call | tf_op jit(solution)/shard_map/pallas_call | solution.py:1384
  231.9 1.6 multiply_reduce_fusion.2
  237.4 9.0 %fusion.35 = f32[1024,896]{1,0:T(8,128)S(1)} fusion(bf16[1024,2560]{1,0:T(8,128)(2,1)} %get-tuple-element.60.refs_1_, bf16[2560,896]{1,0:T(8,128)(2,1)} %get-tuple-element.62.refs_5_), kind=kOutput, calls=%fused_computation.113 | convolution fusion | flops 4697620480 | bytes 13500416 | tf_op jit(solution)/shard_map/dot_general | solution.py:1513
  246.5 10.8 %multiply_convert_fusion = (bf16[1024,896]{1,0:T(8,128)(2,1)}, bf16[1024,896]{1,0:T(8,128)(2,1)}, bf16[1024,896]{1,0:T(8,128)(2,1)S(1)}) fusion(f32[1024,896]{1,0:T(8,128)S(1)} %copy-done.38, f32[1024,896]{1,0:T(8,128)S(1)} %fusion.35, bf16[1024,2560]{1,0:T(8,128)(2,1)S(1)} %bitcast.71, bf16[2560,896]{1,0:T(8,128)(2,1)} %get-tuple-element.61.refs_4_), kind=kOutput, calls=%fused_computation.7 | convolution fusion | flops 4712300544 | bytes 22675456 | tf_op jit(solution)/shard_map/dot_general | solution.py:1512
  257.3 7.0 convolution_convert_fusion.refs_0_
  264.4 86.5 %shard_map.255 = (f32[128,2560]{1,0:T(8,128)}, bf16[800,640]{1,0:T(8,128)(2,1)}, bf16[8,80,896]{2,1,0:T(8,128)(2,1)}, bf16[8,4,80,896]{3,2,1,0:T(8,128)(2,1)}) custom-call(bf16[896,2560]{1,0:T(8,128)(2,1)} %convolution_convert_fusion.refs_0_, bf16[1024,2560]{1,0:T(8,128)(2,1)} %get-tuple-element.60.refs_1_, bf16[1024,896]{1,0:T(8,128)(2,1)} %get-tuple-element.113.refs_2_, ...), custom_call_target="tpu_custom_call" | custom-call | tf_op jit(solution)/shard_map/pallas_call | solution.py:672
  350.9 1.9 multiply_reduce_fusion
  352.9 1.4 multiply_convert_fusion.2.refs_0_
  354.3 1.4 maximum_bitcast_fusion.refs_1_
  355.7 95.2 %shard_map.256 = (bf16[1024,2560]{1,0:T(8,128)(2,1)}, bf16[8,2,128,320]{3,2,1,0:T(8,128)(2,1)}, bf16[800,2560]{1,0:T(8,128)(2,1)}, bf16[8,80,896]{2,1,0:T(8,128)...) custom-call(bf16[128,2560]{1,0:T(8,128)(2,1)} %multiply_convert_fusi, ...), custom_call_target="tpu_custom_call" | custom-call | tf_op jit(solution)/shard_map/pallas_call | solution.py:766
  452.0 4.2 convolution_convert_fusion.2
  457.6 1.4 collective-permute-start.2
  459.0 1.5 collective-permute-start.1
  461.6 6.2 multiply_reduce_fusion.3
  470.2 2.5 fusion.36
  472.6 3.1 convolution_convert_fusion.1.refs_7_
  477.1 6.7 convert_element_type.123
  489.7 3.8 fusion.10
  494.4 190.1 %shard_map.257 = (bf16[8,4,80,896]{3,2,1,0:T(8,128)(2,1)}, bf16[8,4,80,896]{3,2,1,0:T(8,128)(2,1)}, f32[128,2560]{1,0:T(8,128)}, bf16[320,2560]{1,0:T(8,128)(2,1...) custom-call(bf16[8,80,896]{2,1,0:T(8,128)(2,1)} %get-tuple-element.65., ...), custom_call_target="tpu_custom_call" | custom-call | tf_op jit(solution)/shard_map/pallas_call | solution.py:950
  684.5 1.3 slice.78
  686.9 1.4 fusion.34
  688.3 1.2 bitcast_convert_fusion
  692.3 2.0 copy.55
  694.3 2.6 shard_map.258
  696.9 3.5 convert_element_type.122
  700.5 10.2 %shard_map.259 = (f32[320,6400]{1,0:T(8,128)}, f32[320,6400]{1,0:T(8,128)}) custom-call(bf16[8,4,80,896]{3,2,1,0:T(8,128)(2,1)} %get-tuple-element.99.refs_0_, bf16[8,4,80,896]{3,2,1,0:T(8,128)(2,1)} %get-tuple-element.100.refs_1_), custom_call_target="tpu_custom_call" | custom-call | tf_op jit(solution)/shard_map/pallas_call | solution.py:256
  710.7 2.1 fusion.12
  (176 shorter events, 28.9 us)
Async XLA Ops:
  0.6 6.6 copy-start.21
  233.5 119.3 %copy-start.28 = (f32[128]{0:T(128)}, f32[128]{0:T(128)S(1)}, u32[]{:S(2)}) copy-start(f32[128]{0:T(128)S(1)} %fusion.27) | copy-start | bytes 1540
  236.2 10.2 %slice-start = ((s8[5242880]{0:T(1024)(128)(4,1)}), s8[1048576]{0:T(1024)(128)(4,1)S(1)}, s32[]{:S(2)}) async-start(s8[5242880]{0:T(1024)(128)(4,1)} %bitcast.70), calls=%async_computation | async-start | bytes 2097152
  237.4 9.0 %slice-start.1 = ((s8[5242880]{0:T(1024)(128)(4,1)}), s8[4194304]{0:T(1024)(128)(4,1)S(1)}, s32[]{:S(2)}) async-start(s8[5242880]{0:T(1024)(128)(4,1)} %bitcast.70), calls=%async_computation.1 | async-start | bytes 8388608
  237.4 9.0 %copy-start.38 = (f32[1024,896]{1,0:T(8,128)S(1)}, f32[1024,896]{1,0:T(8,128)}, u32[]{:S(2)}) copy-start(f32[1024,896]{1,0:T(8,128)} %get-tuple-element.64) | copy-start | bytes 11010052
  237.4 19.9 %slice-start.4 = ((s8[5242880]{0:T(1024)(128)(4,1)}), s8[4194304]{0:T(1024)(128)(4,1)S(1)}, s32[]{:S(2)}) async-start(s8[5242880]{0:T(1024)(128)(4,1)} %bitcast.88), calls=%async_computation.4 | async-start | bytes 8388608
  246.5 10.8 %slice-start.5 = ((s8[5242880]{0:T(1024)(128)(4,1)}), s8[1048576]{0:T(1024)(128)(4,1)S(1)}, s32[]{:S(2)}) async-start(s8[5242880]{0:T(1024)(128)(4,1)} %bitcast.88), calls=%async_computation.5 | async-start | bytes 2097152
  257.3 7.1 copy-start.11
  264.4 86.6 %copy-start.1 = (f32[128,2560]{1,0:T(8,128)S(1)}, f32[128,2560]{1,0:T(8,128)}, u32[]{:S(2)}) copy-start(f32[128,2560]{1,0:T(8,128)} %get-tuple-element.59) | copy-start | bytes 3932164
  355.7 96.2 %copy-start.39 = (bf16[256,5120]{1,0:T(8,128)(2,1)S(1)}, bf16[256,5120]{1,0:T(8,128)(2,1)}, u32[]{:S(2)}) copy-start(bf16[256,5120]{1,0:T(8,128)(2,1)} %get-tuple-element.84) | copy-start | bytes 7864324
  452.0 8.5 %copy-start.3 = (bf16[1,128,2560]{2,1,0:T(8,128)(2,1)S(1)}, bf16[1,128,2560]{2,1,0:T(8,128)(2,1)}, u32[]{:S(2)}) copy-start(bf16[1,128,2560]{2,1,0:T(8,128)(2,1)} %param.15) | copy-start | bytes 1966084
  452.0 9.3 %copy-start.9 = (f32[128,768]{1,0:T(8,128)S(1)}, f32[128,768]{1,0:T(8,128)}, u32[]{:S(2)}) copy-start(f32[128,768]{1,0:T(8,128)} %get-tuple-element.82) | copy-start | bytes 1179652
  452.0 20.6 %slice-start.2 = ((s8[5242880]{0:T(1024)(128)(4,1)}), s8[4194304]{0:T(1024)(128)(4,1)S(1)}, s32[]{:S(2)}) async-start(s8[5242880]{0:T(1024)(128)(4,1)} %bitcast.86), calls=%async_computation.2 | async-start | bytes 8388608
  456.2 5.3 copy-start.17
  456.2 5.2 copy-start.19
  456.2 5.3 copy-start.13
  457.0 26.8 %collective-permute-start = (bf16[128,288]{1,0:T(8,128)(2,1)}, bf16[128,288]{1,0:T(8,128)(2,1)}, u32[]{:S(2)}, u32[]{:S(2)}) collective-permute-start(bf16[128,288]{1,0:T(8,128)(2,1)} %get-tuple-element.119), channel_id=1, source_target_pairs={{0,8},{8,0},{16,24},{24,16},{1,9},{9,1},{17,25},{25,17},{2,10},{10... | collective-permute-start | bytes 221192 | tf_op jit(solution)/shard_map/ppermute | solution.py:1397
  457.6 26.2 %collective-permute-start.2 = (bf16[128,288]{1,0:T(8,128)(2,1)}, bf16[128,288]{1,0:T(8,128)(2,1)}, u32[]{:S(2)}, u32[]{:S(2)}) collective-permute-start(bf16[128,288]{1,0:T(8,128)(2,1)} %get-tuple-element.120), channel_id=1, source_target_pairs={{0,24},{8,16},{16,8},{24,0},{1,25},{9,17},{17,9},{25,1},{2,26},{10... | collective-permute-start | bytes 221192 | tf_op jit(solution)/shard_map/ppermute | solution.py:1397
  459.0 24.8 %collective-permute-start.1 = (bf16[128,288]{1,0:T(8,128)(2,1)}, bf16[128,288]{1,0:T(8,128)(2,1)}, u32[]{:S(2)}, u32[]{:S(2)}) collective-permute-start(bf16[128,288]{1,0:T(8,128)(2,1)} %get-tuple-element.121), channel_id=1, source_target_pairs={{0,16},{8,24},{16,0},{24,8},{1,17},{9,25},{17,1},{25,9},{2,18},{10... | collective-permute-start | bytes 221192 | tf_op jit(solution)/shard_map/ppermute | solution.py:1397
  461.5 6.2 copy-start.12
  461.6 11.1 %slice-start.3 = ((s8[5242880]{0:T(1024)(128)(4,1)}), s8[1048576]{0:T(1024)(128)(4,1)S(1)}, s32[]{:S(2)}) async-start(s8[5242880]{0:T(1024)(128)(4,1)} %bitcast.86), calls=%async_computation.3 | async-start | bytes 2097152
  475.7 10.1 %copy-start.33 = (f32[128]{0:T(128)}, f32[128]{0:T(128)S(1)}, u32[]{:S(2)}) copy-start(f32[128]{0:T(128)S(1)} %fusion.29) | copy-start | bytes 1540
  477.1 6.7 copy-start.16
  477.1 6.7 copy-start.18
  477.1 8.7 %copy-start.20 = (f32[128,288]{1,0:T(8,128)S(1)}, f32[128,288]{1,0:T(8,128)}, u32[]{:S(2)}) copy-start(f32[128,288]{1,0:T(8,128)} %get-tuple-element.86) | copy-start | bytes 442372
  700.4 10.3 %copy-start.5 = (bf16[1,128,2560]{2,1,0:T(8,128)(2,1)S(1)}, bf16[1,128,2560]{2,1,0:T(8,128)(2,1)}, u32[]{:S(2)}) copy-start(bf16[1,128,2560]{2,1,0:T(8,128)(2,1)} %param.16) | copy-start | bytes 1966084
  700.4 10.3 %copy-start.6 = (f32[128,2560]{1,0:T(8,128)S(1)}, f32[128,2560]{1,0:T(8,128)}, u32[]{:S(2)}) copy-start(f32[128,2560]{1,0:T(8,128)} %get-tuple-element.135) | copy-start | bytes 3932164
  700.4 10.3 %copy-start.14 = (f32[128,2560]{1,0:T(8,128)S(1)}, f32[128,2560]{1,0:T(8,128)}, u32[]{:S(2)}) copy-start(f32[128,2560]{1,0:T(8,128)} %get-tuple-element.93) | copy-start | bytes 3932164
  700.4 10.3 %copy-start.25 = (f32[2560]{0:T(1024)S(1)}, f32[2560]{0:T(1024)}, u32[]{:S(2)}) copy-start(f32[2560]{0:T(1024)} %get-tuple-element.126) | copy-start | bytes 30724
  700.4 10.3 %copy-start.29 = (f32[128]{0:T(128)S(1)}, f32[128]{0:T(128)}, u32[]{:S(2)}) copy-start(f32[128]{0:T(128)} %copy-done.28) | copy-start | bytes 1540
  700.4 10.3 %copy-start.31 = (f32[128]{0:T(128)S(1)}, f32[128]{0:T(128)}, u32[]{:S(2)}) copy-start(f32[128]{0:T(128)} %copy-done.30) | copy-start | bytes 1540
  700.4 10.3 %copy-start.32 = (f32[128]{0:T(128)S(1)}, f32[128]{0:T(128)}, u32[]{:S(2)}) copy-start(f32[128]{0:T(128)} %fusion.30) | copy-start | bytes 1540
  (19 other events, 42.4 us)

commit v5 on v4

--- a/solution.py
+++ b/solution.py
@@ -217,49 +217,60 @@
     return quarter
 
 
-def widen_kernel(*refs):
-    n = len(refs) // 2
-    for strips, out in zip(refs[:n], refs[n:]):
-        each = out.shape[1] // 8
-        for s in range(8):
-            first, last = s * each // 128, (s + 1) * each // 128
-            tiles = strips[s, 0].astype(jnp.float32)
-            if s * each % 128:
-                shared = strips[s - 1, 0, :, (first - (s - 1) * each // 128) * 128 :][:, :128]
-                out[:, first * 128 : first * 128 + 128] = tiles[:, :128] + shared.astype(jnp.float32)
-                first_full = first + 1
-            else:
-                first_full = first
-            base = s * each // 128
-            out[:, first_full * 128 : last * 128] = tiles[:, (first_full - base) * 128 : (last - base) * 128]
-
-
-def unpack_kernel(heads, packed, out):
+def unpacked(packed, heads):
     pieces = []
     for h in range(heads):
         first, k = h // 10 * 1024, h % 10
         pieces.append(packed[:, first + 64 * k : first + 64 * k + 64])
         pieces.append(packed[:, first + 640 + 32 * k : first + 672 + 32 * k])
-    out[...] = jnp.concatenate(pieces, axis=1).astype(jnp.float32)
-
-
-def unpack(packed, heads):
+    return jnp.concatenate(pieces, axis=1)
+
+
+def widen_kernel(heads, gate, up, down, attn_out, lat, latent_up, query_up, *outs):
+    wide = jnp.float32
+    for strips, out in zip((gate, up), outs[:2]):
+        each = out.shape[1] // 8
+        for s in range(8):
+            first, last = s * each // 128, (s + 1) * each // 128
+            tiles = strips[s, 0].astype(wide)
+            if s * each % 128:
+                shared = strips[s - 1, 0, :, (first - (s - 1) * each // 128) * 128 :][:, :128]
+                out[:, first * 128 : first * 128 + 128] = tiles[:, :128] + shared.astype(wide)
+                first_full = first + 1
+            else:
+                first_full = first
+            out[:, first_full * 128 : last * 128] = tiles[:, (first_full - first) * 128 : (last - first) * 128]
+    down_out, attn_out_out, query_down_out, latent_down_out, latent_up_out, query_up_out = outs[2:]
+    down_out[...] = down[...].astype(wide)
+    attn_out_out[...] = attn_out[...].astype(wide)
+    rank = query_down_out.shape[1]
+    query_down_out[...] = lat[0, :, :rank].astype(wide)
+    latent_down_out[...] = lat[0, :, rank:].astype(wide)
+
+    @pl.when(pl.program_id(0) == 0)
+    def _():
+        latent_up_out[...] = latent_up[...].astype(wide)
+        query_up_out[...] = unpacked(query_up[...], heads).astype(wide)
+
+
+def widen(gate, up, down, attn_out, lat, latent_up, query_up, cols, rank, heads):
+    _, quarters, rows, strip = gate.shape
+    width = attn_out.shape[1]
+    whole = lambda a: pl.BlockSpec(a, lambda q: (0, 0))
+    by_rows = lambda c: pl.BlockSpec((rows, c), lambda q: (q, 0))
+    by_cols = pl.BlockSpec((down.shape[0], width // quarters), lambda q: (0, q))
+    strips = pl.BlockSpec((8, 1, rows, strip), lambda q: (0, q, 0, 0))
+    shapes = [(quarters * rows, cols)] * 2 + [down.shape, attn_out.shape, (quarters * rows, rank),
+                                              (quarters * rows, lat.shape[2] - rank), latent_up.shape, (query_up.shape[0], heads * 96)]
     return pl.pallas_call(
-        functools.partial(unpack_kernel, heads),
-        out_shape=jax.ShapeDtypeStruct((packed.shape[0], heads * 96), jnp.float32), in_specs=[VMEM], out_specs=VMEM,
-    )(packed)
-
-
-def widen(arrays, cols):
-    _, quarters, rows, strip = arrays[0].shape
-    n = len(arrays)
-    return pl.pallas_call(
-        widen_kernel, grid=(quarters,),
-        out_shape=[jax.ShapeDtypeStruct((quarters * rows, cols), jnp.float32)] * n,
-        in_specs=[pl.BlockSpec((8, 1, rows, strip), lambda q: (0, q, 0, 0))] * n,
-        out_specs=[pl.BlockSpec((rows, cols), lambda q: (q, 0))] * n,
+        functools.partial(widen_kernel, heads), grid=(quarters,),
+        out_shape=[jax.ShapeDtypeStruct(s, jnp.float32) for s in shapes],
+        in_specs=[strips, strips, by_cols, by_rows(width), pl.BlockSpec((1,) + lat.shape[1:], lambda q: (q, 0, 0)),
+                  whole(latent_up.shape), whole(query_up.shape)],
+        out_specs=[by_rows(cols)] * 2 + [by_cols, by_rows(width), by_rows(rank), by_rows(lat.shape[2] - rank),
+                                         whole(latent_up.shape), whole(shapes[-1])],
         compiler_params=pltpu.CompilerParams(vmem_limit_bytes=56 * 2**20),
-    )(*arrays)
+    )(gate, up, down, attn_out, lat, latent_up, query_up)
 
 
 class Gather:
@@ -422,7 +433,7 @@
 
 
 def kernel_params(cid):
-    return pltpu.CompilerParams(collective_id=cid, has_side_effects=True, vmem_limit_bytes=56 * 2**20)
+    return pltpu.CompilerParams(collective_id=cid, has_side_effects=True, vmem_limit_bytes=58 * 2**20)
 
 
 VMEM = pl.BlockSpec(memory_space=pltpu.VMEM)
@@ -572,6 +583,39 @@
                 self.copy(i, m).wait_send()
                 if arrive:
                     self.copy(i, m, True).wait_recv()
+
+
+class Strips:
+    def __init__(self, own, whole, sems):
+        rep, zpos, core = place()
+        shard = zpos * 2 + core
+        self.swap = ColumnSwap([(lambda s: own.at[s], lambda s: whole.at[s, rep])], sems[:2] + [None], keeps=False)
+
+        def part(m):
+            return lambda p: whole.at[shard if m == 0 else column_place(zpos, core, m, True), p]
+
+        self.spread = PlaneGather([(None if m else own.at[shard], part(m), m % 2) for m in range(8)], sems[2:5])
+
+    @staticmethod
+    def scratch():
+        return [dma_sems(7, 1), dma_sems(7, 1)] + PlaneGather.scratch(8)
+
+    def start(self):
+        self.swap.start()
+        self.spread.start((0,))
+
+    def arrive(self, *places):
+        for m in places:
+            self.swap.arrive(m)
+            self.spread.start((m,))
+
+    def onward(self, *places):
+        for m in places:
+            self.spread.middle(m)
+
+    def finish(self):
+        self.swap.finish(arrive=False)
+        self.spread.finish()
 
 
 def quarter_cols(ref, first, rows, p):
@@ -682,13 +726,16 @@
 
 
 def middle_kernel(scale, *refs):
-    branch, cols, down, up, attn_out, query_low, latent_low = refs[:7]
-    query, kv, rope, bias, turns, logs = refs[7:13]
-    branch_all, cols_all, down_all, up_own = refs[13:17]
-    grad_query, grad_kv, grad_rope, query_up, latent_up = refs[17:22]
-    scratch = list(refs[22:])
-    left, mixed, packed, strips, strip_sems = scratch[:5]
-    scratch = scratch[5:]
+    gate, refs = refs[0], refs[1:]
+    branch, cols, down, up, attn_out, w_query_up, w_latent_up, query_low, latent_low = refs[:9]
+    query, kv, rope, bias, turns, logs = refs[9:15]
+    w_query, w_latent, tokens, query_lat, latent_proj, gains, grad_residual, gain_ffn = refs[15:23]
+    branch_all, cols_all, down_all, gate_all, up_own, query_up, latent_up, tokens_grad, lats, gain_terms = refs[23:33]
+    scratch = list(refs[33:])
+    (left, mixed, packed, grad_query, grad_kv, grad_rope, strips, query_strips, latent_strips, strip_sems, grad_low,
+     grad_latent, grad_normed, latent_send, rope_send, latent_land, rope_land, lsend, lrecv, query_rows, latent_rows,
+     row_sems) = scratch[:22]
+    scratch = scratch[22:]
     rep, zpos, core = place()
     shard = zpos * 2 + core
     gather = Gather((branch,), (branch_all,), scratch[:5])
@@ -697,93 +744,202 @@
     downs = PlaneGather(
         [(down.at[pl.ds(h * half, half)], functools.partial(quarter_cols, down_all, h * half, half), h) for h in range(2)],
         scratch[8:11])
-    bufs, sems, _ = PlaneSum.split(scratch[11:], 2)
+    strips_out = Strips(gate, gate_all, scratch[11:16])
+    bufs, sems, _ = PlaneSum.split(scratch[16:], 2)
     sums = PlaneSum([(lambda p, h=h: up.at[pl.ds(4 * h, 4), p], up_own.at[pl.ds(4 * h, 4)], h) for h in range(2)], bufs, sems)
-    rows = attn_out.shape[0] // 4
-
-    def strip(i):
-        return pltpu.make_async_copy(
-            attn_out.at[pl.ds(mult(i * rows, 128), rows)], strips.at[i % 2], strip_sems.at[i % 2])
-
-    strip(0).start()
-    greet(rep, zpos, core, plane=2, column=True)
-    gather.start()
+    rows = tokens.shape[0]
+    out_rows = attn_out.shape[0] // 4
+    quarter_width = kv.shape[1] // 4
+    wide, low = jnp.float32, jnp.bfloat16
+
+    def strip(i, k):
+        at = pl.ds(mult(i * quarter_width, 128), quarter_width)
+        src = (attn_out.at[pl.ds(mult(i * out_rows, 128), out_rows)], w_query_up.at[:, at], w_latent_up.at[:, at])[k]
+        return pltpu.make_async_copy(src, (strips, query_strips, latent_strips)[k].at[i % 2], strip_sems.at[i % 2, k])
+
+    def share(k, what):
+        for i, (src, dst) in enumerate(((latent_send, latent_land), (rope_send, rope_land))):
+            getattr(remote(src.at[pl.ds((k + 1) * rows, rows)], dst.at[k], lsend.at[k, i], lrecv.at[k, i],
+                           plane_places(rep)[k], shard), what)()
+
+    for k in range(3):
+        strip(0, k).start()
+    greet(rep, zpos, core, plane=3, column=True)
+    strips_out.start()
     sums.start()
     downs.start()
-    swap.start()
     left[...] = jnp.zeros_like(left)
     grad_rope[...] = jnp.zeros_like(grad_rope)
+    grad_low[...] = jnp.zeros_like(grad_low)
+    grad_latent[...] = jnp.zeros_like(grad_latent)
     quarter = attend_back_heads(
         scale, query, kv, rope, bias, turns, logs, mixed, grad_query, packed, grad_kv, grad_rope, left)
 
+    def after_first():
+        gather.start()
+        swap.start()
+        strips_out.arrive(1, 2, 6)
+
     def after_second():
-        gather.hop(1)
+        strips_out.arrive(3, 7, 4, 5)
         sums.middle(0)
         sums.middle(1)
 
+    def after_third():
+        gather.hop(1)
+        downs.middle(0)
+        downs.middle(1)
+        strips_out.onward(0, 1, 2)
+
     def after_fourth():
         gather.hop(2)
-        downs.middle(0)
-        downs.middle(1)
+        strips_out.onward(6, 3)
 
     def step(i, carry):
-        strip(i).wait()
+        for k in range(3):
+            strip(i, k).wait()
 
         @pl.when(i < 3)
         def _():
-            strip(i + 1).start()
-
-        mixed[:, pl.ds(mult(i * rows, 128), rows)] = dot_nt(branch[...], strips[i % 2]).astype(mixed.dtype)
+            for k in range(3):
+                strip(i + 1, k).start()
+
+        mixed[:, pl.ds(mult(i * out_rows, 128), out_rows)] = dot_nt(branch[...], strips[i % 2]).astype(mixed.dtype)
         quarter(i, carry)
-        pl.when(i == 1)(after_second)
-        pl.when(i == 3)(after_fourth)
+        at = pl.ds(mult(i * quarter_width, 128), quarter_width)
+        grad_low[...] += dot_nt(grad_query[:, at], query_strips[i % 2])
+        grad_latent[...] += dot_nt(grad_kv[:, at], latent_strips[i % 2])
+        for k, service in enumerate((after_first, after_second, after_third, after_fourth)):
+            pl.when(i == k)(service)
         return carry
 
     lax.fori_loop(0, 4, step, 0)
+    latent_send[...] = grad_latent[...].astype(low)
+    rope_send[...] = grad_rope[...].astype(low)
+    for k in range(3):
+        share(k, "start")
 
     def terms(i, carry):
         at = pl.ds(mult(i * 1024, 128), 1024)
         query_up[:, at] = dot_tn(query_low[...], packed[:, at]).astype(query_up.dtype)
-        width = latent_up.shape[1] // 4
-        at = pl.ds(mult(i * width, 128), width)
+        at = pl.ds(mult(i * quarter_width, 128), quarter_width)
         latent_up[:, at] = dot_tn(latent_low[...], grad_kv[:, at]).astype(latent_up.dtype)
         return carry
 
     lax.fori_loop(0, 4, terms, 0)
+    strips_out.onward(7, 4, 5)
     sums.end(0)
     sums.end(1)
+
+    def tile(t):
+        return slice(128 * t, 128 * t + 128)
+
+    def norm_back(src, grad, tiles, first, put):
+        square = sum(jnp.sum(jnp.square(src(t)), axis=1, keepdims=True) for t in range(tiles))
+        factor = lax.rsqrt(square / (128 * tiles) + epsilon)
+        along = jnp.zeros_like(factor)
+        for t in range(tiles):
+            unit = src(t) * factor
+            weighed = grad(t) * unit
+            gain_terms[first + t : first + t + 1, :] = jnp.sum(weighed, axis=0, keepdims=True)
+            along = along + jnp.sum(weighed * gains[first + t : first + t + 1, :], axis=1, keepdims=True)
+        along = along / (128 * tiles)
+        for t in range(tiles):
+            put(t, factor * (grad(t) * gains[first + t : first + t + 1, :] - src(t) * factor * along))
+
+    def put_query(t, value):
+        lats[:, tile(t)] = value.astype(low)
+
+    def put_latent(t, value):
+        lats[:, tile(6 + t)] = value.astype(low)
+
+    def put_tokens(t, value):
+        tokens_grad[:, tile(t)] = (grad_residual[:, tile(t)] + value).astype(low)
+
+    norm_back(lambda t: query_lat[:, tile(t)], lambda t: grad_low[:, tile(t)], 6, 40, put_query)
+    own = grad_latent[0:rows].astype(low).astype(wide)
+    own_rope = grad_rope[0:rows].astype(low).astype(wide)
+    for k in range(3):
+        share(k, "wait_recv")
+        own = own + latent_land[k].astype(wide)
+        own_rope = own_rope + rope_land[k].astype(wide)
+    grad_latent[0:rows] = own
+    norm_back(lambda t: latent_proj[:, tile(t)], lambda t: grad_latent[0:rows, tile(t)], 2, 46, put_latent)
+    turned = turn(own_rope, (turns[0], turns[1], turns[2]), True)
+    lats[:, 1024:1056] = turned[:, 64:96].astype(low)
+    chunk = query_rows.shape[1]
+    chunks = w_query.shape[0] // chunk
+
+    def row_copy(i, k):
+        at = pl.ds(mult(i * chunk, chunk), chunk)
+        return pltpu.make_async_copy((w_query, w_latent)[k].at[at], (query_rows, latent_rows)[k].at[i % 2], row_sems.at[i % 2, k])
+
+    def normed_step(i, carry):
+        for k in range(2):
+            row_copy(i, k).wait()
+
+        @pl.when(i < chunks - 1)
+        def _():
+            for k in range(2):
+                row_copy(i + 1, k).start()
+
+        grad_normed[:, pl.ds(mult(i * chunk, chunk), chunk)] = (
+            dot_nt(lats[:, :768], query_rows[i % 2]) + dot_nt(lats[:, 768:1056], latent_rows[i % 2]))
+        return carry
+
+    for k in range(2):
+        row_copy(0, k).start()
+    lax.fori_loop(0, chunks, normed_step, 0)
+    norm_back(lambda t: tokens[:, tile(t)].astype(wide), lambda t: grad_normed[:, tile(t)], 20, 0, put_tokens)
+    gain_terms[20:40, :] = gain_ffn[...]
     gather.hop(3)
+    for k in range(3):
+        share(k, "wait_send")
     gather.finish()
     swap.finish()
     downs.finish()
     sums.finish()
-
-
-def middle_exchange(cid, scale, branch, cols, down, up, attn_out, query_low, latent_low, attend_in):
+    strips_out.finish()
+
+
+def middle_exchange(cid, scale, gate, branch, cols, down, up, weights, query_low, latent_low, attend_in, norm_in):
     kind = branch.dtype
+    wide = jnp.float32
     query, kv, rope = attend_in[:3]
-    rows = query.shape[0]
+    rows, width = branch.shape
+    attn_out, w_query_up, w_latent_up, w_query, w_latent = weights
+    keys, latent_rank = latent_low.shape
+    query_rank = query_low.shape[1]
+    quarter = kv.shape[1] // 4
+    gains = norm_in[3]
     return pl.pallas_call(
         functools.partial(middle_kernel, scale),
-        out_shape=[jax.ShapeDtypeStruct((8 * branch.shape[0], branch.shape[1]), kind), jax.ShapeDtypeStruct(cols.shape, kind),
-                   jax.ShapeDtypeStruct((down.shape[0], 4 * down.shape[1]), kind), jax.ShapeDtypeStruct((8,) + up.shape[2:], kind),
-                   jax.ShapeDtypeStruct(query.shape, kind),
-                   jax.ShapeDtypeStruct(kv.shape, kind), jax.ShapeDtypeStruct(rope.shape, jnp.float32),
-                   jax.ShapeDtypeStruct((query_low.shape[1], 4096), kind),
-                   jax.ShapeDtypeStruct((latent_low.shape[1], kv.shape[1]), kind)],
-        in_specs=[VMEM] + [ANY] * 2 + [VMEM, ANY] + [VMEM] * 8, out_specs=[ANY] * 3 + [VMEM] * 6,
+        out_shape=[jax.ShapeDtypeStruct((8 * rows, width), kind), jax.ShapeDtypeStruct(cols.shape, kind),
+                   jax.ShapeDtypeStruct((down.shape[0], 4 * down.shape[1]), kind),
+                   jax.ShapeDtypeStruct((8, 4) + gate.shape[1:], kind), jax.ShapeDtypeStruct((8,) + up.shape[2:], kind),
+                   jax.ShapeDtypeStruct((query_rank, 4096), kind), jax.ShapeDtypeStruct((latent_rank, kv.shape[1]), kind),
+                   jax.ShapeDtypeStruct((rows, width), kind),
+                   jax.ShapeDtypeStruct((rows, query_rank + w_latent.shape[1]), kind), jax.ShapeDtypeStruct(gains.shape, wide)],
+        in_specs=[ANY, VMEM] + [ANY] * 2 + [VMEM] + [ANY] * 3 + [VMEM] * 8 + [ANY] * 2 + [VMEM] * 6,
+        out_specs=[ANY] * 4 + [VMEM] * 6,
         scratch_shapes=[pltpu.VMEM((2 * rows, 256), kind), pltpu.VMEM(branch.shape, kind), pltpu.VMEM((rows, 4096), kind),
-                        pltpu.VMEM((2, attn_out.shape[0] // 4, attn_out.shape[1]), kind), dma_sems(2)]
-        + Gather.scratch(1) + ColumnSwap.scratch(1) + PlaneGather.scratch(2)
+                        pltpu.VMEM(query.shape, kind), pltpu.VMEM(kv.shape, kind), pltpu.VMEM(rope.shape, wide),
+                        pltpu.VMEM((2, attn_out.shape[0] // 4, width), kind), pltpu.VMEM((2, query_rank, quarter), kind),
+                        pltpu.VMEM((2, latent_rank, quarter), kind), dma_sems(2, 3),
+                        pltpu.VMEM((rows, query_rank), wide), pltpu.VMEM((keys, latent_rank), wide), pltpu.VMEM((rows, width), wide),
+                        pltpu.VMEM((keys, latent_rank), kind), pltpu.VMEM((keys, 128), kind),
+                        pltpu.VMEM((3, rows, latent_rank), kind), pltpu.VMEM((3, rows, 128), kind), dma_sems(3, 2), dma_sems(3, 2),
+                        pltpu.VMEM((2, width // 5, query_rank), kind), pltpu.VMEM((2, width // 5, w_latent.shape[1]), kind), dma_sems(2, 2)]
+        + Gather.scratch(1) + ColumnSwap.scratch(1) + PlaneGather.scratch(2) + Strips.scratch()
         + PlaneSum.scratch([(4,) + up.shape[2:]] * 2, kind),
         compiler_params=kernel_params(cid),
-    )(branch, cols, down, up, attn_out, query_low, latent_low, *attend_in)
+    )(gate, branch, cols, down, up, attn_out, w_query_up, w_latent_up, query_low, latent_low, *attend_in, w_query, w_latent, *norm_in)
 
 
 def last_kernel(*refs):
-    gate, up, lat, query_up, latent_up, hidden, down, attn_out, cols, gain = refs[:10]
-    gate_all, up_all, out, attn_sum, lat_sum, latent_sum, query_sum, gain_out = refs[10:18]
-    scratch = list(refs[18:])
+    up, lat, query_up, latent_up, hidden, down, attn_out, cols, gain = refs[:9]
+    up_all, out, attn_sum, lat_sum, latent_sum, query_sum, gain_out = refs[9:16]
+    scratch = list(refs[16:])
     rep, zpos, core = place()
     shard = zpos * 2 + core
     places = plane_places(rep)
@@ -793,8 +949,7 @@
         got, scratch = scratch[:n], scratch[n:]
         return got
 
-    swap = ColumnSwap([(lambda s, a=a: a.at[s], lambda s, b=b: b.at[s, rep]) for a, b in ((gate, gate_all), (up, up_all))],
-                      take(2) + [None], keeps=False)
+    strips_out = Strips(up, up_all, take(5))
     spread_sems = take(3)
     lat_all, out_term, lat_term, query_part, latent_own, query_own = take(6)
     gather = Gather((lat,), (lat_all,), take(5))
@@ -807,9 +962,6 @@
     width = query_up.shape[2] // 4
     half = attn_out.shape[0] // 2
 
-    def part(m, b):
-        return lambda p: b.at[shard if m == 0 else column_place(zpos, core, m, True), p]
-
     def query_item(h):
         return (lambda p: query_up.at[pl.ds(4 * h, 4), :, pl.ds(mult(p * width, 128), width)], query_part.at[pl.ds(4 * h, 4)], h)
 
@@ -821,15 +973,14 @@
            (functools.partial(quarter_cols, latent_low, 0, latent_low.shape[0]), owns[3], 1)],
         bufs, sems)
     spread = PlaneGather(
-        [(a.at[shard] if m == 0 else None, part(m, b), h) for m in range(8) for h, (a, b) in enumerate(((gate, gate_all), (up, up_all)))]
-        + [(owns[h], functools.partial(quarter_cols, attn_sum, h * half, half), h) for h in range(2)]
+        [(owns[h], functools.partial(quarter_cols, attn_sum, h * half, half), h) for h in range(2)]
         + [(owns[2], lambda p: lat_sum.at[p], 0),
            (owns[3], functools.partial(quarter_cols, latent_sum, 0, latent_low.shape[0]), 1),
            (owns[4], functools.partial(quarter_cols, query_sum, 0, query_up.shape[1]), 0)], spread_sems)
 
     def gain_copy(m):
         s2 = column_place(zpos, core, m)
-        return remote(gain.at[s2], gain_landed.at[m - 1], gsend.at[m - 1], grecv.at[m - 1], rep, s2)
+        return remote(gain, gain_landed.at[m - 1], gsend.at[m - 1], grecv.at[m - 1], rep, s2)
 
     def gain_on(k):
         return remote(gain_sum, gain_plane.at[k], hsend.at[k], hrecv.at[k], places[k], shard)
@@ -837,9 +988,8 @@
     greet(rep, zpos, core, plane=3, column=True)
     for m in range(1, 8):
         gain_copy(m).start()
-    swap.start()
+    strips_out.start()
     sums.start((0, 1))
-    spread.start((0, 1))
     latent_total.start()
     gather.start()
     sums.start((2, 3))
@@ -850,15 +1000,7 @@
                               preferred_element_type=jnp.float32).astype(out_term.dtype)
         return carry
 
-    def arrive(m):
-        swap.arrive(m)
-        spread.start((2 * m, 2 * m + 1))
-
-    def onward(*ms):
-        for m in ms:
-            spread.middle(2 * m)
-            spread.middle(2 * m + 1)
-
+    arrive, onward = strips_out.arrive, strips_out.onward
     lax.fori_loop(0, 3, term, 0)
     arrive(1)
     latent_total.pair()
@@ -870,7 +1012,7 @@
     arrive(6)
     lax.fori_loop(6, 8, term, 0)
     latent_total.step(1)
-    gain_sum[...] = gain[shard]
+    gain_sum[...] = gain[...]
     for m in range(1, 8):
         gain_copy(m).wait_recv()
         gain_sum[...] += gain_landed[m - 1]
@@ -907,7 +1049,7 @@
     total.step(1)
     sums.end(2)
     sums.end(3)
-    spread.start((16, 17))
+    spread.start((0, 1))
     query_total.step(1)
     onward(4, 5)
     sums.middle(5)
@@ -916,12 +1058,12 @@
     total.step(2)
     query_total.finish()
     owns[4][...] = query_own[...].astype(owns[4].dtype)
-    spread.start((20,))
+    spread.start((4,))
     sums.end(5)
-    spread.start((19,))
+    spread.start((3,))
     sums.end(4)
-    spread.start((18,))
-    for i in (16, 17, 20, 19, 18):
+    spread.start((2,))
+    for i in (0, 1, 4, 3, 2):
         spread.middle(i)
     gain_out[...] = gain_sum[...]
     for k in range(3):
@@ -932,13 +1074,13 @@
         gain_on(k).wait_send()
     for m in range(1, 8):
         gain_copy(m).wait_send()
-    swap.finish(arrive=False)
+    strips_out.finish()
     sums.finish()
     spread.finish()
 
 
-def last_sums(cid, gate, up, lat, query_up, latent_up, hidden, down, attn_out, cols, gain):
-    kind = gate.dtype
+def last_sums(cid, up, lat, query_up, latent_up, hidden, down, attn_out, cols, gain):
+    kind = up.dtype
     wide = jnp.float32
     rows = lat.shape[0]
     lat_shape = (4, cols.shape[1] // 4, lat.shape[1])
@@ -949,21 +1091,21 @@
     query_part = jax.ShapeDtypeStruct((8,) + query_shape, kind)
     return pl.pallas_call(
         last_kernel,
-        out_shape=[jax.ShapeDtypeStruct((8, 4) + gate.shape[1:], kind)] * 2
+        out_shape=[jax.ShapeDtypeStruct((8, 4) + up.shape[1:], kind)]
         + [jax.ShapeDtypeStruct(out_term.shape[1:], wide)]
         + [jax.ShapeDtypeStruct(s, kind) for s in (attn_out.shape, lat_shape, latent_up.shape[1:])]
-        + [jax.ShapeDtypeStruct((query_up.shape[1], query_up.shape[2]), kind), jax.ShapeDtypeStruct(gain.shape[1:], gain.dtype)],
-        in_specs=[ANY] * 3 + [VMEM] * 7, out_specs=[ANY] * 2 + [VMEM] + [ANY] * 4 + [VMEM],
-        scratch_shapes=[dma_sems(7, 2), dma_sems(7, 2)] + PlaneGather.scratch(21)
+        + [jax.ShapeDtypeStruct((query_up.shape[1], query_up.shape[2]), kind), jax.ShapeDtypeStruct(gain.shape, gain.dtype)],
+        in_specs=[ANY] * 2 + [VMEM] * 7, out_specs=[ANY, VMEM] + [ANY] * 4 + [VMEM],
+        scratch_shapes=Strips.scratch() + PlaneGather.scratch(5)
         + [pltpu.VMEM((8 * rows, lat.shape[1]), kind), pltpu.VMEM(out_term.shape, kind), pltpu.VMEM(lat_shape, kind),
            pltpu.VMEM(query_part.shape, kind), pltpu.VMEM(latent_up.shape[1:], wide), pltpu.VMEM(query_shape, wide)]
         + Gather.scratch(1) + [pltpu.VMEM(s, kind) for s in shapes + [query_shape]]
-        + [pltpu.VMEM((7,) + gain.shape[1:], wide), pltpu.VMEM(gain.shape[1:], wide), pltpu.VMEM((3,) + gain.shape[1:], wide)]
+        + [pltpu.VMEM((7,) + gain.shape, wide), pltpu.VMEM(gain.shape, wide), pltpu.VMEM((3,) + gain.shape, wide)]
         + [dma_sems(7)] * 2 + [dma_sems(3)] * 2
         + Total.scratch(out_term) + Total.scratch(query_part) + Total.scratch(latent_up)
         + PlaneSum.scratch([(4,) + query_shape] * 2 + shapes, kind) + [pltpu.VMEM(latent_up.shape[1:], kind)],
         compiler_params=kernel_params(cid),
-    )(gate, up, lat, query_up, latent_up, hidden, down, attn_out, cols, gain)
+    )(up, lat, query_up, latent_up, hidden, down, attn_out, cols, gain)
 
 
 def start_kernel(scale, *refs):
@@ -1494,19 +1636,8 @@
         turns,
         down_w,
     )
-    gains_all = jnp.sum(small_all.reshape(8, -1), axis=0)
-    gain_in, gain_f = gains_all[:width], gains_all[width : 2 * width]
-    gain_q = gains_all[2 * width : 2 * width + query_down.shape[1]]
-    gain_l = gains_all[2 * width + query_down.shape[1] :]
-
-    def key_rotate(values):
-        return rotate(values, cos_part, sin_part)
-
-    inputs = tokens[0].astype(wide)
-    norm_in_back = jax.vjp(rms_scale, inputs, gain_in)[1]
-    norm_q_back = jax.vjp(rms_scale, query_lat, gain_q)[1]
-    norm_l_back = jax.vjp(rms_scale, latent_proj[:, :KR], gain_l)[1]
-    key_back = jax.vjp(key_rotate, latent_proj[:, KR:])[1]
+    gains_all = jnp.sum(small_all.reshape((8,) + small.shape), axis=0)
+    gain_f = gains_all[width // 128 : 2 * width // 128].reshape(-1)
     norm_f_back = jax.vjp(rms_scale, residual, gain_f)[1]
 
     gate_pre = jnp.dot(ffn_all, gate_w, preferred_element_type=wide)
@@ -1529,56 +1660,40 @@
         branch_all,
         cols_all,
         down_all,
+        gate_all,
         up_own,
-        grad_q_proj,
-        grad_kv,
-        grad_rope,
         qup_part,
         lup_part,
+        tokens_grad,
+        grad_lats,
+        gain_terms,
     ) = middle_exchange(
         3,
         scale,
+        gate_own,
         grad_branch,
         cols,
         down_own,
         up_part,
-        aout,
+        (aout, qup, lup, qdown, ldown),
         query_low,
         latent_low,
         (queries, keyvals, rope_tile, bias, turns, logs),
-    )
-    down_grad = down_all.astype(wide)
-    rope_sum = grad_rope[:, ND:head_dim]
-    grad_lat_part = jnp.concatenate([outer_cols(grad_kv, lup), rope_sum], axis=1).astype(low)
-    grad_lat_own = grad_lat_part[:rows].astype(wide)
-    for j in range(1, 4):
-        grad_lat_own = grad_lat_own + plane_swap(
-            grad_lat_part[j * rows : (j + 1) * rows], j
-        ).astype(wide)
-    grad_q_lat_f, grad_gain_query = norm_q_back(outer_cols(grad_q_proj, qup))
-    grad_q_lat = grad_q_lat_f.astype(low)
-    grad_lat_c, grad_gain_latent = norm_l_back(grad_lat_own[:, :KR])
-    grad_lat_r = key_back(grad_lat_own[:, KR:])[0]
-    grad_lat = jnp.concatenate([grad_lat_c, grad_lat_r], axis=1).astype(low)
-    grad_normed = outer_cols(grad_q_lat, qdown) + outer_cols(grad_lat, ldown)
-    grad_in_norm, grad_gain_attn = norm_in_back(grad_normed)
-    tokens_grad = (grad_resid + grad_in_norm).astype(low)
-
-    grad_lats = jnp.concatenate([grad_q_lat, grad_lat], axis=1)
+        (
+            tokens[0],
+            query_lat,
+            latent_proj,
+            gains_all,
+            grad_resid,
+            grad_gain_ffn.reshape(-1, 128),
+        ),
+    )
+
     mixed_cols = cols_all[:, 0].reshape(8 * rows, width // 8)
     normed_cols = cols_all[:, 1].reshape(8 * rows, width // 8)
     aout_part = inner_rows(mixed_cols, branch_all).astype(low)
-    gains = jnp.concatenate(
-        [
-            v.reshape(8, -1)
-            for v in (grad_gain_attn, grad_gain_ffn, grad_gain_query, grad_gain_latent)
-        ]
-        + [jnp.zeros((8, 1024 - 768), wide)],
-        axis=1,
-    ).reshape(8, 8, 128)
-    gate_all, up_all, out_sum, aout_own, lat_own, lup_own, qup_own, gain_own = last_sums(
+    up_all, out_sum, aout_own, lat_own, lup_own, qup_own, gain_own = last_sums(
         4,
-        gate_own,
         up_own,
         grad_lats,
         qup_part.reshape(8, -1, qup_part.shape[1]),
@@ -1587,28 +1702,31 @@
         down_w,
         aout_part,
         normed_cols,
-        gains,
+        gain_terms,
     )
     layer_out = (residual + residual_scale * out_sum).astype(low)
-    gate_grad, up_grad = widen((gate_all, up_all), FF)
-    aout_own = aout_own.astype(wide)
-    lat_own = lat_own.reshape(320, -1).astype(wide)
-    lup_own = lup_own.astype(wide)
-    qup_own = unpack(qup_own, H)
-    gain_own = gain_own.reshape(1024)
+    query_rank = query_down.shape[1]
+    gate_grad, up_grad, down_grad, aout_own, qdown_own, ldown_own, lup_own, qup_own = widen(
+        gate_all, up_all, down_all, aout_own, lat_own, lup_own, qup_own, FF, query_rank, H
+    )
+    gain_own = gain_own.reshape(-1)
+    owned, first = [], 0
+    for v in gain_list:
+        owned.append(lax.dynamic_slice(gain_own, (first + shard * v.shape[0],), (v.shape[0],)))
+        first += 8 * v.shape[0]
 
     return (
         layer_out[None],
         tokens_grad[None],
-        gain_own[:320],
-        lat_own[:, : query_down.shape[1]],
-        gain_own[640:736],
+        owned[0],
+        qdown_own,
+        owned[2],
         qup_own,
-        lat_own[:, query_down.shape[1] :],
-        gain_own[736:768],
+        ldown_own,
+        owned[3],
         lup_own,
         aout_own,
-        gain_own[320:640],
+        owned[1],
         gate_grad,
         up_grad,
         down_grad,

time: 721 us -> 688 us (0.954)
  matrix products: 46.6 us -> 30.4 us
  other arithmetic: 34.7 us -> 21.3 us
    pallas_call x1, Pallas kernels: 95.2 us -> 134 us  [middle_exchange(): pl.pallas_call(functools.partial(middle_kernel, scale), out_shape=[jax.Sh...]
    pallas_call x3 -> x2, Pallas kernels: 203 us -> 171 us  [the longest x1 155 us: last_sums(): pl.pallas_call(last_kernel, out_shape=[jax.ShapeDtypeStruct((8, 4) + up.s...]
    dot_general x4 -> x0, matrix products: 16.7 us -> none  [outer_cols(): lax.dot_general(leading, trailing, (((1,), (1,)), ((), ())), preferred_el...]
    convert_element_type x5 -> x0, other arithmetic: 12.4 us -> none  [the longest x1 6.67 us: column_body(): down_grad = down_all.astype(wide)]
    slice x9 -> x0, local copies, waits for them, and re-layouts: 7.32 us -> none  [the longest x1 1.4 us: column_body(): gain_own[320:640]]
  transfers between devices with their start and end apart: 3 -> 0, of which waited for: 0 -> 0; matrix products, arithmetic and copies ran while one was open for 3% -> 0% of each run, Pallas kernels for 0% -> 0%
where the time goes in v5:
time: 688 us; the launch traced here: 680 us
  Pallas kernels  607 us (88%)
  matrix products  30.4 us (4%)
  other arithmetic  21.3 us (3%)
  local copies, waits for them, and re-layouts  20.4 us (3%)
    pallas_call x1, Pallas kernels, start_gather(): pl.pallas_call(functools.partial(start_kernel, scale), out_shape=out, in_...  215 us
    pallas_call x1, Pallas kernels, last_sums(): pl.pallas_call(last_kernel, out_shape=[jax.ShapeDtypeStruct((8, 4) + up.s...  155 us
    pallas_call x1, Pallas kernels, middle_exchange(): pl.pallas_call(functools.partial(middle_kernel, scale), out_shape=[jax.Sh...  134 us
    pallas_call x1, Pallas kernels, back_sums(): pl.pallas_call(functools.partial(back_kernel, rows % 128), out_shape=[jax...  86.8 us
    pallas_call x1, Pallas kernels, widen(): pl.pallas_call(functools.partial(widen_kernel, heads), grid=(quarters,),...  16.2 us

profile of v5, /device:TPU:0, one launch (start us, length us, event | category | flops | bytes accessed | tf_op | source)
XLA Modules:
  0.0 680.2 jit_solution(6804001113774532624)
XLA Ops:
  0.7 0.9 reduce-window.4
  4.2 0.8 convert_dynamic-update-slice_fusion
  4.9 0.8 convert_dynamic-update-slice_fusion.1
  7.5 1.8 copy.44.refs_2_
  9.3 0.8 and_select_fusion.refs_10_.refs_13_
  10.1 2.0 fusion.4.refs_5_
  12.2 1.5 reshape.110
  13.9 1.1 copy.52
  15.3 1.1 copy-done.2
  16.9 2.1 copy-done
  19.0 215.4 %shard_map.254 = (bf16[2560,2560]{1,0:T(8,128)(2,1)}, bf16[2560,768]{1,0:T(8,128)(2,1)}, bf16[2560,288]{1,0:T(8,128)(2,1)}, bf16[768,5120]{1,0:T(8,128)(2,1)}, b...) custom-call(bf16[320,2560]{1,0:T(8,128)(2,1)} %refs_0_.1, ...), custom_call_target="tpu_custom_call" | custom-call | tf_op jit(solution)/shard_map/pallas_call | solution.py:1526
  234.4 1.6 multiply_reduce_fusion.2
  236.0 1.0 reduce_sum.74.refs_21_
  237.0 1.4 copy.45
  239.5 1.4 maximum_bitcast_fusion.refs_2_
  241.0 9.6 %fusion.11 = f32[1024,896]{1,0:T(8,128)S(1)} fusion(bf16[1024,2560]{1,0:T(8,128)(2,1)} %get-tuple-element.66.refs_1_, bf16[2560,896]{1,0:T(8,128)(2,1)} %get-tuple-element.68.refs_5_), kind=kOutput, calls=%fused_computation.55 | convolution fusion | flops 4697620480 | bytes 13500416 | tf_op jit(solution)/shard_map/dot_general | solution.py:1644
  250.7 8.4 %multiply_convert_fusion = (bf16[1024,896]{1,0:T(8,128)(2,1)}, bf16[1024,896]{1,0:T(8,128)(2,1)}, bf16[1024,896]{1,0:T(8,128)(2,1)S(1)}) fusion(f32[1024,896]{1,0:T(8,128)S(1)} %copy-done.9, f32[1024,896]{1,0:T(8,128)S(1)} %fusion.11, bf16[1024,2560]{1,0:T(8,128)(2,1)S(1)} %bitcast.52, bf16[2560,896]{1,0:T(8,128)(2,1)S(1)} %bitcast.54), kind=kOutput, calls=%fused_computation.6 | convolution fusion | flops 4712300544 | bytes 22675456 | tf_op jit(solution)/shard_map/dot_general | solution.py:1643
  259.1 6.8 %convolution_convert_fusion.refs_0_ = bf16[896,2560]{1,0:T(8,128)(2,1)} fusion(bf16[1024,896]{1,0:T(8,128)(2,1)S(1)} %get-tuple-element.178.refs_4_, bf16[1024,2560]{1,0:T(8,128)(2,1)S(1)} %bitcast.73), kind=kOutput, calls=%fused_computation.1 | convolution fusion | flops 4699914240 | bytes 11665408 | tf_op jit(solution)/shard_map/dot_general | solution.py:58
  266.0 86.8 %shard_map.255 = (f32[128,2560]{1,0:T(8,128)}, bf16[800,640]{1,0:T(8,128)(2,1)}, bf16[8,80,896]{2,1,0:T(8,128)(2,1)}, bf16[8,4,80,896]{3,2,1,0:T(8,128)(2,1)}) custom-call(bf16[896,2560]{1,0:T(8,128)(2,1)} %convolution_convert_fusion.refs_0_, bf16[1024,2560]{1,0:T(8,128)(2,1)} %get-tuple-element.66.refs_1_, bf16[1024,896]{1,0:T(8,128)(2,1)} %get-tuple-element.177.refs_2_, ...), custom_call_target="tpu_custom_call" | custom-call | tf_op jit(solution)/shard_map/pallas_call | solution.py:716
  352.8 2.3 multiply_reduce_fusion
  355.1 3.2 multiply_convert_fusion.2
  358.3 133.9 %shard_map.256 = (bf16[1024,2560]{1,0:T(8,128)(2,1)}, bf16[8,2,128,320]{3,2,1,0:T(8,128)(2,1)}, bf16[800,2560]{1,0:T(8,128)(2,1)}, bf16[8,4,80,896]{3,2,1,0:T(8,...) custom-call(bf16[8,80,896]{2,1,0:T(8,128)(2,1)} %get-tuple-element.7, ...), custom_call_target="tpu_custom_call" | custom-call | tf_op jit(solution)/shard_map/pallas_call | solution.py:915
  492.3 2.4 fusion.9
  494.7 5.5 convolution_convert_fusion.1.refs_6_
  500.2 154.5 %shard_map.257 = (bf16[8,4,80,896]{3,2,1,0:T(8,128)(2,1)}, f32[128,2560]{1,0:T(8,128)}, bf16[320,2560]{1,0:T(8,128)(2,1)}, bf16[4,80,1056]{2,1,0:T(8,128)(2,1)},...) custom-call(bf16[8,80,896]{2,1,0:T(8,128)(2,1)} %get-tuple-element.91.refs_0_, ...), custom_call_target="tpu_custom_call" | custom-call | tf_op jit(solution)/shard_map/pallas_call | solution.py:1092
  654.8 2.3 fusion.5
  657.1 1.3 dynamic_slice.14
  658.3 1.3 dynamic_slice.13
  659.6 1.4 fusion.10
  660.9 16.2 %shard_map.258 = (f32[320,6400]{1,0:T(8,128)}, f32[320,6400]{1,0:T(8,128)}, f32[800,2560]{1,0:T(8,128)}, f32[320,2560]{1,0:T(8,128)}, f32[320,768]{1,0:T(8,128)}...) custom-call(bf16[8,4,80,896]{3,2,1,0:T(8,128)(2,1)} %get-tuple-element.101.gate, ...), custom_call_target="tpu_custom_call" | custom-call | tf_op jit(solution)/shard_map/pallas_call | solution.py:265
  677.2 2.0 copy.49
  679.2 0.8 copy.60
  (68 shorter events, 6.5 us)
Async XLA Ops:
  0.6 11.5 %copy-start.5 = (bf16[96,3840]{1,0:T(8,128)(2,1)S(1)}, bf16[96,3840]{1,0:T(8,128)(2,1)}, u32[]{:S(2)}) copy-start(bf16[96,3840]{1,0:T(8,128)(2,1)} %param.21) | copy-start | bytes 2211844
  13.9 2.5 copy-start.2
  16.9 2.1 copy-start
  234.4 4.4 copy-start.7
  236.9 4.0 copy-start.8
  239.5 11.1 %slice-start = ((s8[5242880]{0:T(1024)(128)(4,1)}), s8[4194304]{0:T(1024)(128)(4,1)S(1)}, s32[]{:S(2)}) async-start(s8[5242880]{0:T(1024)(128)(4,1)} %bitcast.51), calls=%async_computation | async-start | bytes 8388608
  239.5 11.1 %slice-start.2 = ((s8[4587520]{0:T(1024)(128)(4,1)}), s8[4194304]{0:T(1024)(128)(4,1)S(1)}, s32[]{:S(2)}) async-start(s8[4587520]{0:T(1024)(128)(4,1)} %bitcast.53), calls=%async_computation.2 | async-start | bytes 8388608
  241.0 9.7 %slice-start.1 = ((s8[5242880]{0:T(1024)(128)(4,1)}), s8[1048576]{0:T(1024)(128)(4,1)S(1)}, s32[]{:S(2)}) async-start(s8[5242880]{0:T(1024)(128)(4,1)} %bitcast.51), calls=%async_computation.1 | async-start | bytes 2097152
  241.0 9.7 %slice-start.3 = ((s8[4587520]{0:T(1024)(128)(4,1)}), s8[393216]{0:T(1024)(128)(4,1)S(1)}, s32[]{:S(2)}) async-start(s8[4587520]{0:T(1024)(128)(4,1)} %bitcast.53), calls=%async_computation.3 | async-start | bytes 786432
  241.0 9.7 %copy-start.9 = (f32[1024,896]{1,0:T(8,128)S(1)}, f32[1024,896]{1,0:T(8,128)}, u32[]{:S(2)}) copy-start(f32[1024,896]{1,0:T(8,128)} %get-tuple-element.70) | copy-start | bytes 11010052
  241.0 18.2 %slice-start.4 = ((s8[5242880]{0:T(1024)(128)(4,1)}), s8[4194304]{0:T(1024)(128)(4,1)S(1)}, s32[]{:S(2)}) async-start(s8[5242880]{0:T(1024)(128)(4,1)} %bitcast.72), calls=%async_computation.4 | async-start | bytes 8388608
  250.7 8.5 %slice-start.5 = ((s8[5242880]{0:T(1024)(128)(4,1)}), s8[1048576]{0:T(1024)(128)(4,1)S(1)}, s32[]{:S(2)}) async-start(s8[5242880]{0:T(1024)(128)(4,1)} %bitcast.72), calls=%async_computation.5 | async-start | bytes 2097152
  259.1 6.8 %copy-start.4 = (bf16[1024,896]{1,0:T(8,128)(2,1)}, bf16[1024,896]{1,0:T(8,128)(2,1)S(1)}, u32[]{:S(2)}) copy-start(bf16[1024,896]{1,0:T(8,128)(2,1)S(1)} %get-tuple-element.178.refs_4_) | copy-start | bytes 5505028
  266.0 86.8 %copy-start.1 = (f32[128,2560]{1,0:T(8,128)S(1)}, f32[128,2560]{1,0:T(8,128)}, u32[]{:S(2)}) copy-start(f32[128,2560]{1,0:T(8,128)} %get-tuple-element.65) | copy-start | bytes 3932164
  266.0 89.2 %copy-start.3 = (bf16[1,128,2560]{2,1,0:T(8,128)(2,1)S(1)}, bf16[1,128,2560]{2,1,0:T(8,128)(2,1)}, u32[]{:S(2)}) copy-start(bf16[1,128,2560]{2,1,0:T(8,128)(2,1)} %param.16) | copy-start | bytes 1966084
  660.9 18.3 %copy-start.6 = (bf16[128,2560]{1,0:T(8,128)(2,1)S(1)}, bf16[128,2560]{1,0:T(8,128)(2,1)}, u32[]{:S(2)}) copy-start(bf16[128,2560]{1,0:T(8,128)(2,1)} %get-tuple-element.99) | copy-start | bytes 1966084

commit v6 on v5

--- a/solution.py
+++ b/solution.py
@@ -937,9 +937,9 @@
 
 
 def last_kernel(*refs):
-    up, lat, query_up, latent_up, hidden, down, attn_out, cols, gain = refs[:9]
+    up, lat, query_up, latent_up, hidden, down, branch, cols, gain = refs[:9]
     up_all, out, attn_sum, lat_sum, latent_sum, query_sum, gain_out = refs[9:16]
-    scratch = list(refs[16:])
+    attn_out, branch_sem, scratch = refs[16], refs[17], list(refs[18:])
     rep, zpos, core = place()
     shard = zpos * 2 + core
     places = plane_places(rep)
@@ -991,9 +991,16 @@
     strips_out.start()
     sums.start((0, 1))
     latent_total.start()
+    branch_copy = pltpu.make_async_copy(branch, out_term, branch_sem.at[0])
+    branch_copy.start()
     gather.start()
-    sums.start((2, 3))
     rows = lat.shape[0]
+    tokens = 8 * rows
+
+    def attn_term(i, carry):
+        at = pl.ds(mult(i * (attn_out.shape[1] // 4), 128), attn_out.shape[1] // 4)
+        attn_out[:, at] = dot_tn(cols[:, 0].reshape(tokens, -1), out_term[:, :, at].reshape(tokens, -1)).astype(attn_out.dtype)
+        return carry
 
     def term(i, carry):
         out_term[i] = jnp.dot(hidden[pl.ds(mult(i * rows, rows), rows)], down[...],
@@ -1001,6 +1008,9 @@
         return carry
 
     arrive, onward = strips_out.arrive, strips_out.onward
+    branch_copy.wait()
+    lax.fori_loop(0, 4, attn_term, 0)
+    sums.start((2, 3))
     lax.fori_loop(0, 3, term, 0)
     arrive(1)
     latent_total.pair()
@@ -1041,7 +1051,7 @@
     sums.end(1)
     query_total.start()
     gather.finish()
-    lat_term[...] = dot_tn(cols[...], lat_all[...]).astype(lat_term.dtype).reshape(lat_term.shape)
+    lat_term[...] = dot_tn(cols[:, 1].reshape(tokens, -1), lat_all[...]).astype(lat_term.dtype).reshape(lat_term.shape)
     sums.start((4,))
     query_total.pair()
     query_total.step(0)
@@ -1079,11 +1089,12 @@
     spread.finish()
 
 
-def last_sums(cid, up, lat, query_up, latent_up, hidden, down, attn_out, cols, gain):
+def last_sums(cid, up, lat, query_up, latent_up, hidden, down, branch, cols, gain):
     kind = up.dtype
     wide = jnp.float32
     rows = lat.shape[0]
-    lat_shape = (4, cols.shape[1] // 4, lat.shape[1])
+    attn_out = jax.ShapeDtypeStruct((cols.shape[3], branch.shape[2]), kind)
+    lat_shape = (4, cols.shape[3] // 4, lat.shape[1])
     query_shape = (query_up.shape[1], query_up.shape[2] // 4)
     shapes = [(attn_out.shape[0] // 2, attn_out.shape[1] // 4)] * 2 + [
         lat_shape[1:], (latent_up.shape[1], latent_up.shape[2] // 4)]
@@ -1095,8 +1106,8 @@
         + [jax.ShapeDtypeStruct(out_term.shape[1:], wide)]
         + [jax.ShapeDtypeStruct(s, kind) for s in (attn_out.shape, lat_shape, latent_up.shape[1:])]
         + [jax.ShapeDtypeStruct((query_up.shape[1], query_up.shape[2]), kind), jax.ShapeDtypeStruct(gain.shape, gain.dtype)],
-        in_specs=[ANY] * 2 + [VMEM] * 7, out_specs=[ANY, VMEM] + [ANY] * 4 + [VMEM],
-        scratch_shapes=Strips.scratch() + PlaneGather.scratch(5)
+        in_specs=[ANY] * 2 + [VMEM] * 4 + [ANY] + [VMEM] * 2, out_specs=[ANY, VMEM] + [ANY] * 4 + [VMEM],
+        scratch_shapes=[pltpu.VMEM(attn_out.shape, kind), dma_sems(1)] + Strips.scratch() + PlaneGather.scratch(5)
         + [pltpu.VMEM((8 * rows, lat.shape[1]), kind), pltpu.VMEM(out_term.shape, kind), pltpu.VMEM(lat_shape, kind),
            pltpu.VMEM(query_part.shape, kind), pltpu.VMEM(latent_up.shape[1:], wide), pltpu.VMEM(query_shape, wide)]
         + Gather.scratch(1) + [pltpu.VMEM(s, kind) for s in shapes + [query_shape]]
@@ -1105,20 +1116,20 @@
         + Total.scratch(out_term) + Total.scratch(query_part) + Total.scratch(latent_up)
         + PlaneSum.scratch([(4,) + query_shape] * 2 + shapes, kind) + [pltpu.VMEM(latent_up.shape[1:], kind)],
         compiler_params=kernel_params(cid),
-    )(up, lat, query_up, latent_up, hidden, down, attn_out, cols, gain)
+    )(up, lat, query_up, latent_up, hidden, down, branch, cols, gain)
 
 
 def start_kernel(scale, *refs):
-    ins, (gate, up), (tokens, bias, turns, down) = refs[:7], refs[7:9], refs[9:13]
+    ins, (gate, up), (tokens, bias, turns, w_down) = refs[:7], refs[7:9], refs[9:13]
     outs, cols, refs = refs[13:20], refs[20:22], refs[22:]
     (normed, query_low, latent, rope, kv, query, mixed, logs, query_lat, latent_proj, residual, ffn_all,
-     grad_hidden) = refs[:13]
-    refs = refs[13:]
+     grad_hidden, down) = refs[:14]
+    refs = refs[14:]
     (zsend, zrecv, xsend, xrecv, ysend, yrecv, dsend, drecv, csend, crecv, own, gsend, grecv, psend, precv) = refs[:15]
     held, strips = refs[15:22], refs[22:24]
     (small, gains, w_query, w_latent, w_query_up, w_latent_up, w_out, proj, ffn, lsend, lrecv, load_sems,
-     grad_sems) = refs[24:37]
-    gather = Gather((ffn,), (ffn_all,), refs[37:])
+     grad_sems, down_sem) = refs[24:38]
+    gather = Gather((ffn,), (ffn_all,), refs[38:])
     rep, zpos, core = place()
     xrep, yrep, drep = plane_places(rep)
     shard = zpos * 2 + core
@@ -1361,6 +1372,10 @@
     def out_strip(i):
         return pltpu.make_async_copy(outs[0].at[pl.ds(mult(i * out_rows, 128), out_rows)], w_out.at[i % 2], load_sems.at[4 + i % 2])
 
+    down_copy = pltpu.make_async_copy(
+        w_down, down.at[pl.ds(mult(shard % 4 * (w_down.shape[0] % 128), 16), w_down.shape[0])], down_sem.at[0])
+    down[...] = jnp.zeros_like(down)
+    down_copy.start()
     by_hop(from_column, 1, (5, 1, 2))
     by_hop(from_column, 1, (3, 0))
     by_hop(from_column, 2, (5, 1, 2))
@@ -1445,6 +1460,7 @@
         slices_from_plane(m)
     gather.hop(1)
     arrived((5,))
+    down_copy.wait()
     chunk = 2 * tokens.shape[0]
 
     def grad_chunk(i):
@@ -1507,10 +1523,10 @@
                 for a in range(7):
                     to_core(a, k + 1, z, core, "wait_send")
 
-def start_gather(cid, scale, weights, gate, up, tokens, bias, turns, down):
+def start_gather(cid, scale, weights, gate, up, tokens, bias, turns, w_down):
     low, wide = jnp.bfloat16, jnp.float32
     rows, width = tokens.shape
-    strip = down.shape[0]
+    strip = (w_down.shape[0] // 128 + 1) * 128
     attn_out, query_down, latent_down, query_up, latent_up = weights[:5]
     tiles = query_up.shape[1]
     keys = bias.shape[1]
@@ -1520,20 +1536,20 @@
     found = [((rows, width), low), ((rows, query_down.shape[1]), low), ((keys, latent_rank), low), ((keys, 128), low),
              ((keys, tiles), low), ((rows, tiles), low), ((rows, tiles // 2), low), ((rows, 128), wide),
              ((rows, query_down.shape[1]), wide), ((rows, latent_down.shape[1]), wide), ((rows, width), wide),
-             ((8 * rows, width), low), ((8 * rows, strip), wide)]
+             ((8 * rows, width), low), ((8 * rows, strip), wide), ((strip, width), low)]
     out += [jax.ShapeDtypeStruct(s, d) for s, d in found]
     whole = [pltpu.VMEM((a.shape[0] * 8, a.shape[1]), a.dtype) for a in (query_down, latent_down, query_up, latent_up)]
     return pl.pallas_call(
         functools.partial(start_kernel, scale), out_shape=out,
-        in_specs=[ANY] * 9 + [VMEM] * 4, out_specs=[ANY] * 9 + [VMEM] * 11 + [ANY, VMEM],
+        in_specs=[ANY] * 9 + [VMEM] * 3 + [ANY], out_specs=[ANY] * 9 + [VMEM] * 11 + [ANY, VMEM, VMEM],
         scratch_shapes=[dma_sems(2, 3, 6), dma_sems(2, 3, 6)] + [dma_sems(6, 4)] * 6
         + [dma_sems(7, 7), dma_sems(7, 7), dma_sems(2, 9), dma_sems(7, 2), dma_sems(7, 2), dma_sems(3, 7, 2), dma_sems(3, 7, 2)]
         + [pltpu.VMEM(a.shape, a.dtype) for a in weights] + [pltpu.VMEM((gate.shape[0], strip), gate.dtype)] * 2
         + [pltpu.VMEM((8 * weights[6].shape[0], 128), wide), pltpu.VMEM(weights[6].shape, wide)] + whole
         + [pltpu.VMEM((2, 2 * attn_out.shape[0], width), low), pltpu.VMEM((rows, tiles), wide),
-           pltpu.VMEM((rows, width), low), dma_sems(3, 2), dma_sems(3, 2), dma_sems(6), dma_sems(2)] + Gather.scratch(1),
+           pltpu.VMEM((rows, width), low), dma_sems(3, 2), dma_sems(3, 2), dma_sems(6), dma_sems(2), dma_sems(1)] + Gather.scratch(1),
         compiler_params=kernel_params(cid),
-    )(*weights, gate, up, tokens, bias, turns, down)
+    )(*weights, gate, up, tokens, bias, turns, w_down)
 
 def plane_swap(values, j):
     return lax.ppermute(values, "rep", [(i, i ^ j) for i in range(4)])
@@ -1570,8 +1586,10 @@
     gain_list = (gain_attn, gain_ffn, gain_query, gain_latent)
     small = jnp.concatenate(
         [
-            lax.dynamic_update_slice(
-                jnp.zeros((8 * v.shape[0],), wide), v.astype(wide), (shard * v.shape[0],)
+            jnp.where(
+                jnp.arange(8 * v.shape[0], dtype=jnp.int32) // v.shape[0] == shard,
+                jnp.tile(v.astype(wide), 8),
+                0.0,
             )
             for v in gain_list
         ]
@@ -1581,8 +1599,6 @@
     ).reshape(-1, H * 128)
     grad_out = cotangent[0].astype(wide)
     grad_down_in = (residual_scale * grad_out).astype(low)
-    down_w = lax.dynamic_update_slice(jnp.zeros((strip, width), low), w_down, (shift, 0))
-
     local_pos = rep * rows + jnp.arange(rows, dtype=jnp.int32)
     key_pos = jnp.concatenate(
         [(rep ^ j) * rows + jnp.arange(rows, dtype=jnp.int32) for j in range(4)]
@@ -1625,6 +1641,7 @@
         residual,
         ffn_all,
         grad_hidden,
+        down_w,
     ) = start_gather(
         0,
         scale,
@@ -1634,7 +1651,7 @@
         tokens[0],
         bias,
         turns,
-        down_w,
+        w_down,
     )
     gains_all = jnp.sum(small_all.reshape((8,) + small.shape), axis=0)
     gain_f = gains_all[width // 128 : 2 * width // 128].reshape(-1)
@@ -1689,9 +1706,6 @@
         ),
     )
 
-    mixed_cols = cols_all[:, 0].reshape(8 * rows, width // 8)
-    normed_cols = cols_all[:, 1].reshape(8 * rows, width // 8)
-    aout_part = inner_rows(mixed_cols, branch_all).astype(low)
     up_all, out_sum, aout_own, lat_own, lup_own, qup_own, gain_own = last_sums(
         4,
         up_own,
@@ -1700,8 +1714,8 @@
         lup_part.reshape(8, -1, lup_part.shape[1]),
         hidden_low,
         down_w,
-        aout_part,
-        normed_cols,
+        branch_all.reshape(8, rows, width),
+        cols_all,
         gain_terms,
     )
     layer_out = (residual + residual_scale * out_sum).astype(low)

time: 688 us -> 669 us (0.972)
  other arithmetic: 21.3 us -> 12.3 us
where the time goes in v6:
time: 669 us; the launch traced here: 663 us
  Pallas kernels  606 us (91%)
  matrix products  24.9 us (4%)
  local copies, waits for them, and re-layouts  18.2 us (3%)
  other arithmetic  12.3 us (2%)
    pallas_call x1, Pallas kernels, start_gather(): pl.pallas_call(functools.partial(start_kernel, scale), out_shape=out, in_...  215 us
    pallas_call x1, Pallas kernels, last_sums(): pl.pallas_call(last_kernel, out_shape=[jax.ShapeDtypeStruct((8, 4) + up.s...  154 us
    pallas_call x1, Pallas kernels, middle_exchange(): pl.pallas_call(functools.partial(middle_kernel, scale), out_shape=[jax.Sh...  134 us
    pallas_call x1, Pallas kernels, back_sums(): pl.pallas_call(functools.partial(back_kernel, rows % 128), out_shape=[jax...  86.5 us
    pallas_call x1, Pallas kernels, widen(): pl.pallas_call(functools.partial(widen_kernel, heads), grid=(quarters,),...  16.3 us

profile of v6, /device:TPU:0, one launch (start us, length us, event | category | flops | bytes accessed | tf_op | source)
XLA Modules:
  0.0 663.0 jit_solution(15610051595031881015)
XLA Ops:
  0.7 0.9 reduce-window.4
  1.7 0.7 fusion.16
  3.1 0.7 pad_maximum_fusion.refs_11_.refs_14_
  3.8 0.8 and_select_fusion.refs_10_.refs_13_
  4.7 0.7 tile.16
  5.4 0.7 tile.18
  6.2 0.7 tile.40
  6.9 0.7 tile.42
  7.7 0.6 maximum_bitcast_fusion.4.refs_6_
  8.3 2.6 reshape.117
  11.1 1.1 copy.52
  12.2 0.9 fusion.4.refs_5_
  13.2 0.9 copy.44.refs_2_
  14.0 215.3 %shard_map.254 = (bf16[2560,2560]{1,0:T(8,128)(2,1)}, bf16[2560,768]{1,0:T(8,128)(2,1)}, bf16[2560,288]{1,0:T(8,128)(2,1)}, bf16[768,5120]{1,0:T(8,128)(2,1)}, b...) custom-call(bf16[320,2560]{1,0:T(8,128)(2,1)} %refs_0_.1, ...), custom_call_target="tpu_custom_call" | custom-call | tf_op jit(solution)/shard_map/pallas_call | solution.py:1542
  229.3 1.4 copy.45
  231.1 1.4 copy.46
  232.9 1.5 maximum_bitcast_fusion.refs_2_
  234.4 9.6 %fusion.19 = f32[1024,896]{1,0:T(8,128)S(1)} fusion(bf16[1024,2560]{1,0:T(8,128)(2,1)} %get-tuple-element.67.refs_1_, bf16[2560,896]{1,0:T(8,128)(2,1)} %get-tuple-element.69.refs_5_), kind=kOutput, calls=%fused_computation.72 | convolution fusion | flops 4697620480 | bytes 13500416 | tf_op jit(solution)/shard_map/dot_general | solution.py:1661
  244.1 8.4 %multiply_convert_fusion = (bf16[1024,896]{1,0:T(8,128)(2,1)}, bf16[1024,896]{1,0:T(8,128)(2,1)}, bf16[1024,896]{1,0:T(8,128)(2,1)S(1)}) fusion(f32[1024,896]{1,0:T(8,128)S(1)} %copy-done.9, f32[1024,896]{1,0:T(8,128)S(1)} %fusion.19, bf16[1024,2560]{1,0:T(8,128)(2,1)S(1)} %bitcast.49, bf16[2560,896]{1,0:T(8,128)(2,1)S(1)} %bitcast.52), kind=kOutput, calls=%fused_computation.5 | convolution fusion | flops 4712300544 | bytes 22675456 | tf_op jit(solution)/shard_map/dot_general | solution.py:1660
  252.6 6.8 %convolution_convert_fusion.refs_0_ = bf16[896,2560]{1,0:T(8,128)(2,1)} fusion(bf16[1024,896]{1,0:T(8,128)(2,1)S(1)} %get-tuple-element.180.refs_4_, bf16[1024,2560]{1,0:T(8,128)(2,1)S(1)} %bitcast.69), kind=kOutput, calls=%fused_computation.1 | convolution fusion | flops 4699914240 | bytes 11665408 | tf_op jit(solution)/shard_map/dot_general | solution.py:58
  259.4 86.5 %shard_map.255 = (f32[128,2560]{1,0:T(8,128)}, bf16[800,640]{1,0:T(8,128)(2,1)}, bf16[8,80,896]{2,1,0:T(8,128)(2,1)}, bf16[8,4,80,896]{3,2,1,0:T(8,128)(2,1)}) custom-call(bf16[896,2560]{1,0:T(8,128)(2,1)} %convolution_convert_fusion.refs_0_, bf16[1024,2560]{1,0:T(8,128)(2,1)} %get-tuple-element.67.refs_1_, bf16[1024,896]{1,0:T(8,128)(2,1)} %get-tuple-element.179.refs_2_, ...), custom_call_target="tpu_custom_call" | custom-call | tf_op jit(solution)/shard_map/pallas_call | solution.py:716
  346.2 2.5 multiply_reduce_fusion
  348.7 1.7 multiply_convert_fusion.2
  350.4 133.7 %shard_map.256 = (bf16[1024,2560]{1,0:T(8,128)(2,1)}, bf16[8,2,128,320]{3,2,1,0:T(8,128)(2,1)}, bf16[800,2560]{1,0:T(8,128)(2,1)}, bf16[8,4,80,896]{3,2,1,0:T(8,...) custom-call(bf16[8,80,896]{2,1,0:T(8,128)(2,1)} %get-tuple-element.7, ...), custom_call_target="tpu_custom_call" | custom-call | tf_op jit(solution)/shard_map/pallas_call | solution.py:915
  484.1 154.3 %shard_map.257 = (bf16[8,4,80,896]{3,2,1,0:T(8,128)(2,1)}, f32[128,2560]{1,0:T(8,128)}, bf16[320,2560]{1,0:T(8,128)(2,1)}, bf16[4,80,1056]{2,1,0:T(8,128)(2,1)},...) custom-call(bf16[8,80,896]{2,1,0:T(8,128)(2,1)} %get-tuple-element.92.refs_0_, ...), custom_call_target="tpu_custom_call" | custom-call | tf_op jit(solution)/shard_map/pallas_call | solution.py:1103
  638.4 16.3 %shard_map.258 = (f32[320,6400]{1,0:T(8,128)}, f32[320,6400]{1,0:T(8,128)}, f32[800,2560]{1,0:T(8,128)}, f32[320,2560]{1,0:T(8,128)}, f32[320,768]{1,0:T(8,128)}...) custom-call(bf16[8,4,80,896]{3,2,1,0:T(8,128)(2,1)} %get-tuple-element.103.gate, ...), custom_call_target="tpu_custom_call" | custom-call | tf_op jit(solution)/shard_map/pallas_call | solution.py:265
  654.8 2.1 copy.49
  656.8 1.0 fusion.5
  657.8 1.4 fusion.18
  659.2 1.2 dynamic_slice.13
  660.4 1.2 dynamic_slice.14
  661.7 0.8 copy.54
  (67 shorter events, 2.4 us)
Async XLA Ops:
  0.7 11.6 %copy-start.2 = (bf16[1,128,2560]{2,1,0:T(8,128)(2,1)S(1)}, bf16[1,128,2560]{2,1,0:T(8,128)(2,1)}, u32[]{:S(2)}) copy-start(bf16[1,128,2560]{2,1,0:T(8,128)(2,1)} %param.16) | copy-start | bytes 1966084
  3.8 9.3 %copy-start.6 = (bf16[320,288]{0,1:T(8,128)(2,1)S(1)}, bf16[320,288]{0,1:T(8,128)(2,1)}, u32[]{:S(2)}) copy-start(bf16[320,288]{0,1:T(8,128)(2,1)} %param.22) | copy-start | bytes 552964
  232.9 11.2 %slice-start = ((s8[5242880]{0:T(1024)(128)(4,1)}), s8[4194304]{0:T(1024)(128)(4,1)S(1)}, s32[]{:S(2)}) async-start(s8[5242880]{0:T(1024)(128)(4,1)} %bitcast.48), calls=%async_computation | async-start | bytes 8388608
  232.9 11.2 %slice-start.2 = ((s8[4587520]{0:T(1024)(128)(4,1)}), s8[4194304]{0:T(1024)(128)(4,1)S(1)}, s32[]{:S(2)}) async-start(s8[4587520]{0:T(1024)(128)(4,1)} %bitcast.51), calls=%async_computation.2 | async-start | bytes 8388608
  234.4 9.7 %slice-start.1 = ((s8[5242880]{0:T(1024)(128)(4,1)}), s8[1048576]{0:T(1024)(128)(4,1)S(1)}, s32[]{:S(2)}) async-start(s8[5242880]{0:T(1024)(128)(4,1)} %bitcast.48), calls=%async_computation.1 | async-start | bytes 2097152
  234.4 9.7 %slice-start.3 = ((s8[4587520]{0:T(1024)(128)(4,1)}), s8[393216]{0:T(1024)(128)(4,1)S(1)}, s32[]{:S(2)}) async-start(s8[4587520]{0:T(1024)(128)(4,1)} %bitcast.51), calls=%async_computation.3 | async-start | bytes 786432
  234.4 9.7 %copy-start.9 = (f32[1024,896]{1,0:T(8,128)S(1)}, f32[1024,896]{1,0:T(8,128)}, u32[]{:S(2)}) copy-start(f32[1024,896]{1,0:T(8,128)} %get-tuple-element.71) | copy-start | bytes 11010052
  234.4 18.2 %slice-start.4 = ((s8[5242880]{0:T(1024)(128)(4,1)}), s8[4194304]{0:T(1024)(128)(4,1)S(1)}, s32[]{:S(2)}) async-start(s8[5242880]{0:T(1024)(128)(4,1)} %bitcast.68), calls=%async_computation.4 | async-start | bytes 8388608
  244.1 8.5 %slice-start.5 = ((s8[5242880]{0:T(1024)(128)(4,1)}), s8[1048576]{0:T(1024)(128)(4,1)S(1)}, s32[]{:S(2)}) async-start(s8[5242880]{0:T(1024)(128)(4,1)} %bitcast.68), calls=%async_computation.5 | async-start | bytes 2097152
  252.6 6.8 %copy-start.3 = (bf16[1024,896]{1,0:T(8,128)(2,1)}, bf16[1024,896]{1,0:T(8,128)(2,1)S(1)}, u32[]{:S(2)}) copy-start(bf16[1024,896]{1,0:T(8,128)(2,1)S(1)} %get-tuple-element.180.refs_4_) | copy-start | bytes 5505028
  259.4 86.5 %copy-start.7 = (f32[384,128]{1,0:T(8,128)S(1)}, f32[384,128]{1,0:T(8,128)}, u32[]{:S(2)}) copy-start(f32[384,128]{1,0:T(8,128)} %get-tuple-element.74) | copy-start | bytes 589828
  259.4 86.6 %copy-start = (f32[128,2560]{1,0:T(8,128)S(1)}, f32[128,2560]{1,0:T(8,128)}, u32[]{:S(2)}) copy-start(f32[128,2560]{1,0:T(8,128)} %get-tuple-element.66) | copy-start | bytes 3932164
  346.0 2.7 copy-start.1
  346.0 4.4 copy-start.8
  638.4 18.4 %copy-start.4 = (f32[128,2560]{1,0:T(8,128)S(1)}, f32[128,2560]{1,0:T(8,128)}, u32[]{:S(2)}) copy-start(f32[128,2560]{1,0:T(8,128)} %get-tuple-element.100) | copy-start | bytes 3932164
  654.7 6.9 %copy-start.5 = (bf16[128,2560]{1,0:T(8,128)(2,1)S(1)}, bf16[128,2560]{1,0:T(8,128)(2,1)}, u32[]{:S(2)}) copy-start(bf16[128,2560]{1,0:T(8,128)(2,1)} %get-tuple-element.101) | copy-start | bytes 1966084

commit v7 on v6

--- a/solution.py
+++ b/solution.py
@@ -1120,13 +1120,14 @@
 
 
 def start_kernel(scale, *refs):
-    ins, (gate, up), (tokens, bias, turns, w_down) = refs[:7], refs[7:9], refs[9:13]
+    ins, (gate, up), (tokens, bias, turns, w_down) = list(refs[:7]), refs[7:9], refs[9:13]
     outs, cols, refs = refs[13:20], refs[20:22], refs[22:]
     (normed, query_low, latent, rope, kv, query, mixed, logs, query_lat, latent_proj, residual, ffn_all,
      grad_hidden, down) = refs[:14]
     refs = refs[14:]
     (zsend, zrecv, xsend, xrecv, ysend, yrecv, dsend, drecv, csend, crecv, own, gsend, grecv, psend, precv) = refs[:15]
     held, strips = refs[15:22], refs[22:24]
+    cotangent, ins[5] = ins[5], held[5]
     (small, gains, w_query, w_latent, w_query_up, w_latent_up, w_out, proj, ffn, lsend, lrecv, load_sems,
      grad_sems, down_sem) = refs[24:38]
     gather = Gather((ffn,), (ffn_all,), refs[38:])
@@ -1239,13 +1240,16 @@
         return pltpu.make_async_copy(strips[which], cols[which].at[pl.ds(mult(shard * rows, rows), rows)], own.at[1, 7 + which])
 
     near = (1, 2, 6, 3, 7, 4, 5)
+    held[5][...] = (residual_scale * cotangent[...].astype(jnp.float32)).astype(held[5].dtype)
     for a in range(7):
         to_core(a, 0, zpos, core, "start", src=ins[a])
-        keep(a, 0).start()
+        if a != 5:
+            keep(a, 0).start()
     for which in range(2):
         own_slice(which, 0).start()
     for a in range(7):
-        keep(a, 0).wait()
+        if a != 5:
+            keep(a, 0).wait()
         keep(a, 1).start()
     for which in range(2):
         own_slice(which, 0).wait()
@@ -1399,26 +1403,22 @@
     normalize(lambda t: tokens[:, tile(t)].astype(wide), normed, 20, 0)
     by_hop(from_corner, 3, (1, 2))
     by_hop(from_corner, 1, (3, 0))
+    send_own(4)
     down_products()
     by_hop(from_plane, 3, (3, 0))
     by_hop(from_corner, 2, (3, 0))
-    for m in near[:3]:
-        slices_from_column(m)
-    send_own(4)
     by_hop(from_corner, 3, (3, 0))
     arrived((3, 4))
     load(3, w_query_up, 3).start()
     load(4, w_latent_up, 0).start()
-    for m in near[3:]:
-        slices_from_column(m)
     load(3, w_query_up, 3).wait()
     chunk_loop(5, query_chunk)
-    for m in near[:3]:
-        slices_from_plane(m)
     for k in range(3):
         share(k, "wait_recv")
     load(4, w_latent_up, 0).wait()
     chunk_loop(5, key_chunk)
+    for m in near:
+        slices_from_column(m)
     logs[...] = jnp.zeros_like(logs)
     group = attend_heads(scale, proj, kv, rope, bias, turns, query, mixed, logs)
 
@@ -1435,6 +1435,8 @@
         return carry
 
     lax.fori_loop(0, kv.shape[1] // 512, attend_step, 0)
+    for m in near[:3]:
+        slices_from_plane(m)
     arrived((0,))
     out_strip(0).start()
     residual[...] = tokens[...].astype(wide)
@@ -1541,7 +1543,7 @@
     whole = [pltpu.VMEM((a.shape[0] * 8, a.shape[1]), a.dtype) for a in (query_down, latent_down, query_up, latent_up)]
     return pl.pallas_call(
         functools.partial(start_kernel, scale), out_shape=out,
-        in_specs=[ANY] * 9 + [VMEM] * 3 + [ANY], out_specs=[ANY] * 9 + [VMEM] * 11 + [ANY, VMEM, VMEM],
+        in_specs=[ANY] * 5 + [VMEM] + [ANY] * 3 + [VMEM] * 3 + [ANY], out_specs=[ANY] * 9 + [VMEM] * 11 + [ANY, VMEM, VMEM],
         scratch_shapes=[dma_sems(2, 3, 6), dma_sems(2, 3, 6)] + [dma_sems(6, 4)] * 6
         + [dma_sems(7, 7), dma_sems(7, 7), dma_sems(2, 9), dma_sems(7, 2), dma_sems(7, 2), dma_sems(3, 7, 2), dma_sems(3, 7, 2)]
         + [pltpu.VMEM(a.shape, a.dtype) for a in weights] + [pltpu.VMEM((gate.shape[0], strip), gate.dtype)] * 2
@@ -1598,7 +1600,6 @@
         query_up.reshape(-1, H, head_dim), ((0, 0), (0, 0), (0, 128 - head_dim))
     ).reshape(-1, H * 128)
     grad_out = cotangent[0].astype(wide)
-    grad_down_in = (residual_scale * grad_out).astype(low)
     local_pos = rep * rows + jnp.arange(rows, dtype=jnp.int32)
     key_pos = jnp.concatenate(
         [(rep ^ j) * rows + jnp.arange(rows, dtype=jnp.int32) for j in range(4)]
@@ -1645,7 +1646,7 @@
     ) = start_gather(
         0,
         scale,
-        (attn_out, query_down, latent_down, tile_up, latent_up, grad_down_in, small),
+        (attn_out, query_down, latent_down, tile_up, latent_up, cotangent[0], small),
         w_gate,
         w_up,
         tokens[0],

time: 669 us -> 668 us (level)
  no operation moved by 1% of the time
where the time goes in v7:
time: 668 us; the launch traced here: 661 us
  Pallas kernels  605 us (91%)
  matrix products  24.9 us (4%)
  local copies, waits for them, and re-layouts  18.2 us (3%)
  other arithmetic  11.3 us (2%)
    pallas_call x1, Pallas kernels, start_gather(): pl.pallas_call(functools.partial(start_kernel, scale), out_shape=out, in_...  214 us
    pallas_call x1, Pallas kernels, last_sums(): pl.pallas_call(last_kernel, out_shape=[jax.ShapeDtypeStruct((8, 4) + up.s...  154 us
    pallas_call x1, Pallas kernels, middle_exchange(): pl.pallas_call(functools.partial(middle_kernel, scale), out_shape=[jax.Sh...  134 us
    pallas_call x1, Pallas kernels, back_sums(): pl.pallas_call(functools.partial(back_kernel, rows % 128), out_shape=[jax...  86.5 us
    pallas_call x1, Pallas kernels, widen(): pl.pallas_call(functools.partial(widen_kernel, heads), grid=(quarters,),...  16.3 us

profile of v7, /device:TPU:0, one launch (start us, length us, event | category | flops | bytes accessed | tf_op | source)
XLA Modules:
  0.0 661.4 jit_solution(3921505138848833656)
XLA Ops:
  0.7 0.9 reduce-window.4
  1.6 0.7 fusion.16
  3.0 0.7 pad_maximum_fusion.refs_11_.refs_14_
  3.8 0.8 and_select_fusion.refs_10_.refs_13_
  4.6 0.7 tile.16
  5.4 0.7 tile.18
  6.2 0.7 tile.40
  6.9 0.7 tile.42
  7.7 0.6 maximum_bitcast_fusion.4.refs_6_
  8.3 2.6 reshape.115
  11.1 1.1 copy.52
  12.2 0.9 copy.44.refs_2_
  13.1 214.4 %shard_map.254 = (bf16[2560,2560]{1,0:T(8,128)(2,1)}, bf16[2560,768]{1,0:T(8,128)(2,1)}, bf16[2560,288]{1,0:T(8,128)(2,1)}, bf16[768,5120]{1,0:T(8,128)(2,1)}, b...) custom-call(bf16[320,2560]{1,0:T(8,128)(2,1)} %refs_0_.1, ...), custom_call_target="tpu_custom_call" | custom-call | tf_op jit(solution)/shard_map/pallas_call | solution.py:1544
  227.4 1.4 copy.45
  228.8 0.4 copy.47
  229.2 1.4 copy.46
  231.0 1.5 maximum_bitcast_fusion.refs_2_
  232.5 9.6 %fusion.20 = f32[1024,896]{1,0:T(8,128)S(1)} fusion(bf16[1024,2560]{1,0:T(8,128)(2,1)} %get-tuple-element.67.refs_1_, bf16[2560,896]{1,0:T(8,128)(2,1)} %get-tuple-element.69.refs_5_), kind=kOutput, calls=%fused_computation.70 | convolution fusion | flops 4697620480 | bytes 13500416 | tf_op jit(solution)/shard_map/dot_general | solution.py:1662
  242.2 8.4 %multiply_convert_fusion = (bf16[1024,896]{1,0:T(8,128)(2,1)}, bf16[1024,896]{1,0:T(8,128)(2,1)}, bf16[1024,896]{1,0:T(8,128)(2,1)S(1)}) fusion(f32[1024,896]{1,0:T(8,128)S(1)} %copy-done.9, f32[1024,896]{1,0:T(8,128)S(1)} %fusion.20, bf16[1024,2560]{1,0:T(8,128)(2,1)S(1)} %bitcast.47, bf16[2560,896]{1,0:T(8,128)(2,1)S(1)} %bitcast.50), kind=kOutput, calls=%fused_computation.5 | convolution fusion | flops 4712300544 | bytes 22675456 | tf_op jit(solution)/shard_map/dot_general | solution.py:1661
  250.7 6.8 %convolution_convert_fusion.refs_0_ = bf16[896,2560]{1,0:T(8,128)(2,1)} fusion(bf16[1024,896]{1,0:T(8,128)(2,1)S(1)} %get-tuple-element.180.refs_4_, bf16[1024,2560]{1,0:T(8,128)(2,1)S(1)} %bitcast.68), kind=kOutput, calls=%fused_computation.1 | convolution fusion | flops 4699914240 | bytes 11665408 | tf_op jit(solution)/shard_map/dot_general | solution.py:58
  257.5 86.5 %shard_map.255 = (f32[128,2560]{1,0:T(8,128)}, bf16[800,640]{1,0:T(8,128)(2,1)}, bf16[8,80,896]{2,1,0:T(8,128)(2,1)}, bf16[8,4,80,896]{3,2,1,0:T(8,128)(2,1)}) custom-call(bf16[896,2560]{1,0:T(8,128)(2,1)} %convolution_convert_fusion.refs_0_, bf16[1024,2560]{1,0:T(8,128)(2,1)} %get-tuple-element.67.refs_1_, bf16[1024,896]{1,0:T(8,128)(2,1)} %get-tuple-element.179.refs_2_, ...), custom_call_target="tpu_custom_call" | custom-call | tf_op jit(solution)/shard_map/pallas_call | solution.py:716
  344.3 2.5 multiply_reduce_fusion
  346.8 1.7 multiply_convert_fusion.2
  348.5 134.0 %shard_map.256 = (bf16[1024,2560]{1,0:T(8,128)(2,1)}, bf16[8,2,128,320]{3,2,1,0:T(8,128)(2,1)}, bf16[800,2560]{1,0:T(8,128)(2,1)}, bf16[8,4,80,896]{3,2,1,0:T(8,...) custom-call(bf16[8,80,896]{2,1,0:T(8,128)(2,1)} %get-tuple-element.7, ...), custom_call_target="tpu_custom_call" | custom-call | tf_op jit(solution)/shard_map/pallas_call | solution.py:915
  482.5 154.3 %shard_map.257 = (bf16[8,4,80,896]{3,2,1,0:T(8,128)(2,1)}, f32[128,2560]{1,0:T(8,128)}, bf16[320,2560]{1,0:T(8,128)(2,1)}, bf16[4,80,1056]{2,1,0:T(8,128)(2,1)},...) custom-call(bf16[8,80,896]{2,1,0:T(8,128)(2,1)} %get-tuple-element.92.refs_0_, ...), custom_call_target="tpu_custom_call" | custom-call | tf_op jit(solution)/shard_map/pallas_call | solution.py:1103
  636.9 16.3 %shard_map.258 = (f32[320,6400]{1,0:T(8,128)}, f32[320,6400]{1,0:T(8,128)}, f32[800,2560]{1,0:T(8,128)}, f32[320,2560]{1,0:T(8,128)}, f32[320,768]{1,0:T(8,128)}...) custom-call(bf16[8,4,80,896]{3,2,1,0:T(8,128)(2,1)} %get-tuple-element.103.gate, ...), custom_call_target="tpu_custom_call" | custom-call | tf_op jit(solution)/shard_map/pallas_call | solution.py:265
  653.2 2.1 copy.49
  655.3 1.0 fusion.5
  656.2 1.4 fusion.19
  657.6 1.2 dynamic_slice.13
  658.9 1.2 dynamic_slice.14
  660.1 0.8 copy.54
  (66 shorter events, 2.1 us)
Async XLA Ops:
  0.7 11.6 %copy-start.6 = (bf16[320,288]{0,1:T(8,128)(2,1)S(1)}, bf16[320,288]{0,1:T(8,128)(2,1)}, u32[]{:S(2)}) copy-start(bf16[320,288]{0,1:T(8,128)(2,1)} %param.22) | copy-start | bytes 552964
  231.0 11.2 %slice-start = ((s8[5242880]{0:T(1024)(128)(4,1)}), s8[4194304]{0:T(1024)(128)(4,1)S(1)}, s32[]{:S(2)}) async-start(s8[5242880]{0:T(1024)(128)(4,1)} %bitcast.46), calls=%async_computation | async-start | bytes 8388608
  231.0 11.2 %slice-start.2 = ((s8[4587520]{0:T(1024)(128)(4,1)}), s8[4194304]{0:T(1024)(128)(4,1)S(1)}, s32[]{:S(2)}) async-start(s8[4587520]{0:T(1024)(128)(4,1)} %bitcast.49), calls=%async_computation.2 | async-start | bytes 8388608
  232.5 9.7 %slice-start.1 = ((s8[5242880]{0:T(1024)(128)(4,1)}), s8[1048576]{0:T(1024)(128)(4,1)S(1)}, s32[]{:S(2)}) async-start(s8[5242880]{0:T(1024)(128)(4,1)} %bitcast.46), calls=%async_computation.1 | async-start | bytes 2097152
  232.5 9.7 %slice-start.3 = ((s8[4587520]{0:T(1024)(128)(4,1)}), s8[393216]{0:T(1024)(128)(4,1)S(1)}, s32[]{:S(2)}) async-start(s8[4587520]{0:T(1024)(128)(4,1)} %bitcast.49), calls=%async_computation.3 | async-start | bytes 786432
  232.5 9.7 %copy-start.9 = (f32[1024,896]{1,0:T(8,128)S(1)}, f32[1024,896]{1,0:T(8,128)}, u32[]{:S(2)}) copy-start(f32[1024,896]{1,0:T(8,128)} %get-tuple-element.71) | copy-start | bytes 11010052
  232.5 18.2 %slice-start.4 = ((s8[5242880]{0:T(1024)(128)(4,1)}), s8[4194304]{0:T(1024)(128)(4,1)S(1)}, s32[]{:S(2)}) async-start(s8[5242880]{0:T(1024)(128)(4,1)} %bitcast.67), calls=%async_computation.4 | async-start | bytes 8388608
  242.2 8.5 %slice-start.5 = ((s8[5242880]{0:T(1024)(128)(4,1)}), s8[1048576]{0:T(1024)(128)(4,1)S(1)}, s32[]{:S(2)}) async-start(s8[5242880]{0:T(1024)(128)(4,1)} %bitcast.67), calls=%async_computation.5 | async-start | bytes 2097152
  250.7 6.8 %copy-start.3 = (bf16[1024,896]{1,0:T(8,128)(2,1)}, bf16[1024,896]{1,0:T(8,128)(2,1)S(1)}, u32[]{:S(2)}) copy-start(bf16[1024,896]{1,0:T(8,128)(2,1)S(1)} %get-tuple-element.180.refs_4_) | copy-start | bytes 5505028
  257.5 86.5 %copy-start.7 = (f32[384,128]{1,0:T(8,128)S(1)}, f32[384,128]{1,0:T(8,128)}, u32[]{:S(2)}) copy-start(f32[384,128]{1,0:T(8,128)} %get-tuple-element.74) | copy-start | bytes 589828
  257.5 86.6 %copy-start = (f32[128,2560]{1,0:T(8,128)S(1)}, f32[128,2560]{1,0:T(8,128)}, u32[]{:S(2)}) copy-start(f32[128,2560]{1,0:T(8,128)} %get-tuple-element.66) | copy-start | bytes 3932164
  344.0 2.8 copy-start.1
  344.0 2.8 copy-start.2
  344.1 4.4 copy-start.8
  636.9 18.4 %copy-start.4 = (f32[128,2560]{1,0:T(8,128)S(1)}, f32[128,2560]{1,0:T(8,128)}, u32[]{:S(2)}) copy-start(f32[128,2560]{1,0:T(8,128)} %get-tuple-element.100) | copy-start | bytes 3932164
  653.2 6.9 %copy-start.5 = (bf16[128,2560]{1,0:T(8,128)(2,1)S(1)}, bf16[128,2560]{1,0:T(8,128)(2,1)}, u32[]{:S(2)}) copy-start(bf16[128,2560]{1,0:T(8,128)(2,1)} %get-tuple-element.101) | copy-start | bytes 1966084
